TPU v7x, 32 devices: a whole 2x2x4 slice. The times are simulated.
32 devices in a mesh: dp: 16 (over z, y, x), tensor: 2 (over core).
Axes of the slice: x: 2, y: 2, z: 4, core: 2. Of those that a mesh axis runs over, the one named last changes fastest.
Arguments:
- tokens: bfloat16 [10240, 2048], P(('dp', 'tensor')), may hold values from -6 to 6
- seq_ends: int32 [16, 4], P('dp'), may hold values from 128 to 640, as said below
- w_query: bfloat16 [2048, 2048], P('dp', 'tensor'), may hold values from -0.125 to 0.125
- w_key: bfloat16 [2048, 1024], P('dp', 'tensor'), may hold values from -0.125 to 0.125
- w_value: bfloat16 [2048, 1024], P('dp', 'tensor'), may hold values from -0.125 to 0.125
- w_out: bfloat16 [2048, 2048], P('tensor', 'dp'), may hold values from -1 to 1
- w_gate: bfloat16 [2048, 6144], P('dp', 'tensor'), may hold values from -0.125 to 0.125
- w_up: bfloat16 [2048, 6144], P('dp', 'tensor'), may hold values from -0.125 to 0.125
- w_down: bfloat16 [6144, 2048], P('tensor', 'dp'), may hold values from -0.078125 to 0.078125
- gain_attn: float32 [2048], replicated, may hold values from 0.1 to 1.9
- gain_mlp: float32 [2048], replicated, may hold values from 0.1 to 1.9
- gain_query: float32 [128], replicated, may hold values from 0.1 to 1.9
- gain_key: float32 [128], replicated, may hold values from 0.1 to 1.9
- cotangent: bfloat16 [10240, 2048], P(('dp', 'tensor')), may hold values from -6 to 6
Outputs:
- out_tokens: bfloat16 [10240, 2048], P(('dp', 'tensor'))
- grad_tokens: float32 [10240, 2048], P(('dp', 'tensor'))
- grad_query: float32 [2048, 2048], P('dp', 'tensor')
- grad_key: float32 [2048, 1024], P('dp', 'tensor')
- grad_value: float32 [2048, 1024], P('dp', 'tensor')
- grad_out: float32 [2048, 2048], P('tensor', 'dp')
- grad_gate: float32 [2048, 6144], P('dp', 'tensor')
- grad_up: float32 [2048, 6144], P('dp', 'tensor')
- grad_down: float32 [6144, 2048], P('tensor', 'dp')
- grad_gain_attn: float32 [2048], replicated
- grad_gain_mlp: float32 [2048], replicated
- grad_gain_query: float32 [128], replicated
- grad_gain_key: float32 [128], replicated
Inputs may be any that keep to these rules, and one draw needn't show every extreme that they name: `seq_ends`: each row rises strictly and every entry is a multiple of 128, so every sequence is a whole number of 128-slot blocks, one block or more. The last entry is the group's used slots: at least 512, more than 320, and equal to 640 in some group. No entry other than the last equals 320, so one sequence of every group spans slots 320 - 1 and 320.
All inputs are finite; a program needn't handle non-finite values.
Results may differ from a plain program's by a relative error of at most 0.015.
Values may be sent and summed in bfloat16 or wider, within the bound.
No kernel may reach another device: no remote copies, remote signals or barrier semaphores. Data moves between devices by JAX's collectives and lax.ppermute only.
A program may use at most 256 MiB of HBM per device.

v0:
```python
import jax
import jax.numpy as jnp
from jax import lax
from jax.sharding import PartitionSpec as P

EPSILON = 1e-06
ROPE_BASE = 1000000.0


def rms_norm(values, gain_vec):
    return (
        values * lax.rsqrt(jnp.mean(values * values, axis=-1, keepdims=True) + EPSILON) * gain_vec
    )


def rotary(values, cosine_table, sine_table):
    half_width = values.shape[-1] // 2
    front_half = values[..., :half_width]
    back_half = values[..., half_width:]
    cosine_table = cosine_table[:, None, :]
    sine_table = sine_table[:, None, :]
    return jnp.concatenate(
        [
            front_half * cosine_table - back_half * sine_table,
            back_half * cosine_table + front_half * sine_table,
        ],
        axis=-1,
    )


def rope_tables(positions, width):
    half_width = width // 2
    frequency = ROPE_BASE ** (-2.0 * jnp.arange(half_width, dtype=jnp.float32) / width)
    angles = positions.astype(jnp.float32)[:, None] * frequency[None, :]
    return (jnp.cos(angles), jnp.sin(angles))


def token_layout(seq_ends, slot_count):
    token_index = jnp.arange(slot_count, dtype=jnp.int32)
    segment = jnp.sum((token_index[:, None] >= seq_ends[None, :]).astype(jnp.int32), axis=1)
    starts = jnp.concatenate([jnp.zeros((1,), jnp.int32), seq_ends[:-1]])
    onehot = (segment[:, None] == jnp.arange(seq_ends.shape[0], dtype=jnp.int32)[None, :]).astype(
        jnp.int32
    )
    positions = token_index - jnp.sum(onehot * starts[None, :], axis=1)
    return (segment, positions)


def head_path(raw_in, gain_in, cosine_table, sine_table):
    heads = raw_in.reshape(raw_in.shape[0], -1, gain_in.shape[0])
    return rotary(rms_norm(heads, gain_in), cosine_table, sine_table)


def matmul(left, right):
    return jnp.dot(left, right, preferred_element_type=jnp.float32)


def mat_rows(left, right):
    return lax.dot_general(
        left, right, (((0,), (0,)), ((), ())), preferred_element_type=jnp.float32
    )


def mat_cols(left, right):
    return lax.dot_general(
        left, right, (((1,), (1,)), ((), ())), preferred_element_type=jnp.float32
    )


def per_device(
    tokens,
    seq_ends,
    w_query,
    w_key,
    w_value,
    w_out,
    w_gate,
    w_up,
    w_down,
    gain_attn,
    gain_mlp,
    gain_query,
    gain_key,
    cotangent,
):
    rows_dev = tokens.shape[0]
    group_rows = rows_dev * lax.axis_size("tensor")
    tensor_place = lax.axis_index("tensor")
    head_width = gain_query.shape[0]
    score_scale = head_width ** (-0.5)
    segment, positions = token_layout(seq_ends[0], group_rows)
    live_group = segment < seq_ends.shape[1]
    live_float = live_group.astype(jnp.float32)
    live_mine = lax.dynamic_slice_in_dim(live_float, tensor_place * rows_dev, rows_dev)[:, None]
    cosine_table, sine_table = rope_tables(positions, head_width)
    places = jnp.arange(group_rows, dtype=jnp.int32)
    allowed = (
        (segment[:, None] == segment[None, :])
        & (places[None, :] <= places[:, None])
        & live_group[:, None]
    )
    allowed_float = allowed.astype(jnp.float32)
    gathered = (
        lax.all_gather(w_query, "dp", axis=0, tiled=True),
        lax.all_gather(w_key, "dp", axis=0, tiled=True),
        lax.all_gather(w_value, "dp", axis=0, tiled=True),
        lax.all_gather(w_out, "dp", axis=1, tiled=True),
        lax.all_gather(w_gate, "dp", axis=0, tiled=True),
        lax.all_gather(w_up, "dp", axis=0, tiled=True),
        lax.all_gather(w_down, "dp", axis=1, tiled=True),
    )
    full_query, full_key, full_value, full_out, full_gate, full_up, full_down = gathered
    token_float = tokens.astype(jnp.float32)
    normed, attn_norm_pull = jax.vjp(rms_norm, token_float, gain_attn)
    normed_all = lax.all_gather(normed.astype(jnp.bfloat16), "tensor", axis=0, tiled=True)
    query_raw = matmul(normed_all, full_query)
    key_raw = matmul(normed_all, full_key)
    value_low = (
        matmul(normed_all, full_value).astype(jnp.bfloat16).reshape(group_rows, -1, head_width)
    )
    query_rot, query_pull = jax.vjp(
        lambda raw_in, gain_in: head_path(raw_in, gain_in, cosine_table, sine_table),
        query_raw,
        gain_query,
    )
    key_rot, key_pull = jax.vjp(
        lambda raw_in, gain_in: head_path(raw_in, gain_in, cosine_table, sine_table),
        key_raw,
        gain_key,
    )
    key_low = key_rot.astype(jnp.bfloat16)
    kv_local = key_low.shape[1]
    query_grouped = query_rot.astype(jnp.bfloat16).reshape(group_rows, kv_local, -1, head_width)

    def masked_scores():
        scores = (
            jnp.einsum("qkgd,skd->kgqs", query_grouped, key_low, preferred_element_type=jnp.float32)
            * score_scale
        )
        return jnp.where(allowed, scores, -1e30)

    masked = masked_scores()
    row_max = jnp.max(masked, axis=-1, keepdims=True)
    row_total = (
        jnp.sum(jnp.exp(masked - row_max) * allowed_float, axis=-1, keepdims=True)
        + 1.0
        - live_float[:, None]
    )
    probability = jnp.exp(masked - row_max) * allowed_float / row_total
    context_low = (
        jnp.einsum(
            "kgqs,skd->qkgd",
            probability.astype(jnp.bfloat16),
            value_low,
            preferred_element_type=jnp.float32,
        )
        .reshape(group_rows, -1)
        .astype(jnp.bfloat16)
    )
    attn_sum = lax.psum_scatter(
        matmul(context_low, full_out), "tensor", scatter_dimension=0, tiled=True
    )
    hidden_in = token_float + attn_sum
    mlp_normed, mlp_norm_pull = jax.vjp(rms_norm, hidden_in, gain_mlp)
    mlp_all = lax.all_gather(mlp_normed.astype(jnp.bfloat16), "tensor", axis=0, tiled=True)
    gate_proj = matmul(mlp_all, full_gate)
    up_proj = matmul(mlp_all, full_up)
    hidden_low = (jax.nn.silu(gate_proj) * up_proj).astype(jnp.bfloat16)
    mlp_sum = lax.psum_scatter(
        matmul(hidden_low, full_down).astype(jnp.bfloat16),
        "tensor",
        scatter_dimension=0,
        tiled=True,
    ).astype(jnp.float32)
    out_tokens = (hidden_in + live_mine * mlp_sum).astype(jnp.bfloat16)
    again = (
        lax.all_gather(w_query, "dp", axis=0, tiled=True),
        lax.all_gather(w_key, "dp", axis=0, tiled=True),
        lax.all_gather(w_value, "dp", axis=0, tiled=True),
        lax.all_gather(w_out, "dp", axis=1, tiled=True),
        lax.all_gather(w_gate, "dp", axis=0, tiled=True),
        lax.all_gather(w_up, "dp", axis=0, tiled=True),
        lax.all_gather(w_down, "dp", axis=1, tiled=True),
    )
    back_query, back_key, back_value, back_out, back_gate, back_up, back_down = again
    cot_float = cotangent.astype(jnp.float32)
    branch_all = lax.all_gather(
        (live_mine * cot_float).astype(jnp.bfloat16), "tensor", axis=0, tiled=True
    )
    grad_down_full = mat_rows(hidden_low, branch_all)
    hidden_grad = mat_cols(branch_all, back_down)
    sigmoid_gate = jax.nn.sigmoid(gate_proj)
    gate_grad = (
        hidden_grad * up_proj * sigmoid_gate * (1.0 + gate_proj * (1.0 - sigmoid_gate))
    ).astype(jnp.bfloat16)
    up_grad = (hidden_grad * jax.nn.silu(gate_proj)).astype(jnp.bfloat16)
    grad_gate_full = mat_rows(mlp_all, gate_grad)
    grad_up_full = mat_rows(mlp_all, up_grad)
    mlp_back = lax.psum_scatter(
        mat_cols(gate_grad, back_gate) + mat_cols(up_grad, back_up),
        "tensor",
        scatter_dimension=0,
        tiled=True,
    )
    hidden_from, gain_mlp_part = mlp_norm_pull(mlp_back)
    hidden_grad_total = cot_float + hidden_from
    mlp_grads = (
        lax.psum_scatter(grad_gate_full, "dp", scatter_dimension=0, tiled=True),
        lax.psum_scatter(grad_up_full, "dp", scatter_dimension=0, tiled=True),
        lax.psum_scatter(grad_down_full, "dp", scatter_dimension=1, tiled=True),
    )
    attn_cot_all = lax.all_gather(
        hidden_grad_total.astype(jnp.bfloat16), "tensor", axis=0, tiled=True
    )
    grad_out_full = mat_rows(context_low, attn_cot_all)
    context_grad = (
        mat_cols(attn_cot_all, back_out)
        .astype(jnp.bfloat16)
        .reshape(group_rows, kv_local, -1, head_width)
    )
    masked = masked_scores()
    probability = jnp.exp(masked - row_max) * allowed_float / row_total
    prob_grad = jnp.einsum(
        "qkgd,skd->kgqs", context_grad, value_low, preferred_element_type=jnp.float32
    )
    value_grad = (
        jnp.einsum(
            "kgqs,qkgd->skd",
            probability.astype(jnp.bfloat16),
            context_grad,
            preferred_element_type=jnp.float32,
        )
        .astype(jnp.bfloat16)
        .reshape(group_rows, -1)
    )
    score_grad = (
        probability * (prob_grad - jnp.sum(probability * prob_grad, axis=-1, keepdims=True))
    ).astype(jnp.bfloat16)
    query_rot_grad = (
        jnp.einsum(
            "kgqs,skd->qkgd", score_grad, key_low, preferred_element_type=jnp.float32
        ).reshape(group_rows, -1, head_width)
        * score_scale
    )
    key_rot_grad = (
        jnp.einsum("kgqs,qkgd->skd", score_grad, query_grouped, preferred_element_type=jnp.float32)
        * score_scale
    )
    query_grad, gain_query_part = query_pull(query_rot_grad)
    key_grad, gain_key_part = key_pull(key_rot_grad)
    query_grad_low = query_grad.astype(jnp.bfloat16)
    key_grad_low = key_grad.astype(jnp.bfloat16)
    grad_query_full = mat_rows(normed_all, query_grad_low)
    grad_key_full = mat_rows(normed_all, key_grad_low)
    grad_value_full = mat_rows(normed_all, value_grad)
    attn_back = lax.psum_scatter(
        (
            mat_cols(query_grad_low, back_query)
            + mat_cols(key_grad_low, back_key)
            + mat_cols(value_grad, back_value)
        ).astype(jnp.bfloat16),
        "tensor",
        scatter_dimension=0,
        tiled=True,
    ).astype(jnp.float32)
    token_from, gain_attn_part = attn_norm_pull(attn_back)
    grad_tokens = hidden_grad_total + token_from
    attn_grads = (
        lax.psum_scatter(grad_query_full, "dp", scatter_dimension=0, tiled=True),
        lax.psum_scatter(grad_key_full, "dp", scatter_dimension=0, tiled=True),
        lax.psum_scatter(grad_value_full, "dp", scatter_dimension=0, tiled=True),
        lax.psum_scatter(grad_out_full, "dp", scatter_dimension=1, tiled=True),
    )
    gain_sums = lax.psum(
        (gain_attn_part, gain_mlp_part, gain_query_part, gain_key_part), ("dp", "tensor")
    )
    return (
        out_tokens,
        grad_tokens,
        attn_grads[0],
        attn_grads[1],
        attn_grads[2],
        attn_grads[3],
        mlp_grads[0],
        mlp_grads[1],
        mlp_grads[2],
        gain_sums[0],
        gain_sums[1],
        gain_sums[2],
        gain_sums[3],
    )


def solution(mesh):
    in_specs = (
        P(("dp", "tensor"), None),
        P("dp", None),
        P("dp", "tensor"),
        P("dp", "tensor"),
        P("dp", "tensor"),
        P("tensor", "dp"),
        P("dp", "tensor"),
        P("dp", "tensor"),
        P("tensor", "dp"),
        P(),
        P(),
        P(),
        P(),
        P(("dp", "tensor"), None),
    )
    out_specs = (
        P(("dp", "tensor"), None),
        P(("dp", "tensor"), None),
        P("dp", "tensor"),
        P("dp", "tensor"),
        P("dp", "tensor"),
        P("tensor", "dp"),
        P("dp", "tensor"),
        P("dp", "tensor"),
        P("tensor", "dp"),
        P(),
        P(),
        P(),
        P(),
    )
    return jax.shard_map(
        per_device, mesh=mesh, in_specs=in_specs, out_specs=out_specs, check_vma=False
    )
```

profile of v0, /device:TPU:0, one launch (start us, length us, event | category | flops | bytes accessed | tf_op | source)
XLA Modules:
  0.0 2719.3 jit_solution(7229806353198946887)
XLA Ops:
  27.0 64.7 %all-gather.16.cloned.1.call-done = bf16[2048,512]{1,0:T(8,128)(2,1)} async-done(((bf16[128,512]{1,0:T(8,128)(2,1)}), bf16[2048,512]{1,0:T(8,128)(2,1)}) %all-gather.16.cloned.1.call-update) | async-done | bytes 2097168 | tf_op jit(solution)/shard_map/all_gather | solution.py:105
  98.6 55.3 %all-gather.14.cloned.1.call-done = bf16[2048,512]{1,0:T(8,128)(2,1)} async-done(((bf16[128,512]{1,0:T(8,128)(2,1)}), bf16[2048,512]{1,0:T(8,128)(2,1)}) %all-gather.14.cloned.1.call-update) | async-done | bytes 2097168 | tf_op jit(solution)/shard_map/all_gather | solution.py:106
  159.1 72.2 %all-gather.18.cloned.1.call-done = bf16[2048,1024]{1,0:T(8,128)(2,1)} async-done(((bf16[128,1024]{1,0:T(8,128)(2,1)}), bf16[2048,1024]{1,0:T(8,128)(2,1)}) %all-gather.18.cloned.1.call-update) | async-done | bytes 4194320 | tf_op jit(solution)/shard_map/all_gather | solution.py:104
  263.0 58.7 %all-gather.20.cloned.1.call-done = bf16[1024,2048]{1,0:T(8,128)(2,1)} async-done(((bf16[1024,128]{1,0:T(8,128)(2,1)}), bf16[1024,2048]{1,0:T(8,128)(2,1)}) %all-gather.20.cloned.1.call-update) | async-done | bytes 4194320 | tf_op jit(solution)/shard_map/all_gather | solution.py:107
  357.5 156.4 %all-gather.26.cloned.1.call-done = bf16[2048,3072]{1,0:T(8,128)(2,1)} async-done(((bf16[128,3072]{1,0:T(8,128)(2,1)}), bf16[2048,3072]{1,0:T(8,128)(2,1)}) %all-gather.26.cloned.1.call-update) | async-done | bytes 12582928 | tf_op jit(solution)/shard_map/all_gather | solution.py:109
  513.9 14.0 fusion.57
  527.9 139.4 %all-gather.24.cloned.1.call-done = bf16[2048,3072]{1,0:T(8,128)(2,1)} async-done(((bf16[128,3072]{1,0:T(8,128)(2,1)}), bf16[2048,3072]{1,0:T(8,128)(2,1)}) %all-gather.24.cloned.1.call-update) | async-done | bytes 12582928 | tf_op jit(solution)/shard_map/all_gather | solution.py:108
  667.3 13.9 fusion.56
  681.3 197.9 %all-gather.28.cloned.1.call-done = bf16[3072,2048]{1,0:T(8,128)(2,1)} async-done(((bf16[3072,128]{1,0:T(8,128)(2,1)}), bf16[3072,2048]{1,0:T(8,128)(2,1)}) %all-gather.28.cloned.1.call-update) | async-done | bytes 12582928 | tf_op jit(solution)/shard_map/all_gather | solution.py:110
  879.2 20.8 multiply_convert_fusion
  900.0 12.8 fusion.58
  912.8 13.1 convolution_add_fusion
  943.3 12.7 all-gather.32.cloned.1.call-done
  1020.9 13.6 convolution_convert_fusion
  1065.8 15.5 fusion.64
  1081.4 15.5 fusion.63
  1098.7 15.7 fusion.65
  1118.1 43.0 %all-reduce.4 = (f32[2048]{0:T(1024)}, f32[2048]{0:T(1024)}, f32[128]{0:T(128)}, f32[128]{0:T(128)}) all-reduce(f32[2048]{0:T(1024)S(1)} %get-tuple-element.19, f32[2048]{0:T(1024)S(1)} %copy-done.40, f32[128]{0:T(128)S(1)} %get-tuple-element.13, f32[128]{0:T(128)S(1)} %get-tuple-element.17), channel_id=1, replica_groups=mesh['dp'=16,'tensor'=2] {'dp','tensor'}, use_global_device_ids=true, to_apply=%region_25.26 | all-reduce | flops 4352 | bytes 34816 | tf_op jit(solution)/shard_map/psum | solution.py:274
  1166.7 77.2 %reduce-scatter.22.cloned.1.call-done = f32[128,512]{1,0:T(8,128)} async-done(((f32[2048,512]{1,0:T(8,128)}), f32[128,512]{1,0:T(8,128)}) %reduce-scatter.22.cloned.1.call-update) | async-done | bytes 262160 | tf_op jit(solution)/shard_map/reduce_scatter | solution.py:270
  1243.9 180.2 %reduce-scatter.26.cloned.1.call-done = f32[1024,128]{1,0:T(8,128)} async-done(((f32[1024,2048]{1,0:T(8,128)}), f32[1024,128]{1,0:T(8,128)}) %reduce-scatter.26.cloned.1.call-update) | async-done | bytes 524304 | tf_op jit(solution)/shard_map/reduce_scatter | solution.py:272
  1424.1 183.1 %reduce-scatter.20.cloned.1.call-done = f32[128,1024]{1,0:T(8,128)} async-done(((f32[2048,1024]{1,0:T(8,128)}), f32[128,1024]{1,0:T(8,128)}) %reduce-scatter.20.cloned.1.call-update) | async-done | bytes 524304 | tf_op jit(solution)/shard_map/reduce_scatter | solution.py:269
  1607.2 370.4 %reduce-scatter.30.cloned.1.call-done = f32[128,3072]{1,0:T(8,128)} async-done(((f32[2048,3072]{1,0:T(8,128)}), f32[128,3072]{1,0:T(8,128)}) %reduce-scatter.30.cloned.1.call-update) | async-done | bytes 1572880 | tf_op jit(solution)/shard_map/reduce_scatter | solution.py:209
  1977.6 367.1 %reduce-scatter.28.cloned.1.call-done = f32[128,3072]{1,0:T(8,128)} async-done(((f32[2048,3072]{1,0:T(8,128)}), f32[128,3072]{1,0:T(8,128)}) %reduce-scatter.28.cloned.1.call-update) | async-done | bytes 1572880 | tf_op jit(solution)/shard_map/reduce_scatter | solution.py:208
  2344.7 367.4 %reduce-scatter.32.cloned.1.call-done = f32[3072,128]{1,0:T(8,128)} async-done(((f32[3072,2048]{1,0:T(8,128)}), f32[3072,128]{1,0:T(8,128)}) %reduce-scatter.32.cloned.1.call-update) | async-done | bytes 1572880 | tf_op jit(solution)/shard_map/reduce_scatter | solution.py:210
  (258 shorter events, 223.1 us)
Async XLA Ops:
  7.2 19.9 all-gather.12.cloned.1.call-start
  12.8 78.9 %all-gather.16.cloned.1.call-start = ((), (), s32[]{:S(2)}) async-start(), calls=%async_computation.13 | async-start | bytes 2228224 | tf_op jit(solution)/shard_map/all_gather | solution.py:105
  13.6 140.3 %all-gather.14.cloned.1.call-start = ((), (), s32[]{:S(2)}) async-start(), calls=%async_computation.12 | async-start | bytes 2228224 | tf_op jit(solution)/shard_map/all_gather | solution.py:106
  14.3 217.0 %all-gather.18.cloned.1.call-start = ((), (), s32[]{:S(2)}) async-start(), calls=%async_computation.14 | async-start | bytes 4456448 | tf_op jit(solution)/shard_map/all_gather | solution.py:104
  14.9 306.8 %all-gather.20.cloned.1.call-start = ((), (), s32[]{:S(2)}) async-start(), calls=%async_computation.15 | async-start | bytes 4456448 | tf_op jit(solution)/shard_map/all_gather | solution.py:107
  15.5 325.2 %reduce-scatter.12.cloned.1.call-start = ((), (), s32[]{:S(2)}) async-start(), calls=%async_computation.16 | async-start | bytes 7864320 | tf_op jit(solution)/shard_map/reduce_scatter | solution.py:160
  329.1 28.4 %all-gather.22.cloned.1.call-start = ((), (), s32[]{:S(2)}) async-start(), calls=%async_computation.17 | async-start | bytes 3932160 | tf_op jit(solution)/shard_map/all_gather | solution.py:165
  343.2 597.5 %copy-start.2 = (f32[320,2048]{1,0:T(8,128)}, f32[320,2048]{1,0:T(8,128)S(1)}, u32[]{:S(2)}) copy-start(f32[320,2048]{1,0:T(8,128)S(1)} %get-tuple-element.26) | copy-start | bytes 7864324
  343.2 597.5 %copy-start.36 = (f32[320]{0:T(512)}, f32[320]{0:T(512)S(1)}, u32[]{:S(2)}) copy-start(f32[320]{0:T(512)S(1)} %fusion.47) | copy-start | bytes 3844
  344.8 169.1 %all-gather.26.cloned.1.call-start = ((), (), s32[]{:S(2)}) async-start(), calls=%async_computation.19 | async-start | bytes 13369344 | tf_op jit(solution)/shard_map/all_gather | solution.py:109
  345.5 321.8 %all-gather.24.cloned.1.call-start = ((), (), s32[]{:S(2)}) async-start(), calls=%async_computation.18 | async-start | bytes 13369344 | tf_op jit(solution)/shard_map/all_gather | solution.py:108
  346.3 335.0 %all-gather.30.cloned.1.call-start = ((), (), s32[]{:S(2)}) async-start(), calls=%async_computation.22 | async-start | bytes 3932160 | tf_op jit(solution)/shard_map/all_gather | solution.py:187
  349.2 529.9 %all-gather.28.cloned.1.call-start = ((), (), s32[]{:S(2)}) async-start(), calls=%async_computation.20 | async-start | bytes 13369344 | tf_op jit(solution)/shard_map/all_gather | solution.py:110
  350.0 587.6 %reduce-scatter.16.cloned.1.call-start = ((), (), s32[]{:S(2)}) async-start(), calls=%async_computation.23 | async-start | bytes 7864320 | tf_op jit(solution)/shard_map/reduce_scatter | solution.py:199
  926.0 30.0 %all-gather.32.cloned.1.call-start = ((), (), s32[]{:S(2)}) async-start(), calls=%async_computation.24 | async-start | bytes 3932160 | tf_op jit(solution)/shard_map/all_gather | solution.py:212
  943.2 171.3 %reduce-scatter.18.cloned.1.call-start = ((), (), s32[]{:S(2)}) async-start(), calls=%async_computation.25 | async-start | bytes 3932160 | tf_op jit(solution)/shard_map/reduce_scatter | solution.py:256
  1020.9 140.2 %reduce-scatter.14.cloned.1.call-start = ((), (), s32[]{:S(2)}) async-start(), calls=%async_computation.21 | async-start | bytes 3932160 | tf_op jit(solution)/shard_map/reduce_scatter | solution.py:169
  1034.5 132.2 %reduce-scatter.24.cloned.1.call-start = ((), (), s32[]{:S(2)}) async-start(), calls=%async_computation.28 | async-start | bytes 4456448 | tf_op jit(solution)/shard_map/reduce_scatter | solution.py:271
  1040.3 203.6 %reduce-scatter.22.cloned.1.call-start = ((), (), s32[]{:S(2)}) async-start(), calls=%async_computation.27 | async-start | bytes 4456448 | tf_op jit(solution)/shard_map/reduce_scatter | solution.py:270
  1046.4 377.7 %reduce-scatter.26.cloned.1.call-start = ((), (), s32[]{:S(2)}) async-start(), calls=%async_computation.29 | async-start | bytes 8912896 | tf_op jit(solution)/shard_map/reduce_scatter | solution.py:272
  1055.0 552.2 %reduce-scatter.20.cloned.1.call-start = ((), (), s32[]{:S(2)}) async-start(), calls=%async_computation.26 | async-start | bytes 8912896 | tf_op jit(solution)/shard_map/reduce_scatter | solution.py:269
  1064.1 913.5 %reduce-scatter.30.cloned.1.call-start = ((), (), s32[]{:S(2)}) async-start(), calls=%async_computation.31 | async-start | bytes 26738688 | tf_op jit(solution)/shard_map/reduce_scatter | solution.py:209
  1081.4 1263.3 %reduce-scatter.28.cloned.1.call-start = ((), (), s32[]{:S(2)}) async-start(), calls=%async_computation.30 | async-start | bytes 26738688 | tf_op jit(solution)/shard_map/reduce_scatter | solution.py:208
  1097.0 1615.1 %reduce-scatter.32.cloned.1.call-start = ((), (), s32[]{:S(2)}) async-start(), calls=%async_computation.32 | async-start | bytes 26738688 | tf_op jit(solution)/shard_map/reduce_scatter | solution.py:210
  (65 other events, 1287.0 us)
Sparse Core Ops, SparseCore 0:
  13.0 14.0 all-gather.11
  29.8 61.8 all-gather.15
  94.5 59.3 all-gather.13
  156.5 74.7 all-gather.17
  233.8 87.7 all-gather.19
  329.2 11.3 reduce-scatter.11
  344.9 12.5 all-gather.21
  360.7 153.1 all-gather.25
  517.1 150.1 all-gather.23
  669.3 9.5 all-gather.29
  682.0 197.1 all-gather.27
  926.1 11.3 reduce-scatter.15
  943.4 12.5 all-gather.31
  1021.0 11.3 reduce-scatter.17
  1034.6 11.3 reduce-scatter.13
  1048.8 97.0 reduce-scatter.23
  1148.6 95.2 reduce-scatter.21
  1246.6 177.3 reduce-scatter.25
  1426.9 180.2 reduce-scatter.19
  1613.4 364.1 reduce-scatter.29
  1983.9 360.7 reduce-scatter.27
  2351.0 361.0 reduce-scatter.31
where the time goes:
time: 2730 us; the launch traced here: 2720 us
  waiting for transfers between devices  2350 us (86%)
  matrix products  233 us (9%)
  other arithmetic  54.8 us (2%)
  blocking collectives  43 us (2%)
    reduce_scatter x1, waiting for transfers between devices, per_device(): lax.psum_scatter(grad_up_full, 'dp', scatter_dimension=0, tiled=True)  370 us
    reduce_scatter x1, waiting for transfers between devices, per_device(): lax.psum_scatter(grad_down_full, 'dp', scatter_dimension=1, tiled=True)  367 us
    reduce_scatter x1, waiting for transfers between devices, per_device(): lax.psum_scatter(grad_gate_full, 'dp', scatter_dimension=0, tiled=True)  367 us
    all_gather x1, waiting for transfers between devices, per_device(): lax.all_gather(w_down, 'dp', axis=1, tiled=True)  198 us
    reduce_scatter x1, waiting for transfers between devices, per_device(): lax.psum_scatter(grad_query_full, 'dp', scatter_dimension=0, tiled=True)  183 us
    reduce_scatter x1, waiting for transfers between devices, per_device(): lax.psum_scatter(grad_out_full, 'dp', scatter_dimension=1, tiled=True)  180 us
    all_gather x1, waiting for transfers between devices, per_device(): lax.all_gather(w_up, 'dp', axis=0, tiled=True)  156 us
    all_gather x1, waiting for transfers between devices, per_device(): lax.all_gather(w_gate, 'dp', axis=0, tiled=True)  139 us
  transfers between devices with their start and end apart: 22, of which 18 were waited for; matrix products, arithmetic and copies ran while one was open for 6% of the time, Pallas kernels for 0%

commit v1 on v0

v1 whole, which is shorter than its diff:
```python
import functools

import jax
import jax.numpy as jnp
from jax import lax
from jax.experimental import pallas as pl
from jax.experimental.pallas import tpu as pltpu
from jax.sharding import PartitionSpec as P

EPSILON = 1e-06
ROPE_BASE = 1000000.0
X_BIT, Y_BIT, PAIR = 1, 2, 4
MLP_PARTS = 3
LANES = 128


def rms_norm(values, gain_vec):
    return (
        values * lax.rsqrt(jnp.mean(values * values, axis=-1, keepdims=True) + EPSILON) * gain_vec
    )


def rope_tables(positions, width):
    half_width = width // 2
    frequency = ROPE_BASE ** (-2.0 * jnp.arange(half_width, dtype=jnp.float32) / width)
    angles = positions.astype(jnp.float32)[:, None] * frequency[None, :]
    return (jnp.cos(angles), jnp.sin(angles))


def token_layout(seq_ends, token_index):
    segment = jnp.sum((token_index[:, None] >= seq_ends[None, :]).astype(jnp.int32), axis=1)
    starts = jnp.concatenate([jnp.zeros((1,), jnp.int32), seq_ends[:-1]])
    onehot = (segment[:, None] == jnp.arange(seq_ends.shape[0], dtype=jnp.int32)[None, :]).astype(
        jnp.int32
    )
    positions = token_index - jnp.sum(onehot * starts[None, :], axis=1)
    return (segment, positions)


def matmul(left, right):
    return jnp.dot(left, right, preferred_element_type=jnp.float32)


def mat_rows(left, right):
    return lax.dot_general(
        left, right, (((0,), (0,)), ((), ())), preferred_element_type=jnp.float32
    )


def mat_cols(left, right):
    return lax.dot_general(
        left, right, (((1,), (1,)), ((), ())), preferred_element_type=jnp.float32
    )


def low(values):
    return values.astype(jnp.bfloat16)


def wide(values):
    return values.astype(jnp.float32)


def exchange(values, mask):
    size = lax.axis_size("dp")
    return lax.ppermute(values, "dp", [(i, i ^ mask) for i in range(size)])


def bit_side(bit):
    return jnp.minimum(lax.axis_index("dp") & bit, 1)


def team_side():
    return bit_side(PAIR)


def in_turn(mine, theirs, axis, bit=PAIR):
    return jnp.where(
        bit_side(bit) == 0,
        jnp.concatenate([mine, theirs], axis=axis),
        jnp.concatenate([theirs, mine], axis=axis),
    )


VMEM_BYTES = 56 * 1024 * 1024
UNIT_TILE = 256


def params():
    return pltpu.CompilerParams(vmem_limit_bytes=VMEM_BYTES)


def small_cost():
    return pl.CostEstimate(flops=1000, bytes_accessed=1000, transcendentals=0)


def unit_tile(units):
    return UNIT_TILE if units % UNIT_TILE == 0 else units


def whole(shape):
    return pl.BlockSpec(shape, lambda *_: (0,) * len(shape), pipeline_mode=pl.Buffered(1))


def anywhere():
    return pl.BlockSpec(memory_space=pl.ANY)


def in_lanes(width):
    return (width // lax.axis_size("dp")) % LANES == 0


def to_order(values, parts=4):
    width = values.shape[-1]
    if in_lanes(width):
        return values
    devices = lax.axis_size("dp")
    split = values.reshape(*values.shape[:-1], devices // parts, parts, width // devices)
    return jnp.swapaxes(split, -2, -3).reshape(values.shape)


def from_order(values, parts=4):
    width = values.shape[-1]
    if in_lanes(width):
        return values
    devices = lax.axis_size("dp")
    split = values.reshape(*values.shape[:-1], parts, devices // parts, width // devices)
    return jnp.swapaxes(split, -2, -3).reshape(values.shape)


def pieces_of(parts, width, devices):
    part_width, block = width // parts, width // devices
    if block % LANES:
        return [(p, 0, p * part_width, part_width) for p in range(parts)]
    return [
        (d % parts, (d // parts) * block, d * block, block) for d in range(devices)
    ]


def side_by_side(pieces, ref):
    return jnp.concatenate([ref[p][:, at : at + size] for p, at, _, size in pieces], axis=1)


def fetch(parts, scratch, sems):
    rows = parts[0].shape[0]
    copies = [
        pltpu.make_async_copy(part, scratch.at[pl.ds(i * rows, rows), :], sems.at[i])
        for i, part in enumerate(parts)
    ]
    for copy in copies:
        copy.start()
    return copies


def hidden_tile(pieces, row_tile, mlp_all, branch_all, gate_ref, up_ref, down_ref, store):
    gate_w, up_w, down_w = (side_by_side(pieces, r) for r in (gate_ref, up_ref, down_ref))

    def step(index, carry):
        rows = pl.ds(pl.multiple_of(index * row_tile, row_tile), row_tile)
        mlp_rows = mlp_all[rows, :]
        gate_proj = mat_cols(mlp_rows, gate_w)
        up_proj = mat_cols(mlp_rows, up_w)
        hidden_grad = mat_cols(branch_all[rows, :], down_w)
        sigmoid_gate = 1.0 / (1.0 + jnp.exp(-gate_proj))
        silu_gate = gate_proj * sigmoid_gate
        store(
            0,
            rows,
            low(hidden_grad * up_proj * sigmoid_gate * (1.0 + gate_proj * (1.0 - sigmoid_gate))),
        )
        store(1, rows, low(hidden_grad * silu_gate))
        store(2, rows, low(silu_gate * up_proj))
        return carry

    lax.fori_loop(0, mlp_all.shape[0] // row_tile, step, 0)


def store_grad(pieces, out_ref, grad):
    for p, at, first, size in pieces:
        out_ref[p, :, at : at + size] = grad[:, first : first + size]


def mlp_kernel(pieces, tiles, with_grad, *refs):
    mlp_parts, branch_parts = refs[:4], refs[4:8]
    weights = refs[8:11]
    if with_grad:
        acts_ref, grad_ref, mlp_all, branch_all, acts_all, sems = refs[11:]
    else:
        acts_ref, mlp_all, branch_all, sems = refs[11:]
    step = pl.program_id(0)
    rows = mlp_parts[0].shape[0]
    tile = weights[0].shape[1]

    @pl.when(step == 0)
    def _():
        copies = fetch(mlp_parts, mlp_all, sems.at[0]) + fetch(branch_parts, branch_all, sems.at[1])
        for copy in copies:
            copy.wait()

    def forward():
        def store(kind, where, values):
            acts_ref[kind, where, :] = values
            if with_grad:
                acts_all[step, kind, where, :] = values

        hidden_tile(pieces, rows, mlp_all, branch_all, *weights, store)

    if not with_grad:
        forward()
        return

    pl.when(step < tiles)(forward)

    @pl.when((step >= tiles) & (step < 3 * tiles))
    def _():
        index = step - tiles
        acts = acts_all[lax.rem(index, tiles), lax.div(index, tiles)]
        store_grad(pieces, grad_ref, low(mat_rows(acts, mlp_all[...])))

    @pl.when(step >= 3 * tiles)
    def _():
        acts = acts_all[step - 3 * tiles, 2]
        store_grad(pieces, grad_ref, low(mat_rows(acts, branch_all[...])))


def mlp_units(mlp_parts, branch_parts, weight, with_grad):
    part_rows, width = mlp_parts[0].shape
    rows = 4 * part_rows
    parts, units3, part_width = weight.shape
    units = units3 // 3
    tile = unit_tile(units)
    tiles = units // tile
    pieces = pieces_of(parts, width, lax.axis_size("dp"))

    def weight_spec(kind):
        return pl.BlockSpec(
            (parts, tile, part_width), lambda i: (0, kind * tiles + jnp.minimum(i, tiles - 1), 0)
        )

    out_shape = [jax.ShapeDtypeStruct((3, rows, units), jnp.bfloat16)]
    out_specs = [pl.BlockSpec((3, rows, tile), lambda i: (0, 0, jnp.minimum(i, tiles - 1)))]
    scratch = [pltpu.VMEM((rows, width), jnp.bfloat16)] * 2
    if with_grad:
        out_shape.append(jax.ShapeDtypeStruct(weight.shape, jnp.bfloat16))
        out_specs.append(
            pl.BlockSpec((parts, tile, part_width), lambda i: (0, jnp.maximum(i - tiles, 0), 0))
        )
        scratch.append(pltpu.VMEM((tiles, 3, rows, tile), jnp.bfloat16))
    return pl.pallas_call(
        functools.partial(mlp_kernel, pieces, tiles, with_grad),
        grid=(4 * tiles if with_grad else tiles,),
        out_shape=out_shape,
        in_specs=[anywhere()] * 8 + [weight_spec(k) for k in range(3)],
        out_specs=out_specs,
        scratch_shapes=scratch + [pltpu.SemaphoreType.DMA((2, 4))],
        compiler_params=params(),
        cost_estimate=small_cost(),
    )(*mlp_parts, *branch_parts, weight, weight, weight)


def project_kernel(pieces, row_tile, parts, *refs):
    keep_ref, send_ref = refs[-2:]
    count = (len(refs) - 2) // 2
    lefts, rights = refs[:count], refs[count : 2 * count]
    part = pl.program_id(0)

    def step(index, carry):
        rows = pl.ds(pl.multiple_of(index * row_tile, row_tile), row_tile)
        total = None
        for left, right in zip(lefts, rights):
            left_rows = left[rows, :] if len(left.shape) == 2 else left[0, rows, :]
            term = matmul(left_rows, right[0])
            total = term if total is None else total + term

        def store(out_ref):
            size = pieces[0][3]
            if size == total.shape[1]:
                out_ref[index // 2, :, pl.ds(pl.multiple_of(part * size, size), size)] = (
                    total.astype(out_ref.dtype)
                )
            else:
                for k in range(total.shape[1] // size):
                    first = pl.multiple_of((k * parts + part) * size, size)
                    out_ref[index // 2, :, pl.ds(first, size)] = total[
                        :, k * size : (k + 1) * size
                    ].astype(out_ref.dtype)

        pl.when(index % 2 == 0)(lambda: store(keep_ref))
        pl.when(index % 2 == 1)(lambda: store(send_ref))
        return carry

    lax.fori_loop(0, 4, step, 0)


def project(terms):
    rows = terms[0][0].shape[-2] // 4
    parts, _, part_width = terms[0][2].shape
    width = parts * part_width
    pieces = pieces_of(parts, width, lax.axis_size("dp"))
    left_specs, right_specs = [], []
    for acts, kind, weight, first, units in terms:
        if kind is None:
            left_specs.append(whole(acts.shape))
        else:
            left_specs.append(
                pl.BlockSpec(
                    (1, *acts.shape[1:]), lambda j, k=kind: (k, 0, 0), pipeline_mode=pl.Buffered(1)
                )
            )
        right_specs.append(
            pl.BlockSpec((1, units, part_width), lambda j, f=first // units: (j, f, 0))
        )
    out_spec = whole((2, rows, width))
    return pl.pallas_call(
        functools.partial(project_kernel, pieces, rows, parts),
        grid=(parts,),
        out_shape=[
            jax.ShapeDtypeStruct((2, rows, width), jnp.float32),
            jax.ShapeDtypeStruct((2, rows, width), jnp.bfloat16),
        ],
        in_specs=left_specs + right_specs,
        out_specs=[out_spec, out_spec],
        compiler_params=params(),
        cost_estimate=small_cost(),
    )(*[t[0] for t in terms], *[t[2] for t in terms])


def weight_grad_kernel(pieces, cuts, left_ref, *refs):
    count = len(cuts)
    out_ref, right_all, sems = refs[4 * count :]
    step = pl.program_id(0)

    @pl.when(step == 0)
    def _():
        copies = []
        for k in range(count):
            copies += fetch(refs[4 * k : 4 * k + 4], right_all.at[k], sems.at[k])
        for copy in copies:
            copy.wait()

    left = left_ref[...].reshape(left_ref.shape[-2:])
    for k, (start, stop) in enumerate(cuts):

        @pl.when((step >= start) & (step < stop))
        def _():
            store_grad(pieces, out_ref, low(mat_rows(left, right_all[k])))


def weight_grad(parts, left, *rights):
    part_rows, width = rights[0][0][0].shape
    rows, units = left.shape[-2:]
    tile = unit_tile(units)
    tiles = units // tile
    pieces = pieces_of(parts, width, lax.axis_size("dp"))
    cuts, first = [], 0
    for _, kinds in rights:
        cuts.append((first, first + kinds * tiles))
        first += kinds * tiles
    if left.ndim == 3:
        left_spec = pl.BlockSpec((1, rows, tile), lambda i: (i // tiles, 0, i % tiles))
    else:
        left_spec = pl.BlockSpec((rows, tile), lambda i: (0, i))
    return pl.pallas_call(
        functools.partial(weight_grad_kernel, pieces, tuple(cuts)),
        grid=(first,),
        out_shape=jax.ShapeDtypeStruct((parts, first * tile, width // parts), jnp.bfloat16),
        in_specs=[left_spec] + [anywhere()] * (4 * len(rights)),
        out_specs=pl.BlockSpec((parts, tile, width // parts), lambda i: (0, i, 0)),
        scratch_shapes=[
            pltpu.VMEM((len(rights), rows, width), jnp.bfloat16),
            pltpu.SemaphoreType.DMA((len(rights), 4)),
        ],
        compiler_params=params(),
        cost_estimate=small_cost(),
    )(left, *[part for row_parts, _ in rights for part in row_parts])


def turn(values):
    half = values.shape[-1] // 2
    return jnp.concatenate([values[:, half:], values[:, :half]], axis=-1)


def heads_kernel(
    pieces, q_heads, kv_heads, *refs
):
    normed_parts, (weight_ref, gain_q, gain_k, cos_ref, sin_ref) = refs[:4], refs[4:9]
    raw, rot, value, normed_all, weight_all, sems = refs[9:]
    width = gain_q.shape[1]
    rows = normed_parts[0].shape[0]

    @pl.when(pl.program_id(0) == 0)
    def _():
        copies = fetch(normed_parts, normed_all, sems)
        weight_all[...] = side_by_side(pieces, weight_ref)
        for copy in copies:
            copy.wait()

    here = pl.ds(pl.multiple_of(pl.program_id(0) * rows, rows), rows)
    out = mat_cols(normed_all[here, :], weight_all[...])
    for head in range(q_heads + kv_heads):
        columns = slice(head * width, (head + 1) * width)
        unit = out[:, columns]
        gain = gain_q[...] if head < q_heads else gain_k[...]
        normed = (
            unit * lax.rsqrt(jnp.mean(unit * unit, axis=-1, keepdims=True) + EPSILON) * gain
        )
        raw[:, columns] = unit
        rot[:, columns] = low(normed * cos_ref[...] + turn(normed) * sin_ref[...])
    value[...] = low(out[:, (q_heads + kv_heads) * width :])


def heads(normed_parts, weight, gain_query, gain_key, cos, sin, q_heads, kv_heads):
    part_rows, width = normed_parts[0].shape
    rows = 4 * part_rows
    parts, _, part_width = weight.shape
    head_width = gain_query.shape[1]
    units = (q_heads + 2 * kv_heads) * head_width
    tile = rows // 4
    qk = (q_heads + kv_heads) * head_width
    kv = kv_heads * head_width

    def rows_spec(columns):
        return pl.BlockSpec((tile, columns), lambda i: (i, 0))

    return pl.pallas_call(
        functools.partial(
            heads_kernel, pieces_of(parts, width, lax.axis_size("dp")), q_heads, kv_heads
        ),
        grid=(4,),
        out_shape=[
            jax.ShapeDtypeStruct((rows, qk), jnp.float32),
            jax.ShapeDtypeStruct((rows, qk), jnp.bfloat16),
            jax.ShapeDtypeStruct((rows, kv), jnp.bfloat16),
        ],
        in_specs=[
            *[anywhere()] * 4,
            whole((parts, units, part_width)),
            whole((1, head_width)),
            whole((1, head_width)),
            rows_spec(head_width),
            rows_spec(head_width),
        ],
        out_specs=[rows_spec(qk), rows_spec(qk), rows_spec(kv)],
        scratch_shapes=[
            pltpu.VMEM((rows, width), jnp.bfloat16),
            pltpu.VMEM((units, width), jnp.bfloat16),
            pltpu.SemaphoreType.DMA((4,)),
        ],
        compiler_params=params(),
        cost_estimate=small_cost(),
    )(*normed_parts, weight, gain_query, gain_key, cos, sin)


def probabilities(query, key, row_segment, column_segment, row_slot, column_slot, dead, scale):
    allowed = (row_segment == column_segment) & (column_slot <= row_slot)
    masked = jnp.where(allowed, mat_cols(query, key) * scale, -1e30)
    weights = jnp.where(allowed, jnp.exp(masked - jnp.max(masked, axis=-1, keepdims=True)), 0.0)
    total = jnp.sum(weights, axis=-1, keepdims=True) + dead
    return weights * (1.0 / total)


def attend_kernel(scale, q_ref, k_ref, v_ref, row_ref, column_ref, out_ref):
    width = k_ref.shape[1]
    marks = (row_ref[0, :, 0:1], column_ref[0, 0:1, :], row_ref[0, :, 1:2], column_ref[0, 1:2, :])
    dead = wide(row_ref[0, :, 2:3])
    for head in range(q_ref.shape[1] // width):
        columns = slice(head * width, (head + 1) * width)
        probs = probabilities(q_ref[:, columns], k_ref[...], *marks, dead, scale)
        out_ref[:, columns] = low(matmul(low(probs), v_ref[...]))


def attention_specs(rows, head_width, q_heads, kv_heads):
    group_rows = rows // 2
    per = q_heads // kv_heads
    query = pl.BlockSpec((group_rows, per * head_width), lambda g, k: (g, k))
    key = pl.BlockSpec((group_rows, head_width), lambda g, k: (g, q_heads + k))
    value = pl.BlockSpec((group_rows, head_width), lambda g, k: (g, k))
    row_marks = pl.BlockSpec((1, group_rows, 8), lambda g, k: (g, 0, 0))
    column_marks = pl.BlockSpec((1, 8, group_rows), lambda g, k: (g, 0, 0))
    return query, key, value, row_marks, column_marks


def attend(rot, value, row_marks, column_marks, head_width, q_heads, kv_heads):
    rows = rot.shape[0]
    query, key, value_spec, row_spec, column_spec = attention_specs(
        rows, head_width, q_heads, kv_heads
    )
    return pl.pallas_call(
        functools.partial(attend_kernel, head_width ** (-0.5)),
        grid=(2, kv_heads),
        out_shape=jax.ShapeDtypeStruct((rows, q_heads * head_width), jnp.bfloat16),
        in_specs=[query, key, value_spec, row_spec, column_spec],
        out_specs=query,
        compiler_params=params(),
        cost_estimate=small_cost(),
    )(rot, rot, value, row_marks, column_marks)


def head_back(grad, raw, gain, cos, sin):
    grad = grad * cos - turn(grad) * sin
    scale = lax.rsqrt(jnp.mean(raw * raw, axis=-1, keepdims=True) + EPSILON)
    unit = raw * scale
    through = grad * gain
    raw_grad = scale * (through - unit * jnp.mean(through * unit, axis=-1, keepdims=True))
    return low(raw_grad), jnp.sum(grad * unit, axis=0, keepdims=True)


def attend_back_kernel(
    pieces,
    scale,
    q_heads,
    kv_heads,
    cot_a,
    cot_b,
    cot_c,
    cot_d,
    weight_ref,
    q_ref,
    k_ref,
    v_ref,
    q_raw,
    k_raw,
    row_ref,
    column_ref,
    gain_q,
    gain_k,
    cos_ref,
    sin_ref,
    grad_ref,
    gain_ref,
    cot_all,
    sems,
):
    group, kv = pl.program_id(0), pl.program_id(1)
    rows, width = k_ref.shape
    per = q_heads // kv_heads

    @pl.when((group == 0) & (kv == 0))
    def _():
        gain_ref[...] = jnp.zeros_like(gain_ref)
        for copy in fetch((cot_a, cot_b, cot_c, cot_d), cot_all, sems):
            copy.wait()

    marks = (row_ref[0, :, 0:1], column_ref[0, 0:1, :], row_ref[0, :, 1:2], column_ref[0, 1:2, :])
    dead = wide(row_ref[0, :, 2:3])
    here = pl.ds(pl.multiple_of(group * rows, rows), rows)
    context_grad = low(mat_cols(cot_all[here, :], side_by_side(pieces, weight_ref)))
    key, value, cos, sin = k_ref[...], v_ref[...], cos_ref[...], sin_ref[...]
    key_grad = value_grad = None
    gain_sum = None
    for head in range(per):
        columns = slice(head * width, (head + 1) * width)
        query, grad = q_ref[:, columns], context_grad[:, columns]
        probs = probabilities(query, key, *marks, dead, scale)
        prob_grad = mat_cols(grad, value)
        part = mat_rows(low(probs), grad)
        value_grad = part if value_grad is None else value_grad + part
        score_grad = low(
            probs * (prob_grad - jnp.sum(probs * prob_grad, axis=-1, keepdims=True))
        )
        part = mat_rows(score_grad, query)
        key_grad = part if key_grad is None else key_grad + part
        query_grad, gain_part = head_back(
            matmul(score_grad, key) * scale, q_raw[:, columns], gain_q[...], cos, sin
        )
        gain_sum = gain_part if gain_sum is None else gain_sum + gain_part
        first = pl.multiple_of((kv * per + head) * width, width)
        grad_ref[here, pl.ds(first, width)] = query_grad
    key_out, gain_part = head_back(key_grad * scale, k_raw[...], gain_k[...], cos, sin)
    gain_ref[0:1, :] += gain_sum
    gain_ref[1:2, :] += gain_part
    grad_ref[here, pl.ds(pl.multiple_of((q_heads + kv) * width, width), width)] = key_out
    first = pl.multiple_of((q_heads + kv_heads + kv) * width, width)
    grad_ref[here, pl.ds(first, width)] = low(value_grad)


def attend_back(
    cot_parts, weight, rot, value, raw, row_marks, column_marks, gain_query, gain_key, cos, sin,
    q_heads, kv_heads,
):
    part_rows, width = cot_parts[0].shape
    rows = 4 * part_rows
    parts, _, part_width = weight.shape
    head_width = gain_query.shape[1]
    units = q_heads * head_width // kv_heads
    first = (q_heads + 2 * kv_heads) * head_width // units
    group_rows = rows // 2
    query, key, value_spec, row_spec, column_spec = attention_specs(
        rows, head_width, q_heads, kv_heads
    )
    columns = (q_heads + 2 * kv_heads) * head_width

    def group_spec(size):
        return pl.BlockSpec((group_rows, size), lambda g, k: (g, 0))

    return pl.pallas_call(
        functools.partial(
            attend_back_kernel,
            pieces_of(parts, width, lax.axis_size("dp")),
            head_width ** (-0.5),
            q_heads,
            kv_heads,
        ),
        grid=(2, kv_heads),
        out_shape=[
            jax.ShapeDtypeStruct((rows, columns), jnp.bfloat16),
            jax.ShapeDtypeStruct((8, head_width), jnp.float32),
        ],
        in_specs=[
            *[anywhere()] * 4,
            pl.BlockSpec((parts, units, part_width), lambda g, k: (0, first + k, 0)),
            query,
            key,
            value_spec,
            query,
            key,
            row_spec,
            column_spec,
            whole((1, head_width)),
            whole((1, head_width)),
            group_spec(head_width),
            group_spec(head_width),
        ],
        out_specs=[whole((rows, columns)), whole((8, head_width))],
        scratch_shapes=[
            pltpu.VMEM((rows, width), jnp.bfloat16),
            pltpu.SemaphoreType.DMA((4,)),
        ],
        compiler_params=params(),
        cost_estimate=small_cost(),
    )(
        *cot_parts, weight, rot, rot, value, raw, raw, row_marks, column_marks,
        gain_query, gain_key, cos, sin,
    )


class Sequence:
    def __init__(self):
        self.last = ()

    def tie(self, *values):
        out = lax.optimization_barrier((*values, *self.last))[: len(values)]
        return out[0] if len(values) == 1 else out

    def mark(self, *values):
        self.last = values
        return values[0] if len(values) == 1 else values

    def wait(self, *values):
        out = self.tie(*values)
        return self.mark(out) if len(values) == 1 else self.mark(*out)


def swap_core(values):
    return lax.ppermute(values, "tensor", [(0, 1), (1, 0)])


def outer_bits():
    size = lax.axis_size("dp")
    return [1 << i for i in range(size.bit_length() - 1) if (1 << i) > PAIR]


def xy_groups():
    size = lax.axis_size("dp")
    return [[first + i for i in range(4)] for first in range(0, size, 4)]


def far_masks():
    masks = [0, PAIR]
    for bit in outer_bits():
        masks = masks + [m ^ bit for m in masks]
    return masks


def near_start(own, other):
    return [exchange(other if m & PAIR else own, m) for m in far_masks()[1:]]


def near_end(own, received):
    blocks = [own, *received]
    for bit in [PAIR] + outer_bits():
        blocks = [in_turn(x, y, 1, bit) for x, y in zip(blocks[::2], blocks[1::2])]
    return blocks[0]


def gather_weight(block):
    return lax.all_gather(block, "dp", axis_index_groups=xy_groups(), axis=0)


def near_x_y(block):
    return (exchange(block, X_BIT), exchange(block, Y_BIT))


def far_x_y(from_x, from_y):
    half = from_x.shape[1] // 2
    return (exchange(from_y[:, :half], X_BIT), exchange(from_x[:, half:], Y_BIT))


def assemble_kernel(slot_ref, own_ref, x_ref, y_ref, left_ref, right_ref, out_ref):
    own, from_x, from_y = own_ref[...], x_ref[...], y_ref[...]
    far = jnp.concatenate([left_ref[...], right_ref[...]], axis=1)
    x_side, y_side = slot_ref[0] % 2 == 1, slot_ref[0] // 2 == 1
    near = [jnp.where(x_side, from_x, own), jnp.where(x_side, own, from_x)]
    other = [jnp.where(x_side, far, from_y), jnp.where(x_side, from_y, far)]
    for k in range(2):
        out_ref[k] = jnp.where(y_side, other[k], near[k])
        out_ref[2 + k] = jnp.where(y_side, near[k], other[k])


def assemble(block, from_x, from_y, left, right):
    units, columns = block.shape
    tile = unit_tile(units)
    slot = (lax.axis_index("dp") & (X_BIT | Y_BIT)).reshape(1).astype(jnp.int32)

    def rows_of(size):
        return pl.BlockSpec((tile, size), lambda i: (i, 0))

    return pl.pallas_call(
        assemble_kernel,
        grid=(units // tile,),
        out_shape=jax.ShapeDtypeStruct((4, units, columns), block.dtype),
        in_specs=[pl.BlockSpec(memory_space=pltpu.SMEM)]
        + [rows_of(columns)] * 3
        + [rows_of(columns // 2)] * 2,
        out_specs=pl.BlockSpec((4, tile, columns), lambda i: (0, i, 0)),
        compiler_params=params(),
        cost_estimate=small_cost(),
    )(slot, block, from_x, from_y, left, right)


def scatter_grad(full):
    return lax.psum_scatter(
        full, "dp", axis_index_groups=xy_groups(), scatter_dimension=0
    )


def part_of(full, flip):
    place = (lax.axis_index("dp") & (X_BIT | Y_BIT)) ^ flip
    return lax.dynamic_index_in_dim(full, place, 0, keepdims=False)


def scatter_near(full):
    half = full.shape[1] // 2
    far = part_of(full, X_BIT | Y_BIT)
    by_x, by_y = part_of(full, X_BIT), part_of(full, Y_BIT)
    return (
        exchange(far[:half], X_BIT),
        exchange(far[half:], Y_BIT),
        exchange(by_x[:half], X_BIT),
        exchange(by_y[half:], Y_BIT),
        by_x[half:],
        by_y[:half],
    )


def scatter_far(far_top, far_bottom, x_top, y_bottom, x_rest, y_rest):
    x_bottom = exchange(low(wide(x_rest) + wide(far_bottom)), X_BIT)
    y_top = exchange(low(wide(y_rest) + wide(far_top)), Y_BIT)
    return (x_top, x_bottom, y_top, y_bottom)


def scatter_end(full, x_top, x_bottom, y_top, y_bottom):
    own = wide(part_of(full, 0))
    half = own.shape[0] // 2
    return jnp.concatenate(
        [
            own[:half] + wide(x_top) + wide(y_top),
            own[half:] + wide(x_bottom) + wide(y_bottom),
        ],
        axis=0,
    )


def last_start(total):
    total = total.reshape(total.shape[-2:])
    masks = far_masks()
    size = total.shape[1] // len(masks)
    place = lax.axis_index("dp") // 4

    def columns(mask):
        return lax.dynamic_slice_in_dim(total, (place ^ (mask // 4)) * size, size, 1)

    return [wide(columns(0))] + [exchange(low(columns(m)), m) for m in masks[1:]]


def last_end(own, received):
    mine, other = own, None
    for mask, values in zip(far_masks()[1:], received):
        if mask & PAIR:
            other = wide(values) if other is None else other + wide(values)
        else:
            mine = mine + wide(values)
    return mine, other


def team_halves(projected):
    keep, send = projected
    received = swap_core(send)
    return (keep[0] + wide(received[0]), low(keep[1] + wide(received[1])))


def total_sum(values):
    values = values + swap_core(values)
    bit = 1
    while bit < lax.axis_size("dp"):
        values = values + exchange(values, bit)
        bit *= 2
    return values


def per_device(
    tokens,
    seq_ends,
    w_query,
    w_key,
    w_value,
    w_out,
    w_gate,
    w_up,
    w_down,
    gain_attn,
    gain_mlp,
    gain_query,
    gain_key,
    cotangent,
):
    rows_dev, width = tokens.shape
    core = lax.axis_index("tensor")
    side = team_side()
    parts = len(xy_groups()[0])
    head_width = gain_query.shape[0]
    seq = Sequence()

    def halves(weight, axis):
        size = weight.shape[axis] // 2
        return (
            lax.dynamic_slice_in_dim(weight, side * size, size, axis),
            lax.dynamic_slice_in_dim(weight, (1 - side) * size, size, axis),
        )

    q_half, k_half, v_half = halves(w_query, 1), halves(w_key, 1), halves(w_value, 1)
    q_cols, kv_cols = q_half[0].shape[1], k_half[0].shape[1]
    qkv_cols = q_cols + 2 * kv_cols
    q_heads, kv_heads = q_cols // head_width, kv_cols // head_width
    out_half = halves(w_out, 0)
    attn_own, attn_other = [
        jnp.concatenate(
            [jnp.concatenate([q_half[s], k_half[s], v_half[s]], axis=1).T, out_half[s]], axis=0
        )
        for s in (0, 1)
    ]
    ends_mate = exchange(wide(seq_ends), PAIR)
    attn_far = near_start(attn_own, attn_other)
    g_half, u_half, d_half = halves(w_gate, 1), halves(w_up, 1), halves(w_down, 0)
    all_units = g_half[0].shape[1]
    units = all_units // MLP_PARTS

    def chunk_own(chunk, s):
        cut = slice(chunk * units, (chunk + 1) * units)
        return jnp.concatenate([g_half[s][:, cut].T, u_half[s][:, cut].T, d_half[s][cut]], axis=0)

    token_float = to_order(wide(tokens))
    cot_float = to_order(wide(cotangent))
    gain_attn_o, gain_mlp_o = to_order(gain_attn), to_order(gain_mlp)
    near = jnp.arange(rows_dev, dtype=jnp.int32)
    slots = jnp.concatenate([core * rows_dev + near, (1 - core) * rows_dev + near])
    layouts = [token_layout(e, slots) for e in (seq_ends[0], ends_mate[0].astype(jnp.int32))]
    segment = jnp.stack([s for s, _ in layouts])
    positions = jnp.concatenate([p for _, p in layouts])
    live_group = segment < seq_ends.shape[1]
    live_mine = wide(live_group)[0, :rows_dev, None]

    normed, attn_norm_pull = jax.vjp(rms_norm, token_float, gain_attn_o)
    normed_low = low(normed)
    branch_low = low(live_mine * cot_float)
    normed_core = swap_core(normed_low)
    cosine_table, sine_table = rope_tables(positions, head_width)
    cos = jnp.concatenate([cosine_table, cosine_table], axis=1)
    sin = jnp.concatenate([-sine_table, sine_table], axis=1)
    slots_both = jnp.stack([slots, slots])
    marks = [
        jnp.where(live_group, segment, -1),
        slots_both,
        1 - live_group.astype(jnp.int32),
    ] + [jnp.zeros_like(segment)] * 5
    row_marks = jnp.stack(marks, axis=2)
    column_marks = jnp.stack([segment, slots_both] + marks[3:] + marks[3:4], axis=1)
    gain_q, gain_k = gain_query[None, :], gain_key[None, :]
    chunks = [(chunk_own(c, 0), chunk_own(c, 1)) for c in range(MLP_PARTS)]
    seq.mark(cos, sin, row_marks, column_marks, normed_low, *[v for c in chunks for v in c])

    attn_far = seq.wait(*attn_far)
    attn_near = near_end(attn_own, attn_far)
    attn_x, attn_y = near_x_y(attn_near)
    first_far = near_start(*chunks[0])
    normed_mate = exchange(seq.tie(normed_low), PAIR)
    attn_x, attn_y, *first_far = seq.wait(attn_x, attn_y, *first_far)
    attn_left, attn_right = far_x_y(attn_x, attn_y)
    mlp_full = [gather_weight(near_end(chunks[0][0], first_far))]
    second_far = near_start(*chunks[1])
    attn_left, attn_right, normed_mate, *second_far = seq.wait(
        attn_left, attn_right, normed_mate, *second_far
    )
    full_attn = assemble(attn_near, attn_x, attn_y, attn_left, attn_right)
    normed_all = (normed_low, normed_core, normed_mate, swap_core(normed_mate))
    second_near = near_end(chunks[1][0], second_far)
    chunk_x, chunk_y = near_x_y(second_near)
    third_far = near_start(*chunks[2])
    qk_raw, qk_rot, value_low = heads(
        normed_all, full_attn, gain_q, gain_k, cos, sin, q_heads, kv_heads
    )
    value_low = seq.mark(value_low)
    context_low = seq.mark(
        attend(
            qk_rot, seq.tie(value_low), row_marks, column_marks, head_width, q_heads, kv_heads
        )
    )
    attn_mine, attn_mate = team_halves(project([(context_low, None, full_attn, qkv_cols, q_cols)]))
    seq.mark(attn_mate)
    attn_mate = exchange(attn_mate, PAIR)
    chunk_x, chunk_y, *third_far = seq.wait(chunk_x, chunk_y, *third_far)
    chunk_left, chunk_right = far_x_y(chunk_x, chunk_y)
    mlp_full += [None, gather_weight(near_end(chunks[2][0], third_far))]
    branch_mate = exchange(seq.tie(branch_low), PAIR)
    attn_mate = seq.wait(attn_mate)
    hidden_in = token_float + (attn_mine + wide(attn_mate))
    mlp_normed, mlp_norm_pull = jax.vjp(rms_norm, hidden_in, gain_mlp_o)
    mlp_low = seq.mark(low(mlp_normed))
    mlp_row_mate = exchange(mlp_low, PAIR)
    mlp_row_mate = seq.wait(mlp_row_mate)
    mlp_all = (mlp_low, swap_core(mlp_low), mlp_row_mate, swap_core(mlp_row_mate))
    branch_mate = seq.wait(branch_mate)
    branch_all = (branch_low, swap_core(branch_low), branch_mate, swap_core(branch_mate))

    all_acts, mlp_scattered = [], []
    mlp_full[0], chunk_left, chunk_right = seq.wait(mlp_full[0], chunk_left, chunk_right)
    mlp_full[1] = assemble(second_near, chunk_x, chunk_y, chunk_left, chunk_right)
    acts, grad_full = mlp_units(mlp_all, branch_all, mlp_full[0], True)
    all_acts.append(acts)
    grad_full = seq.mark(grad_full)
    mlp_scattered.append(scatter_grad(grad_full))
    mlp_full[2] = seq.wait(mlp_full[2])
    mlp_full[1] = seq.tie(mlp_full[1])
    acts, grad_full = mlp_units(mlp_all, branch_all, mlp_full[1], True)
    all_acts.append(acts)
    grad_full = seq.mark(grad_full)
    mlp_scattered.append(scatter_grad(grad_full))
    mlp_full[2] = seq.tie(mlp_full[2])
    (acts,) = mlp_units(mlp_all, branch_all, mlp_full[2], False)
    all_acts.append(acts)
    terms = [
        (a, kind, w, kind * units, units) for a, w in zip(all_acts, mlp_full) for kind in (0, 1)
    ]
    back_mine, back_mate = team_halves(project(terms))
    seq.mark(back_mate)
    back_mate = exchange(back_mate, PAIR)
    acts = seq.tie(acts)
    grad_full = seq.mark(weight_grad(parts, acts, (mlp_all, 2), (branch_all, 1)))
    mlp_scattered.append(scatter_grad(grad_full))
    terms = [(seq.tie(a), 2, w, 2 * units, units) for a, w in zip(all_acts, mlp_full)]
    sum_mine, sum_mate = team_halves(project(terms))
    sum_mate = seq.mark(sum_mate)
    back_mate = seq.wait(back_mate)
    mlp_back = back_mine + wide(back_mate)
    hidden_from, gain_mlp_part = mlp_norm_pull(mlp_back)
    hidden_grad_total = cot_float + hidden_from
    cot_low = seq.mark(low(hidden_grad_total))
    cot_mate = exchange(cot_low, PAIR)
    cot_core = swap_core(cot_low)
    sum_mate = exchange(seq.tie(sum_mate), PAIR)
    mlp_scattered[0] = seq.wait(mlp_scattered[0])
    lasts = [last_start(mlp_scattered[0])]
    mlp_scattered[1], cot_mate = seq.wait(mlp_scattered[1], cot_mate)
    lasts.append(last_start(mlp_scattered[1]))
    cot_all = (cot_low, cot_core, cot_mate, swap_core(cot_mate))
    out_grad = seq.mark(weight_grad(parts, context_low, (cot_all, 1)))
    out_steps = scatter_near(out_grad)
    qkv_grad, gain_parts = attend_back(
        cot_all, seq.tie(full_attn), qk_rot, value_low, qk_raw, row_marks, column_marks,
        gain_q, gain_k, cos, sin, q_heads, kv_heads,
    )
    qkv_grad = seq.mark(qkv_grad)
    mlp_scattered[2], *out_steps = seq.wait(mlp_scattered[2], *out_steps)
    out_steps = scatter_far(*out_steps)
    lasts.append(last_start(mlp_scattered[2]))
    token_mine, token_mate = team_halves(
        project([(seq.tie(qkv_grad), None, full_attn, 0, qkv_cols)])
    )
    token_mate = seq.mark(token_mate)
    token_mate = exchange(token_mate, PAIR)
    qkv_full = seq.mark(weight_grad(parts, seq.tie(qkv_grad), (normed_all, 1)))
    qkv_steps = scatter_near(qkv_full)
    count = len(out_steps)
    out_steps = seq.wait(*out_steps, *lasts[0])
    out_steps, lasts[0] = out_steps[:count], out_steps[count:]
    out_total = scatter_end(out_grad, *out_steps)
    qkv_steps = seq.wait(*qkv_steps)
    qkv_steps = scatter_far(*qkv_steps)
    token_mate = seq.wait(token_mate)
    attn_back = token_mine + wide(token_mate)
    token_from, gain_attn_part = attn_norm_pull(attn_back)
    gain_sums = total_sum(
        jnp.concatenate(
            [from_order(gain_attn_part), from_order(gain_mlp_part), gain_parts[0], gain_parts[1]]
        )
    )
    grad_tokens = seq.mark(from_order(hidden_grad_total + token_from))
    qkv_steps = seq.wait(*qkv_steps)
    attn_last = last_start(
        jnp.concatenate([scatter_end(qkv_full, *qkv_steps), out_total], axis=0)
    )
    lasts[1] = seq.wait(*lasts[1])
    mlp_sum = sum_mine + wide(seq.wait(sum_mate))
    out_tokens = from_order(low(hidden_in + live_mine * mlp_sum))
    lasts[2] = seq.wait(*lasts[2])
    teams = [last_end(last[0], last[1:]) for last in lasts]
    attn_team = last_end(attn_last[0], attn_last[1:])

    def pick(pair, start, stop):
        return in_turn(pair[0][start:stop], pair[1][start:stop], 0)

    grad_query = pick(attn_team, 0, q_cols).T
    grad_key = pick(attn_team, q_cols, q_cols + kv_cols).T
    grad_value = pick(attn_team, q_cols + kv_cols, qkv_cols).T
    grad_out = pick(attn_team, qkv_cols, qkv_cols + q_cols)

    def units_of(kind):
        cut = slice(kind * units, (kind + 1) * units)
        return in_turn(
            jnp.concatenate([keep[cut] for keep, _ in teams], axis=0),
            jnp.concatenate([other[cut] for _, other in teams], axis=0),
            0,
        )

    grad_gate = units_of(0).T
    grad_up = units_of(1).T
    grad_down = units_of(2)
    return (
        out_tokens,
        grad_tokens,
        grad_query,
        grad_key,
        grad_value,
        grad_out,
        grad_gate,
        grad_up,
        grad_down,
        gain_sums[:width],
        gain_sums[width : 2 * width],
        gain_sums[2 * width : 2 * width + head_width],
        gain_sums[2 * width + head_width :],
    )


def solution(mesh):
    weight_in = P("dp", "tensor")
    weight_out = P("tensor", "dp")
    rows = P(("dp", "tensor"), None)
    weights = (weight_in, weight_in, weight_in, weight_out, weight_in, weight_in, weight_out)
    gains = (P(), P(), P(), P())
    return jax.shard_map(
        per_device,
        mesh=mesh,
        in_specs=(rows, P("dp", None), *weights, *gains, rows),
        out_specs=(rows, rows, *weights, *gains),
        check_vma=False,
    )
```

time: 2730 us -> 858 us (0.31)
  waiting for transfers between devices: 2350 us -> 362 us
  Pallas kernels: 0 us -> 262 us
  matrix products: 233 us -> 0 us
  starting transfers between devices: 1.53 us -> 79.7 us
  blocking collectives: 43 us -> 0 us
  other arithmetic: 54.8 us -> 87 us
    reduce_scatter x11 -> x0, waiting for transfers between devices: 1570 us -> none  [the longest x1 370 us: per_device(): lax.psum_scatter(grad_up_full, 'dp', scatter_dimension=0, tiled=True)]
    all_gather x11 -> x2, waiting for transfers between devices: 773 us -> 0.01 us  [gather_weight(): return lax.all_gather(block, 'dp', axis_index_groups=xy_groups(), axis=0)]
    ppermute x0 -> x70, waiting for transfers between devices: none -> 362 us  [the longest x57 350 us: exchange(): return lax.ppermute(values, 'dp', [(i, i ^ mask) for i in range(size)])]
    pallas_call x0 -> x15, Pallas kernels: none -> 262 us  [the longest x3 76.5 us: mlp_units(): pl.pallas_call(functools.partial(mlp_kernel, pieces, tiles, with_grad), g...]
    dot_general x26 -> x0, matrix products: 221 us -> none  [the longest x7 70.7 us: mat_rows(): lax.dot_general(left, right, (((0,), (0,)), ((), ())), preferred_element_...]
    ppermute x0 -> x70, starting transfers between devices: none -> 78.7 us  [the longest x57 77.1 us: exchange(): return lax.ppermute(values, 'dp', [(i, i ^ mask) for i in range(size)])]
    psum x1 -> x0, blocking collectives: 43 us -> none  [per_device(): lax.psum((gain_attn_part, gain_mlp_part, gain_query_part, gain_key_part),...]
  transfers between devices with their start and end apart: 22 -> 75, of which waited for: 18 -> 35; matrix products, arithmetic and copies ran while one was open for 6% -> 13% of each run, Pallas kernels for 0% -> 29%
where the time goes in v1:
time: 858 us; the launch traced here: 850 us
  waiting for transfers between devices  362 us (42%)
  Pallas kernels  262 us (31%)
  other arithmetic  87 us (10%)
  starting transfers between devices  79.7 us (9%)
  local copies, waits for them, and re-layouts  43.2 us (5%)
  between operations  15.7 us (2%)
    ppermute x57, waiting for transfers between devices, exchange(): return lax.ppermute(values, 'dp', [(i, i ^ mask) for i in range(size)])  350 us
    ppermute x57, starting transfers between devices, exchange(): return lax.ppermute(values, 'dp', [(i, i ^ mask) for i in range(size)])  77.1 us
    pallas_call x3, Pallas kernels, mlp_units(): pl.pallas_call(functools.partial(mlp_kernel, pieces, tiles, with_grad), g...  76.5 us
    pallas_call x4, Pallas kernels, project(): pl.pallas_call(functools.partial(project_kernel, pieces, rows, parts), gr...  73.4 us
    pallas_call x3, Pallas kernels, weight_grad(): pl.pallas_call(functools.partial(weight_grad_kernel, pieces, tuple(cuts))...  35.9 us
    pallas_call x1, Pallas kernels, attend_back(): pl.pallas_call(functools.partial(attend_back_kernel, pieces_of(parts, wid...  34.6 us
    convert_element_type x13, other arithmetic, low(): return values.astype(jnp.bfloat16)  24 us
    unnamed x223, local copies, waits for them, and re-layouts  21 us
  transfers between devices with their start and end apart: 75, of which 35 were waited for; matrix products, arithmetic and copies ran while one was open for 13% of the time, Pallas kernels for 29%

profile of v1, /device:TPU:0, one launch (start us, length us, event | category | flops | bytes accessed | tf_op | source)
XLA Modules:
  0.0 849.6 jit_solution(10436737612663879156)
XLA Ops:
  61.9 23.8 %collective-permute-done.8 = bf16[1536,128]{1,0:T(8,128)(2,1)S(1)} collective-permute-done((bf16[1536,128]{1,0:T(8,128)(2,1)S(1)}, bf16[1536,128]{1,0:T(8,128)(2,1)S(1)}, u32[]{:S(2)}, u32[]{:S(2)}) %collective-permute-start.8) | collective-permute-done | bytes 393248 | tf_op jit(solution)/shard_map/ppermute | solution.py:66
  104.2 31.8 %collective-permute-done.14 = bf16[1536,128]{1,0:T(8,128)(2,1)S(1)} collective-permute-done((bf16[1536,128]{1,0:T(8,128)(2,1)}, bf16[1536,128]{1,0:T(8,128)(2,1)S(1)}, u32[]{:S(2)}, u32[]{:S(2)}) %collective-permute-start.14) | collective-permute-done | bytes 393248 | tf_op jit(solution)/shard_map/ppermute | solution.py:66
  160.7 13.3 %shard_map.238 = (f32[1280,768]{1,0:T(8,128)}, bf16[1280,768]{1,0:T(8,128)(2,1)}, bf16[1280,256]{1,0:T(8,128)(2,1)}) custom-call(bf16[320,2048]{1,0:T(8,128)(2,1)} %copy-done.3, bf16[320,2048]{1,0:T(8,128)(2,1)} %collective-permute-done.refs_1_, bf16[320,2048]{1,0:T(8,128)(2,1)} %copy-done.11, bf16[320,2048]{1,0:T(8,128)(2,1)} %collective-permute-done.16.refs_3_, ...), custom_call_target="tpu_custom_call" | custom-call | flops 1000 | bytes 1000 | tf_op jit(solution)/shard_map/pallas_call | solution.py:425
  174.0 14.1 %shard_map.239.refs_0_.left_ref = bf16[1280,512]{1,0:T(8,128)(2,1)} custom-call(bf16[1280,768]{1,0:T(8,128)(2,1)} %get-tuple-element.120.q_ref.k_ref, bf16[1280,768]{1,0:T(8,128)(2,1)} %get-tuple-element.120.q_ref.k_ref, bf16[1280,256]{1,0:T(8,128)(2,1)} %get-tuple-element.122.v_ref, s32[2,640,8]{2,1,0:T(8,128)} %stack.55.row_ref, ...), custom_call_target="tpu_custom_call" | custom-call | flops 1000 | bytes 1000 | tf_op jit(solution)/shard_map/pallas_call | solution.py:488
  188.1 11.6 %shard_map.240 = (f32[2,320,2048]{2,1,0:T(8,128)}, bf16[2,320,2048]{2,1,0:T(8,128)(2,1)}) custom-call(bf16[1280,512]{1,0:T(8,128)(2,1)} %shard_map.239.refs_0_.left_ref, bf16[4,1536,512]{2,1,0:T(8,128)(2,1)} %shard_map.237.refs_4_.refs_1_.weight_ref), custom_call_target="tpu_custom_call" | custom-call | flops 1000 | bytes 1000 | tf_op jit(solution)/shard_map/pallas_call | solution.py:314
  208.5 23.8 %collective-permute-done.22 = bf16[1536,128]{1,0:T(8,128)(2,1)S(1)} collective-permute-done((bf16[1536,128]{1,0:T(8,128)(2,1)S(1)}, bf16[1536,128]{1,0:T(8,128)(2,1)S(1)}, u32[]{:S(2)}, u32[]{:S(2)}) %collective-permute-start.22) | collective-permute-done | bytes 393248 | tf_op jit(solution)/shard_map/ppermute | solution.py:66
  245.8 26.8 %collective-permute-done.18 = bf16[320,2048]{1,0:T(8,128)(2,1)S(1)} collective-permute-done((bf16[320,2048]{1,0:T(8,128)(2,1)}, bf16[320,2048]{1,0:T(8,128)(2,1)S(1)}, u32[]{:S(2)}, u32[]{:S(2)}) %collective-permute-start.18) | collective-permute-done | bytes 1310752 | tf_op jit(solution)/shard_map/ppermute | solution.py:66
  280.8 28.2 %collective-permute-done.25.refs_2_ = bf16[320,2048]{1,0:T(8,128)(2,1)} collective-permute-done((bf16[320,2048]{1,0:T(8,128)(2,1)}, bf16[320,2048]{1,0:T(8,128)(2,1)}, u32[]{:S(2)}, u32[]{:S(2)}) %collective-permute-start.25) | collective-permute-done | bytes 1310752 | tf_op jit(solution)/shard_map/ppermute | solution.py:66
  309.0 25.6 %collective-permute-done.28.refs_6_ = bf16[320,2048]{1,0:T(8,128)(2,1)} collective-permute-done((bf16[320,2048]{1,0:T(8,128)(2,1)}, bf16[320,2048]{1,0:T(8,128)(2,1)}, u32[]{:S(2)}, u32[]{:S(2)}) %collective-permute-start.28) | collective-permute-done | bytes 1310752 | tf_op jit(solution)/shard_map/ppermute | solution.py:66
  336.3 18.4 %collective-permute-done.31.right_ref = bf16[1536,256]{1,0:T(8,128)(2,1)} collective-permute-done((bf16[1536,256]{1,0:T(8,128)(2,1)S(1)}, bf16[1536,256]{1,0:T(8,128)(2,1)}, u32[]{:S(2)}, u32[]{:S(2)}) %collective-permute-start.31) | collective-permute-done | bytes 786464 | tf_op jit(solution)/shard_map/ppermute | solution.py:66
  354.8 28.5 %shard_map.241 = (bf16[3,1280,512]{2,1,0:T(8,128)(2,1)}, bf16[4,1536,512]{2,1,0:T(8,128)(2,1)}) custom-call(bf16[320,2048]{1,0:T(8,128)(2,1)} %multiply_convert_fusion.refs_0_, bf16[320,2048]{1,0:T(8,128)(2,1)} %collective-permute-done.24.refs_1_, bf16[320,2048]{1,0:T(8,128)(2,1)} %collective-permute-done.25.refs_2_, ...), custom_call_target="tpu_custom_call" | custom-call | flops 1000 | bytes 1000 | tf_op jit(solution)/shard_map/pallas_call | solution.py:249
  390.5 29.5 %shard_map.243 = (bf16[3,1280,512]{2,1,0:T(8,128)(2,1)}, bf16[4,1536,512]{2,1,0:T(8,128)(2,1)}) custom-call(bf16[320,2048]{1,0:T(8,128)(2,1)} %multiply_convert_fusion.refs_0_, bf16[320,2048]{1,0:T(8,128)(2,1)} %collective-permute-done.24.refs_1_, bf16[320,2048]{1,0:T(8,128)(2,1)} %collective-permute-done.25.refs_2_, ...), custom_call_target="tpu_custom_call" | custom-call | flops 1000 | bytes 1000 | tf_op jit(solution)/shard_map/pallas_call | solution.py:249
  420.2 18.4 %shard_map.244.refs_4_.refs_5_.left_ref.refs_2_ = bf16[3,1280,512]{2,1,0:T(8,128)(2,1)} custom-call(bf16[320,2048]{1,0:T(8,128)(2,1)} %multiply_convert_fusion.refs_0_, bf16[320,2048]{1,0:T(8,128)(2,1)} %collective-permute-done.24.refs_1_, bf16[320,2048]{1,0:T(8,128)(2,1)} %collective-permute-done.25.refs_2_, ...), custom_call_target="tpu_custom_call" | custom-call | flops 1000 | bytes 1000 | tf_op jit(solution)/shard_map/pallas_call | solution.py:249
  438.6 28.7 %shard_map.245 = (f32[2,320,2048]{2,1,0:T(8,128)}, bf16[2,320,2048]{2,1,0:T(8,128)(2,1)}) custom-call(bf16[3,1280,512]{2,1,0:T(8,128)(2,1)} %get-tuple-element.150.refs_0_.refs_1_, bf16[3,1280,512]{2,1,0:T(8,128)(2,1)} %get-tuple-element.150.refs_0_.refs_1_, bf16[3,1280,512]{2,1,0:T(8,128)(2,1)} %get-tuple-element.151.refs_2_.refs_3_.refs_1_, ...), custom_call_target="tpu_custom_call" | custom-call | flops 1000 | bytes 1000 | tf_op jit(solution)/shard_map/pallas_call | solution.py:314
  477.2 16.6 %shard_map.246 = bf16[4,1536,512]{2,1,0:T(8,128)(2,1)} custom-call(bf16[3,1280,512]{2,1,0:T(8,128)(2,1)} %shard_map.244.refs_4_.refs_5_.left_ref.refs_2_, bf16[320,2048]{1,0:T(8,128)(2,1)} %multiply_convert_fusion.refs_0_, bf16[320,2048]{1,0:T(8,128)(2,1)} %collective-permute-done.24.refs_1_, bf16[320,2048]{1,0:T(8,128)(2,1)} %collective-permute-done.25.refs_2_, ...), custom_call_target="tpu_custom_call" | custom-call | flops 1000 | bytes 1000 | tf_op jit(solution)/shard_map/pallas_call | solution.py:363
  493.8 18.3 %shard_map.247 = (f32[2,320,2048]{2,1,0:T(8,128)}, bf16[2,320,2048]{2,1,0:T(8,128)(2,1)}) custom-call(bf16[3,1280,512]{2,1,0:T(8,128)(2,1)} %get-tuple-element.150.refs_0_.refs_1_, bf16[3,1280,512]{2,1,0:T(8,128)(2,1)} %get-tuple-element.151.refs_2_.refs_3_.refs_1_, bf16[3,1280,512]{2,1,0:T(8,128)(2,1)} %shard_map.244.refs_4_.refs_5_.left_ref.refs_2_, ...), custom_call_target="tpu_custom_call" | custom-call | flops 1000 | bytes 1000 | tf_op jit(solution)/shard_map/pallas_call | solution.py:314
  521.5 21.9 %collective-permute-done.34 = bf16[320,2048]{1,0:T(8,128)(2,1)S(1)} collective-permute-done((bf16[320,2048]{1,0:T(8,128)(2,1)S(1)}, bf16[320,2048]{1,0:T(8,128)(2,1)S(1)}, u32[]{:S(2)}, u32[]{:S(2)}) %collective-permute-start.34) | collective-permute-done | bytes 1310752 | tf_op jit(solution)/shard_map/ppermute | solution.py:66
  551.0 29.3 %collective-permute-done.36.refs_2_.cot_c = bf16[320,2048]{1,0:T(8,128)(2,1)} collective-permute-done((bf16[320,2048]{1,0:T(8,128)(2,1)}, bf16[320,2048]{1,0:T(8,128)(2,1)}, u32[]{:S(2)}, u32[]{:S(2)}) %collective-permute-start.36) | collective-permute-done | bytes 1310752 | tf_op jit(solution)/shard_map/ppermute | solution.py:66
  597.9 34.6 %shard_map.249 = (bf16[1280,1024]{1,0:T(8,128)(2,1)}, f32[8,128]{1,0:T(8,128)}) custom-call(bf16[320,2048]{1,0:T(8,128)(2,1)} %get-tuple-element.274.refs_0_.cot_a, bf16[320,2048]{1,0:T(8,128)(2,1)} %collective-permute-done.40.refs_1_.cot_b, bf16[320,2048]{1,0:T(8,128)(2,1)} %collective-permute-done.36.refs_2_.cot_c, ...), custom_call_target="tpu_custom_call" | custom-call | flops 1000 | bytes 1000 | tf_op jit(solution)/shard_map/pallas_call | solution.py:596
  632.6 14.8 %shard_map.250 = (f32[2,320,2048]{2,1,0:T(8,128)}, bf16[2,320,2048]{2,1,0:T(8,128)(2,1)}) custom-call(bf16[1280,1024]{1,0:T(8,128)(2,1)} %get-tuple-element.173.refs_0_.left_ref, bf16[4,1536,512]{2,1,0:T(8,128)(2,1)} %shard_map.237.refs_4_.refs_1_.weight_ref), custom_call_target="tpu_custom_call" | custom-call | flops 1000 | bytes 1000 | tf_op jit(solution)/shard_map/pallas_call | solution.py:314
  671.1 11.4 %shard_map.251 = bf16[4,1024,512]{2,1,0:T(8,128)(2,1)} custom-call(bf16[1280,1024]{1,0:T(8,128)(2,1)} %get-tuple-element.173.refs_0_.left_ref, bf16[320,2048]{1,0:T(8,128)(2,1)} %copy-done.3, bf16[320,2048]{1,0:T(8,128)(2,1)} %collective-permute-done.refs_1_, bf16[320,2048]{1,0:T(8,128)(2,1)} %copy-done.11, bf16[320,2048]{1,0:T(8,128)(2,1)} %collective-permute-done.16.refs_3_), custom_call_target="tpu_custom_call" | custom-call | flops 1000 | bytes 1000 | tf_op jit(solution)/shard_map/pallas_call | solution.py:363
  762.0 18.1 %collective-permute-done.37 = bf16[1536,128]{1,0:T(8,128)(2,1)S(1)} collective-permute-done((bf16[1536,128]{1,0:T(8,128)(2,1)S(1)}, bf16[1536,128]{1,0:T(8,128)(2,1)S(1)}, u32[]{:S(2)}, u32[]{:S(2)}) %collective-permute-start.37) | collective-permute-done | bytes 393248 | tf_op jit(solution)/shard_map/ppermute | solution.py:66
  781.7 10.6 %collective-permute-done.63 = bf16[1536,128]{1,0:T(8,128)(2,1)S(1)} collective-permute-done((bf16[1536,128]{1,0:T(8,128)(2,1)S(1)}, bf16[1536,128]{1,0:T(8,128)(2,1)S(1)}, u32[]{:S(2)}, u32[]{:S(2)}) %collective-permute-start.63) | collective-permute-done | bytes 393248 | tf_op jit(solution)/shard_map/ppermute | solution.py:66
  811.4 16.1 %collective-permute-done.68 = f32[4352]{0:T(1024)S(1)} collective-permute-done((f32[4352]{0:T(1024)S(1)}, f32[4352]{0:T(1024)S(1)}, u32[]{:S(2)}, u32[]{:S(2)}) %collective-permute-start.68) | collective-permute-done | bytes 17440 | tf_op jit(solution)/shard_map/ppermute | solution.py:66
  (502 shorter events, 319.8 us)
Async XLA Ops:
  7.2 347.5 %all-gather.3.cloned.1.call-start = ((), (), s32[]{:S(2)}) async-start(), calls=%async_computation.3 | async-start | bytes 7864320 | tf_op jit(solution)/shard_map/all_gather | solution.py:687
  10.5 41.4 %collective-permute-start.3 = (bf16[1536,128]{1,0:T(8,128)(2,1)}, bf16[1536,128]{1,0:T(8,128)(2,1)}, u32[]{:S(2)}, u32[]{:S(2)}) collective-permute-start(bf16[1536,128]{1,0:T(8,128)(2,1)} %pad_maximum_fusion.4), channel_id=1, source_target_pairs={{0,24},{2,26},{4,28},{6,30},{8,16},{10,18},{12,20},{14,22},{16,8},... | collective-permute-start | bytes 1179656 | tf_op jit(solution)/shard_map/ppermute | solution.py:66
  94.2 296.3 %all-gather.5.cloned.1.call-start = ((), (), s32[]{:S(2)}) async-start(), calls=%async_computation.4 | async-start | bytes 7864320 | tf_op jit(solution)/shard_map/all_gather | solution.py:687
  94.5 58.1 %collective-permute-start.12 = (bf16[320,2048]{1,0:T(8,128)(2,1)S(1)}, bf16[320,2048]{1,0:T(8,128)(2,1)S(1)}, u32[]{:S(2)}, u32[]{:S(2)}) collective-permute-start(bf16[320,2048]{1,0:T(8,128)(2,1)S(1)} %fusion.2.refs_0_), channel_id=1, source_target_pairs={{0,8},{2,10},{4,12},{6,14},{8,0},{10,2},{12,4},{14,6},{16,24},{18,... | collective-permute-start | bytes 3932168 | tf_op jit(solution)/shard_map/ppermute | solution.py:66
  101.8 50.8 %collective-permute-start.11 = (bf16[1536,256]{1,0:T(8,128)(2,1)S(1)}, bf16[1536,256]{1,0:T(8,128)(2,1)S(1)}, u32[]{:S(2)}, u32[]{:S(2)}) collective-permute-start(bf16[1536,256]{1,0:T(8,128)(2,1)S(1)} %slice.345), channel_id=1, source_target_pairs={{0,4},{2,6},{4,0},{6,2},{8,12},{10,14},{12,8},{14,10},{16,20},{18,... | collective-permute-start | bytes 2359304 | tf_op jit(solution)/shard_map/ppermute | solution.py:66
  102.2 50.3 %collective-permute-start.10 = (bf16[1536,256]{1,0:T(8,128)(2,1)S(1)}, bf16[1536,256]{1,0:T(8,128)(2,1)}, u32[]{:S(2)}, u32[]{:S(2)}) collective-permute-start(bf16[1536,256]{1,0:T(8,128)(2,1)S(1)} %slice.344), channel_id=1, source_target_pairs={{0,2},{2,0},{4,6},{6,4},{8,10},{10,8},{12,14},{14,12},{16,18},{18,... | collective-permute-start | bytes 2359304 | tf_op jit(solution)/shard_map/ppermute | solution.py:66
  102.8 44.4 %collective-permute-start.15 = (bf16[1536,128]{1,0:T(8,128)(2,1)S(1)}, bf16[1536,128]{1,0:T(8,128)(2,1)S(1)}, u32[]{:S(2)}, u32[]{:S(2)}) collective-permute-start(bf16[1536,128]{1,0:T(8,128)(2,1)S(1)} %copy-done.67), channel_id=1, source_target_pairs={{0,24},{2,26},{4,28},{6,30},{8,16},{10,18},{12,20},{14,22},{16,8},... | collective-permute-start | bytes 1179656 | tf_op jit(solution)/shard_map/ppermute | solution.py:66
  241.6 309.4 %reduce-scatter.12.cloned.1.call-start = ((), (), s32[]{:S(2)}) async-start(), calls=%async_computation.6 | async-start | bytes 7864320
  278.7 55.9 %collective-permute-start.28 = (bf16[320,2048]{1,0:T(8,128)(2,1)}, bf16[320,2048]{1,0:T(8,128)(2,1)}, u32[]{:S(2)}, u32[]{:S(2)}) collective-permute-start(bf16[320,2048]{1,0:T(8,128)(2,1)} %fusion.4.refs_4_), channel_id=1, source_target_pairs={{0,8},{2,10},{4,12},{6,14},{8,0},{10,2},{12,4},{14,6},{16,24},{18,... | collective-permute-start | bytes 3932168 | tf_op jit(solution)/shard_map/ppermute | solution.py:66
  279.0 56.1 %collective-permute-start.30 = (bf16[1536,256]{1,0:T(8,128)(2,1)S(1)}, bf16[1536,256]{1,0:T(8,128)(2,1)S(1)}, u32[]{:S(2)}, u32[]{:S(2)}) collective-permute-start(bf16[1536,256]{1,0:T(8,128)(2,1)S(1)} %slice.351), channel_id=1, source_target_pairs={{0,2},{2,0},{4,6},{6,4},{8,10},{10,8},{12,14},{14,12},{16,18},{18,... | collective-permute-start | bytes 2359304 | tf_op jit(solution)/shard_map/ppermute | solution.py:66
  280.3 74.5 %collective-permute-start.27 = (bf16[320,2048]{1,0:T(8,128)(2,1)}, bf16[320,2048]{1,0:T(8,128)(2,1)}, u32[]{:S(2)}, u32[]{:S(2)}) collective-permute-start(bf16[320,2048]{1,0:T(8,128)(2,1)} %fusion.4.refs_4_), channel_id=1, source_target_pairs={{0,1},{1,0},{2,3},{3,2},{4,5},{5,4},{6,7},{7,6},{8,9},{9,8},{10,11... | collective-permute-start | bytes 3932168 | tf_op jit(solution)/shard_map/ppermute | solution.py:655
  280.3 74.5 %collective-permute-start.24 = (bf16[320,2048]{1,0:T(8,128)(2,1)}, bf16[320,2048]{1,0:T(8,128)(2,1)}, u32[]{:S(2)}, u32[]{:S(2)}) collective-permute-start(bf16[320,2048]{1,0:T(8,128)(2,1)} %multiply_convert_fusion.refs_0_), channel_id=1, source_target_pairs={{0,1},{1,0},{2,3},{3,2},{4,5},{5,4},{6,7},{7,6},{8,9},{9,8},{10,11... | collective-permute-start | bytes 3932168 | tf_op jit(solution)/shard_map/ppermute | solution.py:655
  383.4 197.0 %reduce-scatter.10.cloned.1.call-start = ((), (), s32[]{:S(2)}) async-start(), calls=%async_computation.5 | async-start | bytes 7864320
  420.0 212.6 %reduce-scatter.14.cloned.1.call-start = ((), (), s32[]{:S(2)}) async-start(), calls=%async_computation.7 | async-start | bytes 7864320
  593.9 38.7 %collective-permute-start.45 = (bf16[256,512]{1,0:T(8,128)(2,1)S(1)}, bf16[256,512]{1,0:T(8,128)(2,1)}, u32[]{:S(2)}, u32[]{:S(2)}) collective-permute-start(bf16[256,512]{1,0:T(8,128)(2,1)S(1)} %get-tuple-element.290), channel_id=1, source_target_pairs={{0,4},{2,6},{4,0},{6,2},{8,12},{10,14},{12,8},{14,10},{16,20},{18,... | collective-permute-start | bytes 786440 | tf_op jit(solution)/shard_map/ppermute | solution.py:66
  706.1 75.1 %collective-permute-start.35 = (bf16[320,2048]{1,0:T(8,128)(2,1)S(1)}, bf16[320,2048]{1,0:T(8,128)(2,1)S(1)}, u32[]{:S(2)}, u32[]{:S(2)}) collective-permute-start(bf16[320,2048]{1,0:T(8,128)(2,1)S(1)} %copy-done.28), channel_id=1, source_target_pairs={{0,8},{2,10},{4,12},{6,14},{8,0},{10,2},{12,4},{14,6},{16,24},{18,... | collective-permute-start | bytes 3932168 | tf_op jit(solution)/shard_map/ppermute | solution.py:66
  707.4 45.5 %collective-permute-start.39 = (bf16[1536,128]{1,0:T(8,128)(2,1)S(1)}, bf16[1536,128]{1,0:T(8,128)(2,1)S(1)}, u32[]{:S(2)}, u32[]{:S(2)}) collective-permute-start(bf16[1536,128]{1,0:T(8,128)(2,1)S(1)} %copy-done.64), channel_id=1, source_target_pairs={{0,24},{2,26},{4,28},{6,30},{8,16},{10,18},{12,20},{14,22},{16,8},... | collective-permute-start | bytes 1179656 | tf_op jit(solution)/shard_map/ppermute | solution.py:66
  717.2 41.2 %collective-permute-start.38 = (bf16[1536,128]{1,0:T(8,128)(2,1)S(1)}, bf16[1536,128]{1,0:T(8,128)(2,1)}, u32[]{:S(2)}, u32[]{:S(2)}) collective-permute-start(bf16[1536,128]{1,0:T(8,128)(2,1)S(1)} %copy-done.63), channel_id=1, source_target_pairs={{0,16},{2,18},{4,20},{6,22},{8,24},{10,26},{12,28},{14,30},{16,0},... | collective-permute-start | bytes 1179656 | tf_op jit(solution)/shard_map/ppermute | solution.py:66
  717.2 62.8 %collective-permute-start.37 = (bf16[1536,128]{1,0:T(8,128)(2,1)S(1)}, bf16[1536,128]{1,0:T(8,128)(2,1)S(1)}, u32[]{:S(2)}, u32[]{:S(2)}) collective-permute-start(bf16[1536,128]{1,0:T(8,128)(2,1)S(1)} %copy-done.62), channel_id=1, source_target_pairs={{0,8},{2,10},{4,12},{6,14},{8,0},{10,2},{12,4},{14,6},{16,24},{18,... | collective-permute-start | bytes 1179656 | tf_op jit(solution)/shard_map/ppermute | solution.py:66
  743.1 38.6 %collective-permute-start.64 = (bf16[1536,128]{1,0:T(8,128)(2,1)S(1)}, bf16[1536,128]{1,0:T(8,128)(2,1)S(1)}, u32[]{:S(2)}, u32[]{:S(2)}) collective-permute-start(bf16[1536,128]{1,0:T(8,128)(2,1)S(1)} %copy-done.61), channel_id=1, source_target_pairs={{0,24},{2,26},{4,28},{6,30},{8,16},{10,18},{12,20},{14,22},{16,8},... | collective-permute-start | bytes 1179656 | tf_op jit(solution)/shard_map/ppermute | solution.py:66
  752.9 39.3 %collective-permute-start.63 = (bf16[1536,128]{1,0:T(8,128)(2,1)S(1)}, bf16[1536,128]{1,0:T(8,128)(2,1)S(1)}, u32[]{:S(2)}, u32[]{:S(2)}) collective-permute-start(bf16[1536,128]{1,0:T(8,128)(2,1)S(1)} %copy-done.60), channel_id=1, source_target_pairs={{0,16},{2,18},{4,20},{6,22},{8,24},{10,26},{12,28},{14,30},{16,0},... | collective-permute-start | bytes 1179656 | tf_op jit(solution)/shard_map/ppermute | solution.py:66
  796.9 39.5 %collective-permute-start.59 = (bf16[1536,128]{1,0:T(8,128)(2,1)}, bf16[1536,128]{1,0:T(8,128)(2,1)}, u32[]{:S(2)}, u32[]{:S(2)}) collective-permute-start(bf16[1536,128]{1,0:T(8,128)(2,1)} %get-tuple-element.284), channel_id=1, source_target_pairs={{0,16},{2,18},{4,20},{6,22},{8,24},{10,26},{12,28},{14,30},{16,0},... | collective-permute-start | bytes 1179656 | tf_op jit(solution)/shard_map/ppermute | solution.py:66
  797.6 40.2 %collective-permute-start.61 = (bf16[1536,128]{1,0:T(8,128)(2,1)S(1)}, bf16[1536,128]{1,0:T(8,128)(2,1)}, u32[]{:S(2)}, u32[]{:S(2)}) collective-permute-start(bf16[1536,128]{1,0:T(8,128)(2,1)S(1)} %get-tuple-element.285), channel_id=1, source_target_pairs={{0,24},{2,26},{4,28},{6,30},{8,16},{10,18},{12,20},{14,22},{16,8},... | collective-permute-start | bytes 1179656 | tf_op jit(solution)/shard_map/ppermute | solution.py:66
  799.5 38.2 %collective-permute-start.60 = (bf16[1536,128]{1,0:T(8,128)(2,1)S(1)}, bf16[1536,128]{1,0:T(8,128)(2,1)}, u32[]{:S(2)}, u32[]{:S(2)}) collective-permute-start(bf16[1536,128]{1,0:T(8,128)(2,1)S(1)} %get-tuple-element.286), channel_id=1, source_target_pairs={{0,8},{2,10},{4,12},{6,14},{8,0},{10,2},{12,4},{14,6},{16,24},{18,... | collective-permute-start | bytes 1179656 | tf_op jit(solution)/shard_map/ppermute | solution.py:66
  (147 other events, 2464.4 us)
Sparse Core Ops, SparseCore 0:
  94.3 83.7 all-gather.2
  241.7 87.5 all-gather.4
  383.5 71.9 reduce-scatter.11
  458.3 70.2 reduce-scatter.9
  531.4 73.0 reduce-scatter.13

commit v2 on v1

--- a/solution.py
+++ b/solution.py
@@ -92,6 +92,10 @@
 
 def small_cost():
     return pl.CostEstimate(flops=1000, bytes_accessed=1000, transcendentals=0)
+
+
+def large_cost():
+    return pl.CostEstimate(flops=400_000_000_000, bytes_accessed=1000, transcendentals=0)
 
 
 def unit_tile(units):
@@ -141,38 +145,51 @@
     return jnp.concatenate([ref[p][:, at : at + size] for p, at, _, size in pieces], axis=1)
 
 
+def copies_of(parts, scratch, sems):
+    copies, first = [], 0
+    for i, part in enumerate(parts):
+        rows = part.shape[0]
+        copies.append(
+            pltpu.make_async_copy(part, scratch.at[pl.ds(first, rows), :], sems.at[i])
+        )
+        first += rows
+    return copies
+
+
 def fetch(parts, scratch, sems):
-    rows = parts[0].shape[0]
-    copies = [
-        pltpu.make_async_copy(part, scratch.at[pl.ds(i * rows, rows), :], sems.at[i])
-        for i, part in enumerate(parts)
-    ]
+    copies = copies_of(parts, scratch, sems)
     for copy in copies:
         copy.start()
     return copies
 
 
-def hidden_tile(pieces, row_tile, mlp_all, branch_all, gate_ref, up_ref, down_ref, store):
-    gate_w, up_w, down_w = (side_by_side(pieces, r) for r in (gate_ref, up_ref, down_ref))
-
-    def step(index, carry):
-        rows = pl.ds(pl.multiple_of(index * row_tile, row_tile), row_tile)
-        mlp_rows = mlp_all[rows, :]
-        gate_proj = mat_cols(mlp_rows, gate_w)
-        up_proj = mat_cols(mlp_rows, up_w)
-        hidden_grad = mat_cols(branch_all[rows, :], down_w)
-        sigmoid_gate = 1.0 / (1.0 + jnp.exp(-gate_proj))
-        silu_gate = gate_proj * sigmoid_gate
-        store(
-            0,
-            rows,
-            low(hidden_grad * up_proj * sigmoid_gate * (1.0 + gate_proj * (1.0 - sigmoid_gate))),
-        )
-        store(1, rows, low(hidden_grad * silu_gate))
-        store(2, rows, low(silu_gate * up_proj))
-        return carry
-
-    lax.fori_loop(0, mlp_all.shape[0] // row_tile, step, 0)
+def pieces_in(parts, start, stop):
+    found, first = [], 0
+    for i, part in enumerate(parts):
+        if start <= first < stop:
+            found.append(i)
+        first += part.shape[0]
+    return found
+
+
+def rows_in(parts):
+    return sum(part.shape[0] for part in parts)
+
+
+def hidden_rows(rows, mlp_all, branch_all, gate_w, up_w, down_w, store):
+    mlp_rows = mlp_all[rows, :]
+    gate_proj = mat_cols(mlp_rows, gate_w)
+    up_proj = mat_cols(mlp_rows, up_w)
+    hidden_grad = mat_cols(branch_all[rows, :], down_w)
+    sigmoid_gate = 1.0 / (1.0 + jnp.exp(-gate_proj))
+    silu_gate = gate_proj * sigmoid_gate
+    store(
+        0,
+        rows,
+        low(hidden_grad * up_proj * sigmoid_gate * (1.0 + gate_proj * (1.0 - sigmoid_gate))),
+    )
+    store(1, rows, low(hidden_grad * silu_gate))
+    store(2, rows, low(silu_gate * up_proj))
 
 
 def store_grad(pieces, out_ref, grad):
@@ -180,36 +197,44 @@
         out_ref[p, :, at : at + size] = grad[:, first : first + size]
 
 
-def mlp_kernel(pieces, tiles, with_grad, *refs):
-    mlp_parts, branch_parts = refs[:4], refs[4:8]
-    weights = refs[8:11]
+def mlp_kernel(pieces, tiles, with_grad, counts, *refs):
+    count = sum(counts)
+    mlp_parts, branch_parts = refs[: counts[0]], refs[counts[0] : count]
+    weights = refs[count : count + 3]
     if with_grad:
-        acts_ref, grad_ref, mlp_all, branch_all, acts_all, sems = refs[11:]
+        acts_ref, grad_ref, mlp_all, branch_all, acts_all, sems = refs[count + 3 :]
     else:
-        acts_ref, mlp_all, branch_all, sems = refs[11:]
+        acts_ref, mlp_all, branch_all, sems = refs[count + 3 :]
     step = pl.program_id(0)
-    rows = mlp_parts[0].shape[0]
-    tile = weights[0].shape[1]
+    total = mlp_all.shape[0]
+    rows = total // 4
+
+    def store(kind, where, values):
+        acts_ref[kind, where, :] = values
+        if with_grad:
+            acts_all[step, kind, where, :] = values
+
+    def sides():
+        return [side_by_side(pieces, w) for w in weights]
 
     @pl.when(step == 0)
     def _():
-        copies = fetch(mlp_parts, mlp_all, sems.at[0]) + fetch(branch_parts, branch_all, sems.at[1])
-        for copy in copies:
-            copy.wait()
-
-    def forward():
-        def store(kind, where, values):
-            acts_ref[kind, where, :] = values
-            if with_grad:
-                acts_all[step, kind, where, :] = values
-
-        hidden_tile(pieces, rows, mlp_all, branch_all, *weights, store)
+        mlp_copies = fetch(mlp_parts, mlp_all, sems.at[0])
+        branch_copies = fetch(branch_parts, branch_all, sems.at[1])
+        sides_now = sides()
+        for first in range(0, total, rows):
+            for i in pieces_in(mlp_parts, first, first + rows):
+                mlp_copies[i].wait()
+            for i in pieces_in(branch_parts, first, first + rows):
+                branch_copies[i].wait()
+            hidden_rows(slice(first, first + rows), mlp_all, branch_all, *sides_now, store)
+
+    @pl.when((step > 0) & (step < tiles))
+    def _():
+        hidden_rows(slice(0, total), mlp_all, branch_all, *sides(), store)
 
     if not with_grad:
-        forward()
         return
-
-    pl.when(step < tiles)(forward)
 
     @pl.when((step >= tiles) & (step < 3 * tiles))
     def _():
@@ -224,8 +249,8 @@
 
 
 def mlp_units(mlp_parts, branch_parts, weight, with_grad):
-    part_rows, width = mlp_parts[0].shape
-    rows = 4 * part_rows
+    rows, width = rows_in(mlp_parts), mlp_parts[0].shape[1]
+    counts = (len(mlp_parts), len(branch_parts))
     parts, units3, part_width = weight.shape
     units = units3 // 3
     tile = unit_tile(units)
@@ -247,12 +272,12 @@
         )
         scratch.append(pltpu.VMEM((tiles, 3, rows, tile), jnp.bfloat16))
     return pl.pallas_call(
-        functools.partial(mlp_kernel, pieces, tiles, with_grad),
+        functools.partial(mlp_kernel, pieces, tiles, with_grad, counts),
         grid=(4 * tiles if with_grad else tiles,),
         out_shape=out_shape,
-        in_specs=[anywhere()] * 8 + [weight_spec(k) for k in range(3)],
+        in_specs=[anywhere()] * sum(counts) + [weight_spec(k) for k in range(3)],
         out_specs=out_specs,
-        scratch_shapes=scratch + [pltpu.SemaphoreType.DMA((2, 4))],
+        scratch_shapes=scratch + [pltpu.SemaphoreType.DMA((2, max(counts)))],
         compiler_params=params(),
         cost_estimate=small_cost(),
     )(*mlp_parts, *branch_parts, weight, weight, weight)
@@ -264,32 +289,20 @@
     lefts, rights = refs[:count], refs[count : 2 * count]
     part = pl.program_id(0)
 
-    def step(index, carry):
-        rows = pl.ds(pl.multiple_of(index * row_tile, row_tile), row_tile)
-        total = None
-        for left, right in zip(lefts, rights):
-            left_rows = left[rows, :] if len(left.shape) == 2 else left[0, rows, :]
-            term = matmul(left_rows, right[0])
-            total = term if total is None else total + term
-
-        def store(out_ref):
-            size = pieces[0][3]
-            if size == total.shape[1]:
-                out_ref[index // 2, :, pl.ds(pl.multiple_of(part * size, size), size)] = (
-                    total.astype(out_ref.dtype)
-                )
-            else:
-                for k in range(total.shape[1] // size):
-                    first = pl.multiple_of((k * parts + part) * size, size)
-                    out_ref[index // 2, :, pl.ds(first, size)] = total[
-                        :, k * size : (k + 1) * size
-                    ].astype(out_ref.dtype)
-
-        pl.when(index % 2 == 0)(lambda: store(keep_ref))
-        pl.when(index % 2 == 1)(lambda: store(send_ref))
-        return carry
-
-    lax.fori_loop(0, 4, step, 0)
+    total = None
+    for left, right in zip(lefts, rights):
+        left_rows = left[...] if len(left.shape) == 2 else left[0]
+        term = matmul(left_rows, right[0])
+        total = term if total is None else total + term
+    size = pieces[0][3]
+    for index in range(4):
+        rows = slice(index * row_tile, (index + 1) * row_tile)
+        out_ref = keep_ref if index % 2 == 0 else send_ref
+        for k in range(total.shape[1] // size):
+            first = pl.multiple_of((k * parts + part) * size, size)
+            out_ref[index // 2, :, pl.ds(first, size)] = total[
+                rows, k * size : (k + 1) * size
+            ].astype(out_ref.dtype)
 
 
 def project(terms):
@@ -325,21 +338,25 @@
     )(*[t[0] for t in terms], *[t[2] for t in terms])
 
 
-def weight_grad_kernel(pieces, cuts, left_ref, *refs):
-    count = len(cuts)
-    out_ref, right_all, sems = refs[4 * count :]
+def weight_grad_kernel(pieces, cuts, counts, left_ref, *refs):
+    out_ref, right_all, sems = refs[sum(counts) :]
     step = pl.program_id(0)
 
     @pl.when(step == 0)
     def _():
-        copies = []
-        for k in range(count):
-            copies += fetch(refs[4 * k : 4 * k + 4], right_all.at[k], sems.at[k])
-        for copy in copies:
-            copy.wait()
+        first = 0
+        for k, count in enumerate(counts):
+            fetch(refs[first : first + count], right_all.at[k], sems.at[k])
+            first += count
 
     left = left_ref[...].reshape(left_ref.shape[-2:])
     for k, (start, stop) in enumerate(cuts):
+
+        @pl.when(step == start)
+        def _():
+            first = sum(counts[:k])
+            for copy in copies_of(refs[first : first + counts[k]], right_all.at[k], sems.at[k]):
+                copy.wait()
 
         @pl.when((step >= start) & (step < stop))
         def _():
@@ -347,7 +364,8 @@
 
 
 def weight_grad(parts, left, *rights):
-    part_rows, width = rights[0][0][0].shape
+    width = rights[0][0][0].shape[1]
+    counts = tuple(len(row_parts) for row_parts, _ in rights)
     rows, units = left.shape[-2:]
     tile = unit_tile(units)
     tiles = units // tile
@@ -361,14 +379,14 @@
     else:
         left_spec = pl.BlockSpec((rows, tile), lambda i: (0, i))
     return pl.pallas_call(
-        functools.partial(weight_grad_kernel, pieces, tuple(cuts)),
+        functools.partial(weight_grad_kernel, pieces, tuple(cuts), counts),
         grid=(first,),
         out_shape=jax.ShapeDtypeStruct((parts, first * tile, width // parts), jnp.bfloat16),
-        in_specs=[left_spec] + [anywhere()] * (4 * len(rights)),
+        in_specs=[left_spec] + [anywhere()] * sum(counts),
         out_specs=pl.BlockSpec((parts, tile, width // parts), lambda i: (0, i, 0)),
         scratch_shapes=[
             pltpu.VMEM((len(rights), rows, width), jnp.bfloat16),
-            pltpu.SemaphoreType.DMA((len(rights), 4)),
+            pltpu.SemaphoreType.DMA((len(rights), max(counts))),
         ],
         compiler_params=params(),
         cost_estimate=small_cost(),
@@ -390,11 +408,11 @@
 
     @pl.when(pl.program_id(0) == 0)
     def _():
-        copies = fetch(normed_parts, normed_all, sems)
+        fetch(normed_parts, normed_all, sems)
         weight_all[...] = side_by_side(pieces, weight_ref)
-        for copy in copies:
-            copy.wait()
-
+
+    for i, copy in enumerate(copies_of(normed_parts, normed_all, sems)):
+        pl.when(pl.program_id(0) == i)(copy.wait)
     here = pl.ds(pl.multiple_of(pl.program_id(0) * rows, rows), rows)
     out = mat_cols(normed_all[here, :], weight_all[...])
     for head in range(q_heads + kv_heads):
@@ -451,21 +469,31 @@
     )(*normed_parts, weight, gain_query, gain_key, cos, sin)
 
 
-def probabilities(query, key, row_segment, column_segment, row_slot, column_slot, dead, scale):
-    allowed = (row_segment == column_segment) & (column_slot <= row_slot)
-    masked = jnp.where(allowed, mat_cols(query, key) * scale, -1e30)
-    weights = jnp.where(allowed, jnp.exp(masked - jnp.max(masked, axis=-1, keepdims=True)), 0.0)
-    total = jnp.sum(weights, axis=-1, keepdims=True) + dead
-    return weights * (1.0 / total)
-
-
-def attend_kernel(scale, q_ref, k_ref, v_ref, row_ref, column_ref, out_ref):
+def mask_of(row_ref, column_ref):
+    allowed = (row_ref[0, :, 0:1] == column_ref[0, 0:1, :]) & (
+        column_ref[0, 1:2, :] <= row_ref[0, :, 1:2]
+    )
+    return jnp.where(allowed, 0.0, -1e30)
+
+
+def probabilities(query, key, mask, live, scale):
+    masked = mat_cols(query, key) * scale + mask
+    weights = jnp.exp(masked - jnp.max(masked, axis=-1, keepdims=True))
+    total = jnp.sum(weights, axis=-1, keepdims=True)
+    return weights * (live / total)
+
+
+def attend_kernel(scale, q_ref, k_ref, v_ref, row_ref, column_ref, out_ref, mask_ref):
     width = k_ref.shape[1]
-    marks = (row_ref[0, :, 0:1], column_ref[0, 0:1, :], row_ref[0, :, 1:2], column_ref[0, 1:2, :])
-    dead = wide(row_ref[0, :, 2:3])
+
+    @pl.when(pl.program_id(1) == 0)
+    def _():
+        mask_ref[...] = mask_of(row_ref, column_ref)
+
+    live = 1.0 - wide(row_ref[0, :, 2:3])
     for head in range(q_ref.shape[1] // width):
         columns = slice(head * width, (head + 1) * width)
-        probs = probabilities(q_ref[:, columns], k_ref[...], *marks, dead, scale)
+        probs = probabilities(q_ref[:, columns], k_ref[...], mask_ref[...], live, scale)
         out_ref[:, columns] = low(matmul(low(probs), v_ref[...]))
 
 
@@ -491,6 +519,7 @@
         out_shape=jax.ShapeDtypeStruct((rows, q_heads * head_width), jnp.bfloat16),
         in_specs=[query, key, value_spec, row_spec, column_spec],
         out_specs=query,
+        scratch_shapes=[pltpu.VMEM((rows // 2, rows // 2), jnp.float32)],
         compiler_params=params(),
         cost_estimate=small_cost(),
     )(rot, rot, value, row_marks, column_marks)
@@ -529,20 +558,27 @@
     grad_ref,
     gain_ref,
     cot_all,
+    mask_ref,
     sems,
 ):
     group, kv = pl.program_id(0), pl.program_id(1)
+    cot_parts = (cot_a, cot_b, cot_c, cot_d)
     rows, width = k_ref.shape
     per = q_heads // kv_heads
 
     @pl.when((group == 0) & (kv == 0))
     def _():
         gain_ref[...] = jnp.zeros_like(gain_ref)
-        for copy in fetch((cot_a, cot_b, cot_c, cot_d), cot_all, sems):
-            copy.wait()
-
-    marks = (row_ref[0, :, 0:1], column_ref[0, 0:1, :], row_ref[0, :, 1:2], column_ref[0, 1:2, :])
-    dead = wide(row_ref[0, :, 2:3])
+        fetch(cot_parts, cot_all, sems)
+
+    @pl.when(kv == 0)
+    def _():
+        mask_ref[...] = mask_of(row_ref, column_ref)
+
+    for i, copy in enumerate(copies_of(cot_parts, cot_all, sems)):
+        pl.when((group == i // 2) & (kv == 0))(copy.wait)
+
+    live = 1.0 - wide(row_ref[0, :, 2:3])
     here = pl.ds(pl.multiple_of(group * rows, rows), rows)
     context_grad = low(mat_cols(cot_all[here, :], side_by_side(pieces, weight_ref)))
     key, value, cos, sin = k_ref[...], v_ref[...], cos_ref[...], sin_ref[...]
@@ -551,7 +587,7 @@
     for head in range(per):
         columns = slice(head * width, (head + 1) * width)
         query, grad = q_ref[:, columns], context_grad[:, columns]
-        probs = probabilities(query, key, *marks, dead, scale)
+        probs = probabilities(query, key, mask_ref[...], live, scale)
         prob_grad = mat_cols(grad, value)
         part = mat_rows(low(probs), grad)
         value_grad = part if value_grad is None else value_grad + part
@@ -624,14 +660,53 @@
         out_specs=[whole((rows, columns)), whole((8, head_width))],
         scratch_shapes=[
             pltpu.VMEM((rows, width), jnp.bfloat16),
+            pltpu.VMEM((group_rows, group_rows), jnp.float32),
             pltpu.SemaphoreType.DMA((4,)),
         ],
         compiler_params=params(),
-        cost_estimate=small_cost(),
+        cost_estimate=large_cost(),
     )(
         *cot_parts, weight, rot, rot, value, raw, raw, row_marks, column_marks,
         gain_query, gain_key, cos, sin,
     )
+
+
+def norm_back_kernel(mine, mate, values, gain, cot, total_ref, low_ref, gain_ref):
+    @pl.when(pl.program_id(0) == 0)
+    def _():
+        gain_ref[...] = jnp.zeros_like(gain_ref)
+
+    grad = mine[...] + wide(mate[...])
+    rows = values[...]
+    scale = lax.rsqrt(jnp.mean(rows * rows, axis=-1, keepdims=True) + EPSILON)
+    unit = rows * scale
+    through = grad * gain[...]
+    total = wide(cot[...]) + scale * (
+        through - unit * jnp.mean(through * unit, axis=-1, keepdims=True)
+    )
+    total_ref[...] = total
+    low_ref[...] = low(total)
+    gain_ref[...] += jnp.sum(grad * unit, axis=0, keepdims=True)
+
+
+def norm_back(mine, mate, values, gain, cot):
+    rows, width = values.shape
+    tile = 64
+    block = pl.BlockSpec((tile, width), lambda i: (i, 0))
+    total, total_low, gain_grad = pl.pallas_call(
+        norm_back_kernel,
+        grid=(rows // tile,),
+        out_shape=[
+            jax.ShapeDtypeStruct((rows, width), jnp.float32),
+            jax.ShapeDtypeStruct((rows, width), jnp.bfloat16),
+            jax.ShapeDtypeStruct((1, width), jnp.float32),
+        ],
+        in_specs=[block, block, block, whole((1, width)), block],
+        out_specs=[block, block, whole((1, width))],
+        compiler_params=params(),
+        cost_estimate=small_cost(),
+    )(mine, mate, values, gain[None, :], cot)
+    return total, total_low, gain_grad[0]
 
 
 class Sequence:
@@ -681,6 +756,18 @@
     for bit in [PAIR] + outer_bits():
         blocks = [in_turn(x, y, 1, bit) for x, y in zip(blocks[::2], blocks[1::2])]
     return blocks[0]
+
+
+def outer_start(block):
+    return exchange(block, outer_bits()[0])
+
+
+def outer_end(block, received):
+    first, *others = outer_bits()
+    block = in_turn(block, received, 1, first)
+    for bit in others:
+        block = in_turn(block, exchange(block, bit), 1, bit)
+    return block
 
 
 def gather_weight(block):
@@ -729,9 +816,10 @@
 
 
 def scatter_grad(full):
-    return lax.psum_scatter(
+    total = lax.psum_scatter(
         full, "dp", axis_index_groups=xy_groups(), scatter_dimension=0
     )
+    return total.reshape(total.shape[-2:])
 
 
 def part_of(full, flip):
@@ -744,22 +832,21 @@
     far = part_of(full, X_BIT | Y_BIT)
     by_x, by_y = part_of(full, X_BIT), part_of(full, Y_BIT)
     return (
-        exchange(far[:half], X_BIT),
-        exchange(far[half:], Y_BIT),
-        exchange(by_x[:half], X_BIT),
-        exchange(by_y[half:], Y_BIT),
+        exchange(jnp.concatenate([far[:half], by_x[:half]], axis=0), X_BIT),
+        exchange(jnp.concatenate([far[half:], by_y[half:]], axis=0), Y_BIT),
         by_x[half:],
         by_y[:half],
     )
 
 
-def scatter_far(far_top, far_bottom, x_top, y_bottom, x_rest, y_rest):
-    x_bottom = exchange(low(wide(x_rest) + wide(far_bottom)), X_BIT)
-    y_top = exchange(low(wide(y_rest) + wide(far_top)), Y_BIT)
-    return (x_top, x_bottom, y_top, y_bottom)
-
-
-def scatter_end(full, x_top, x_bottom, y_top, y_bottom):
+def scatter_far(from_x, from_y, x_rest, y_rest):
+    half = x_rest.shape[0]
+    x_bottom = exchange(low(wide(x_rest) + wide(from_y[:half])), X_BIT)
+    y_top = exchange(low(wide(y_rest) + wide(from_x[:half])), Y_BIT)
+    return (x_bottom, y_top, from_x[half:], from_y[half:])
+
+
+def scatter_end(full, x_bottom, y_top, x_top, y_bottom):
     own = wide(part_of(full, 0))
     half = own.shape[0] // 2
     return jnp.concatenate(
@@ -771,8 +858,29 @@
     )
 
 
+def split_side(total, bit):
+    size = total.shape[1] // 2
+    side = bit_side(bit)
+    keep = lax.dynamic_slice_in_dim(total, side * size, size, 1)
+    send = lax.dynamic_slice_in_dim(total, (1 - side) * size, size, 1)
+    return (wide(keep), low(send))
+
+
+def outer_scatter_start(total):
+    first, *others = outer_bits()
+    for bit in reversed(others):
+        keep, send = split_side(total, bit)
+        total = keep + wide(exchange(send, bit))
+    keep, send = split_side(total, first)
+    return (keep, exchange(send, first))
+
+
+def team_scatter_start(keep, received):
+    keep, send = split_side(keep + wide(received), PAIR)
+    return (keep, exchange(send, PAIR))
+
+
 def last_start(total):
-    total = total.reshape(total.shape[-2:])
     masks = far_masks()
     size = total.shape[1] // len(masks)
     place = lax.axis_index("dp") // 4
@@ -799,12 +907,16 @@
     return (keep[0] + wide(received[0]), low(keep[1] + wide(received[1])))
 
 
-def total_sum(values):
+def near_sum(values):
     values = values + swap_core(values)
-    bit = 1
-    while bit < lax.axis_size("dp"):
+    for bit in (X_BIT, Y_BIT):
         values = values + exchange(values, bit)
-        bit *= 2
+    return values
+
+
+def far_sum(values):
+    for bit in [PAIR] + outer_bits():
+        values = values + exchange(values, bit)
     return values
 
 
@@ -855,9 +967,12 @@
     all_units = g_half[0].shape[1]
     units = all_units // MLP_PARTS
 
-    def chunk_own(chunk, s):
-        cut = slice(chunk * units, (chunk + 1) * units)
-        return jnp.concatenate([g_half[s][:, cut].T, u_half[s][:, cut].T, d_half[s][cut]], axis=0)
+    def mlp_side(s):
+        gate, up, down = g_half[s].T, u_half[s].T, d_half[s]
+        cuts = [slice(c * units, (c + 1) * units) for c in range(MLP_PARTS)]
+        return [
+            jnp.concatenate([w[cut] for w in (gate, up, down)], axis=0) for cut in cuts
+        ]
 
     token_float = to_order(wide(tokens))
     cot_float = to_order(wide(cotangent))
@@ -872,8 +987,9 @@
 
     normed, attn_norm_pull = jax.vjp(rms_norm, token_float, gain_attn_o)
     normed_low = low(normed)
+    normed_mate = exchange(lax.optimization_barrier((normed_low, ends_mate))[0], PAIR)
+    normed_core = swap_core(normed_low)
     branch_low = low(live_mine * cot_float)
-    normed_core = swap_core(normed_low)
     cosine_table, sine_table = rope_tables(positions, head_width)
     cos = jnp.concatenate([cosine_table, cosine_table], axis=1)
     sin = jnp.concatenate([-sine_table, sine_table], axis=1)
@@ -886,66 +1002,78 @@
     row_marks = jnp.stack(marks, axis=2)
     column_marks = jnp.stack([segment, slots_both] + marks[3:] + marks[3:4], axis=1)
     gain_q, gain_k = gain_query[None, :], gain_key[None, :]
-    chunks = [(chunk_own(c, 0), chunk_own(c, 1)) for c in range(MLP_PARTS)]
-    seq.mark(cos, sin, row_marks, column_marks, normed_low, *[v for c in chunks for v in c])
-
-    attn_far = seq.wait(*attn_far)
+    mlp_own, mlp_other = mlp_side(0), mlp_side(1)
+    rest_other = jnp.concatenate(mlp_other[1:], axis=0)
+    first_pair = exchange(mlp_other[0], PAIR)
+    seq.mark(cos, sin, row_marks, column_marks, branch_low, rest_other, *mlp_own)
+
+    first_pair, *attn_far = seq.wait(first_pair, *attn_far)
     attn_near = near_end(attn_own, attn_far)
     attn_x, attn_y = near_x_y(attn_near)
-    first_far = near_start(*chunks[0])
-    normed_mate = exchange(seq.tie(normed_low), PAIR)
-    attn_x, attn_y, *first_far = seq.wait(attn_x, attn_y, *first_far)
+    first_two = in_turn(mlp_own[0], first_pair, 1)
+    first_far = outer_start(first_two)
+    rest_pair = exchange(seq.tie(rest_other), PAIR)
+    attn_x, attn_y, first_far, normed_mate = seq.wait(attn_x, attn_y, first_far, normed_mate)
     attn_left, attn_right = far_x_y(attn_x, attn_y)
-    mlp_full = [gather_weight(near_end(chunks[0][0], first_far))]
-    second_far = near_start(*chunks[1])
-    attn_left, attn_right, normed_mate, *second_far = seq.wait(
-        attn_left, attn_right, normed_mate, *second_far
-    )
+    normed_all = (normed_low, normed_core, normed_mate, swap_core(normed_mate))
+    attn_left, attn_right, rest_pair = seq.wait(attn_left, attn_right, rest_pair)
+    second_two, third_two = [
+        in_turn(mlp_own[c], rest_pair[(c - 1) * 3 * units : c * 3 * units], 1)
+        for c in range(1, MLP_PARTS)
+    ]
+    second_far = outer_start(second_two)
+    half_rows = rows_dev // 2
+    branch_a = exchange(seq.tie(branch_low[:half_rows]), PAIR)
+    branch_core = swap_core(branch_low)
+    first_near = seq.tie(outer_end(first_two, first_far))
+    first_x, first_y = near_x_y(first_near)
     full_attn = assemble(attn_near, attn_x, attn_y, attn_left, attn_right)
-    normed_all = (normed_low, normed_core, normed_mate, swap_core(normed_mate))
-    second_near = near_end(chunks[1][0], second_far)
-    chunk_x, chunk_y = near_x_y(second_near)
-    third_far = near_start(*chunks[2])
     qk_raw, qk_rot, value_low = heads(
         normed_all, full_attn, gain_q, gain_k, cos, sin, q_heads, kv_heads
     )
     value_low = seq.mark(value_low)
+    second_far, branch_a, first_x, first_y = seq.wait(second_far, branch_a, first_x, first_y)
+    mlp_full = [None, gather_weight(outer_end(second_two, second_far))]
+    first_left, first_right = far_x_y(first_x, first_y)
+    third_far = outer_start(seq.tie(third_two))
+    branch_b = exchange(seq.tie(branch_low[half_rows:]), PAIR)
     context_low = seq.mark(
         attend(
             qk_rot, seq.tie(value_low), row_marks, column_marks, head_width, q_heads, kv_heads
         )
     )
-    attn_mine, attn_mate = team_halves(project([(context_low, None, full_attn, qkv_cols, q_cols)]))
+    keep, send = project([(context_low, None, full_attn, qkv_cols, q_cols)])
+    seq.mark(send)
+    third_far, branch_b, first_left, first_right = seq.wait(
+        third_far, branch_b, first_left, first_right
+    )
+    attn_mine, attn_mate = team_halves((keep, seq.tie(send)))
+    mlp_full.append(gather_weight(outer_end(third_two, third_far)))
     seq.mark(attn_mate)
     attn_mate = exchange(attn_mate, PAIR)
-    chunk_x, chunk_y, *third_far = seq.wait(chunk_x, chunk_y, *third_far)
-    chunk_left, chunk_right = far_x_y(chunk_x, chunk_y)
-    mlp_full += [None, gather_weight(near_end(chunks[2][0], third_far))]
-    branch_mate = exchange(seq.tie(branch_low), PAIR)
+    mlp_full[0] = seq.mark(
+        assemble(seq.tie(first_near), first_x, first_y, first_left, first_right)
+    )
+    branch_all = (
+        branch_low, branch_core, branch_a, branch_b, swap_core(branch_a), swap_core(branch_b)
+    )
     attn_mate = seq.wait(attn_mate)
     hidden_in = token_float + (attn_mine + wide(attn_mate))
-    mlp_normed, mlp_norm_pull = jax.vjp(rms_norm, hidden_in, gain_mlp_o)
-    mlp_low = seq.mark(low(mlp_normed))
+    mlp_low = seq.mark(low(rms_norm(hidden_in, gain_mlp_o)))
     mlp_row_mate = exchange(mlp_low, PAIR)
     mlp_row_mate = seq.wait(mlp_row_mate)
     mlp_all = (mlp_low, swap_core(mlp_low), mlp_row_mate, swap_core(mlp_row_mate))
-    branch_mate = seq.wait(branch_mate)
-    branch_all = (branch_low, swap_core(branch_low), branch_mate, swap_core(branch_mate))
-
     all_acts, mlp_scattered = [], []
-    mlp_full[0], chunk_left, chunk_right = seq.wait(mlp_full[0], chunk_left, chunk_right)
-    mlp_full[1] = assemble(second_near, chunk_x, chunk_y, chunk_left, chunk_right)
     acts, grad_full = mlp_units(mlp_all, branch_all, mlp_full[0], True)
     all_acts.append(acts)
     grad_full = seq.mark(grad_full)
     mlp_scattered.append(scatter_grad(grad_full))
-    mlp_full[2] = seq.wait(mlp_full[2])
-    mlp_full[1] = seq.tie(mlp_full[1])
+    mlp_full[1] = seq.wait(mlp_full[1])
     acts, grad_full = mlp_units(mlp_all, branch_all, mlp_full[1], True)
     all_acts.append(acts)
     grad_full = seq.mark(grad_full)
     mlp_scattered.append(scatter_grad(grad_full))
-    mlp_full[2] = seq.tie(mlp_full[2])
+    mlp_full[2] = seq.wait(mlp_full[2])
     (acts,) = mlp_units(mlp_all, branch_all, mlp_full[2], False)
     all_acts.append(acts)
     terms = [
@@ -954,75 +1082,75 @@
     back_mine, back_mate = team_halves(project(terms))
     seq.mark(back_mate)
     back_mate = exchange(back_mate, PAIR)
-    acts = seq.tie(acts)
-    grad_full = seq.mark(weight_grad(parts, acts, (mlp_all, 2), (branch_all, 1)))
-    mlp_scattered.append(scatter_grad(grad_full))
     terms = [(seq.tie(a), 2, w, 2 * units, units) for a, w in zip(all_acts, mlp_full)]
-    sum_mine, sum_mate = team_halves(project(terms))
-    sum_mate = seq.mark(sum_mate)
-    back_mate = seq.wait(back_mate)
-    mlp_back = back_mine + wide(back_mate)
-    hidden_from, gain_mlp_part = mlp_norm_pull(mlp_back)
-    hidden_grad_total = cot_float + hidden_from
-    cot_low = seq.mark(low(hidden_grad_total))
+    sum_keep, sum_send = project(terms)
+    seq.mark(sum_send)
+    back_mate, mlp_scattered[0] = seq.wait(back_mate, mlp_scattered[0])
+    hidden_grad_total, cot_low, gain_mlp_part = norm_back(
+        back_mine, back_mate, hidden_in, gain_mlp_o, to_order(cotangent)
+    )
+    cot_low = seq.mark(cot_low)
     cot_mate = exchange(cot_low, PAIR)
     cot_core = swap_core(cot_low)
-    sum_mate = exchange(seq.tie(sum_mate), PAIR)
-    mlp_scattered[0] = seq.wait(mlp_scattered[0])
-    lasts = [last_start(mlp_scattered[0])]
-    mlp_scattered[1], cot_mate = seq.wait(mlp_scattered[1], cot_mate)
-    lasts.append(last_start(mlp_scattered[1]))
+    grad_full = seq.mark(weight_grad(parts, seq.tie(acts), (mlp_all, 2), (branch_all, 1)))
+    mlp_scattered.append(scatter_grad(grad_full))
+    cot_mate, mlp_scattered[1] = seq.wait(cot_mate, mlp_scattered[1])
+    early = last_start(jnp.concatenate(mlp_scattered[:2], axis=0))
     cot_all = (cot_low, cot_core, cot_mate, swap_core(cot_mate))
     out_grad = seq.mark(weight_grad(parts, context_low, (cot_all, 1)))
-    out_steps = scatter_near(out_grad)
+    out_scattered = scatter_grad(out_grad)
     qkv_grad, gain_parts = attend_back(
         cot_all, seq.tie(full_attn), qk_rot, value_low, qk_raw, row_marks, column_marks,
         gain_q, gain_k, cos, sin, q_heads, kv_heads,
     )
-    qkv_grad = seq.mark(qkv_grad)
-    mlp_scattered[2], *out_steps = seq.wait(mlp_scattered[2], *out_steps)
-    out_steps = scatter_far(*out_steps)
-    lasts.append(last_start(mlp_scattered[2]))
-    token_mine, token_mate = team_halves(
-        project([(seq.tie(qkv_grad), None, full_attn, 0, qkv_cols)])
-    )
+    qkv_full = seq.mark(weight_grad(parts, qkv_grad, (normed_all, 1)))
+    qkv_steps = scatter_near(qkv_full)
+    keep, send = project([(seq.tie(qkv_grad), None, full_attn, 0, qkv_cols)])
+    seq.mark(send)
+    mlp_scattered[2], *early = seq.wait(mlp_scattered[2], *early)
+    late_keep, late_far = outer_scatter_start(mlp_scattered[2])
+    token_mine, token_mate = team_halves((keep, seq.tie(send)))
     token_mate = seq.mark(token_mate)
     token_mate = exchange(token_mate, PAIR)
-    qkv_full = seq.mark(weight_grad(parts, seq.tie(qkv_grad), (normed_all, 1)))
-    qkv_steps = scatter_near(qkv_full)
-    count = len(out_steps)
-    out_steps = seq.wait(*out_steps, *lasts[0])
-    out_steps, lasts[0] = out_steps[:count], out_steps[count:]
-    out_total = scatter_end(out_grad, *out_steps)
     qkv_steps = seq.wait(*qkv_steps)
     qkv_steps = scatter_far(*qkv_steps)
-    token_mate = seq.wait(token_mate)
+    sum_mine, sum_mate = team_halves((sum_keep, seq.tie(sum_send)))
+    token_mate, late_far = seq.wait(token_mate, late_far)
+    late_mine, late_other = team_scatter_start(late_keep, late_far)
+    sum_mate = exchange(seq.tie(sum_mate), PAIR)
+    early_mine, early_other = last_end(early[0], early[1:])
     attn_back = token_mine + wide(token_mate)
     token_from, gain_attn_part = attn_norm_pull(attn_back)
-    gain_sums = total_sum(
+    grad_tokens = from_order(hidden_grad_total + token_from)
+    gain_parts = near_sum(
         jnp.concatenate(
-            [from_order(gain_attn_part), from_order(gain_mlp_part), gain_parts[0], gain_parts[1]]
+            [
+                from_order(gain_attn_part),
+                from_order(gain_mlp_part),
+                gain_parts[0],
+                gain_parts[1],
+            ]
         )
     )
-    grad_tokens = seq.mark(from_order(hidden_grad_total + token_from))
-    qkv_steps = seq.wait(*qkv_steps)
-    attn_last = last_start(
-        jnp.concatenate([scatter_end(qkv_full, *qkv_steps), out_total], axis=0)
-    )
-    lasts[1] = seq.wait(*lasts[1])
-    mlp_sum = sum_mine + wide(seq.wait(sum_mate))
+    seq.mark(grad_tokens, gain_parts)
+    out_scattered, *qkv_steps = seq.wait(out_scattered, *qkv_steps)
+    final = last_start(
+        jnp.concatenate([scatter_end(qkv_full, *qkv_steps), wide(out_scattered)], axis=0)
+    )
+    late_other, sum_mate = seq.wait(late_other, sum_mate)
+    late_other = wide(late_other)
+    mlp_sum = sum_mine + wide(sum_mate)
     out_tokens = from_order(low(hidden_in + live_mine * mlp_sum))
-    lasts[2] = seq.wait(*lasts[2])
-    teams = [last_end(last[0], last[1:]) for last in lasts]
-    attn_team = last_end(attn_last[0], attn_last[1:])
+    gain_sums = far_sum(seq.tie(gain_parts))
+    cut = 3 * units
+    teams = [
+        (early_mine[:cut], early_other[:cut]),
+        (early_mine[cut:], early_other[cut:]),
+        (late_mine, late_other),
+    ]
 
     def pick(pair, start, stop):
         return in_turn(pair[0][start:stop], pair[1][start:stop], 0)
-
-    grad_query = pick(attn_team, 0, q_cols).T
-    grad_key = pick(attn_team, q_cols, q_cols + kv_cols).T
-    grad_value = pick(attn_team, q_cols + kv_cols, qkv_cols).T
-    grad_out = pick(attn_team, qkv_cols, qkv_cols + q_cols)
 
     def units_of(kind):
         cut = slice(kind * units, (kind + 1) * units)
@@ -1035,6 +1163,13 @@
     grad_gate = units_of(0).T
     grad_up = units_of(1).T
     grad_down = units_of(2)
+    seq.mark(grad_gate, grad_up, grad_down, out_tokens, grad_tokens)
+    final = seq.wait(*final)
+    attn_team = last_end(final[0], final[1:])
+    grad_out = pick(attn_team, qkv_cols, qkv_cols + q_cols)
+    grad_query = pick(attn_team, 0, q_cols).T
+    grad_key = pick(attn_team, q_cols, q_cols + kv_cols).T
+    grad_value = pick(attn_team, q_cols + kv_cols, qkv_cols).T
     return (
         out_tokens,
         grad_tokens,

time: 858 us -> 705 us (0.82)
  waiting for transfers between devices: 362 us -> 266 us
  starting transfers between devices: 79.7 us -> 42.5 us
  other arithmetic: 87 us -> 74.6 us
  Pallas kernels: 262 us -> 250 us
    ppermute x57 -> x42, waiting for transfers between devices: 350 us -> 251 us  [exchange(): return lax.ppermute(values, 'dp', [(i, i ^ mask) for i in range(size)])]
    ppermute x57 -> x42, starting transfers between devices: 77.1 us -> 40.2 us  [exchange(): return lax.ppermute(values, 'dp', [(i, i ^ mask) for i in range(size)])]
    pallas_call x4, Pallas kernels: 73.4 us -> 63.7 us  [project(): pl.pallas_call(functools.partial(project_kernel, pieces, rows, parts), gr...]
    select_n x10 -> x11, other arithmetic: 9.55 us -> 17.3 us  [in_turn(): jnp.where(bit_side(bit) == 0, jnp.concatenate([mine, theirs], axis=axis),...]
    unnamed x223 -> x184, local copies, waits for them, and re-layouts: 21 us -> 27 us
    convert_element_type x13 -> x10, other arithmetic: 24 us -> 20.2 us  [low(): return values.astype(jnp.bfloat16)]
    pallas_call x6 -> x7, Pallas kernels: 112 us -> 114 us  [the longest x3 73.3 us: mlp_units(): pl.pallas_call(functools.partial(mlp_kernel, pieces, tiles, with_grad, co...]
  transfers between devices with their start and end apart: 75 -> 62, of which waited for: 35 -> 29; matrix products, arithmetic and copies ran while one was open for 13% -> 14% of each run, Pallas kernels for 29% -> 36%
where the time goes in v2:
time: 705 us; the launch traced here: 699 us
  waiting for transfers between devices  266 us (38%)
  Pallas kernels  250 us (35%)
  other arithmetic  74.6 us (11%)
  local copies, waits for them, and re-layouts  50.3 us (7%)
  starting transfers between devices  42.5 us (6%)
  between operations  15.6 us (2%)
    ppermute x42, waiting for transfers between devices, exchange(): return lax.ppermute(values, 'dp', [(i, i ^ mask) for i in range(size)])  251 us
    pallas_call x3, Pallas kernels, mlp_units(): pl.pallas_call(functools.partial(mlp_kernel, pieces, tiles, with_grad, co...  73.3 us
    pallas_call x4, Pallas kernels, project(): pl.pallas_call(functools.partial(project_kernel, pieces, rows, parts), gr...  63.7 us
    ppermute x42, starting transfers between devices, exchange(): return lax.ppermute(values, 'dp', [(i, i ^ mask) for i in range(size)])  40.2 us
    pallas_call x3, Pallas kernels, weight_grad(): pl.pallas_call(functools.partial(weight_grad_kernel, pieces, tuple(cuts),...  33.5 us
    pallas_call x1, Pallas kernels, attend_back(): pl.pallas_call(functools.partial(attend_back_kernel, pieces_of(parts, wid...  33.1 us
    unnamed x184, local copies, waits for them, and re-layouts  27 us
    convert_element_type x10, other arithmetic, low(): return values.astype(jnp.bfloat16)  20.2 us
  transfers between devices with their start and end apart: 62, of which 29 were waited for; matrix products, arithmetic and copies ran while one was open for 14% of the time, Pallas kernels for 36%

profile of v2, /device:TPU:0, one launch (start us, length us, event | category | flops | bytes accessed | tf_op | source)
XLA Modules:
  0.0 699.1 jit_solution(10090121695147776724)
XLA Ops:
  66.4 42.2 %collective-permute-done.8 = bf16[1536,256]{1,0:T(8,128)(2,1)S(1)} collective-permute-done((bf16[1536,256]{1,0:T(8,128)(2,1)S(1)}, bf16[1536,256]{1,0:T(8,128)(2,1)S(1)}, u32[]{:S(2)}, u32[]{:S(2)}) %collective-permute-start.8) | collective-permute-done | bytes 786464 | tf_op jit(solution)/shard_map/ppermute | solution.py:66
  115.1 9.6 %collective-permute-done.13 = bf16[3072,128]{1,0:T(8,128)(2,1)S(1)} collective-permute-done((bf16[3072,128]{1,0:T(8,128)(2,1)S(1)}, bf16[3072,128]{1,0:T(8,128)(2,1)S(1)}, u32[]{:S(2)}, u32[]{:S(2)}) %collective-permute-start.13) | collective-permute-done | bytes 786464 | tf_op jit(solution)/shard_map/ppermute | solution.py:66
  145.8 12.1 %shard_map.238 = (f32[1280,768]{1,0:T(8,128)}, bf16[1280,768]{1,0:T(8,128)(2,1)}, bf16[1280,256]{1,0:T(8,128)(2,1)}) custom-call(bf16[320,2048]{1,0:T(8,128)(2,1)} %fusion.2.refs_0_, bf16[320,2048]{1,0:T(8,128)(2,1)} %copy-done.14, bf16[320,2048]{1,0:T(8,128)(2,1)} %collective-permute-done.9.refs_2_, bf16[320,2048]{1,0:T(8,128)(2,1)} %collective-permute-done.10.refs_3_, ...), custom_call_target="tpu_custom_call" | custom-call | flops 1000 | bytes 1000 | tf_op jit(solution)/shard_map/pallas_call | solution.py:443
  174.6 12.5 %shard_map.239.refs_0_.left_ref = bf16[1280,512]{1,0:T(8,128)(2,1)} custom-call(bf16[1280,768]{1,0:T(8,128)(2,1)} %get-tuple-element.113.q_ref.k_ref, bf16[1280,768]{1,0:T(8,128)(2,1)} %get-tuple-element.113.q_ref.k_ref, bf16[1280,256]{1,0:T(8,128)(2,1)} %get-tuple-element.122.v_ref, s32[2,640,8]{2,1,0:T(8,128)} %stack.55.row_ref, ...), custom_call_target="tpu_custom_call" | custom-call | flops 1000 | bytes 1000 | tf_op jit(solution)/shard_map/pallas_call | solution.py:516
  187.1 8.9 %shard_map.240 = (f32[2,320,2048]{2,1,0:T(8,128)}, bf16[2,320,2048]{2,1,0:T(8,128)(2,1)}) custom-call(bf16[1280,512]{1,0:T(8,128)(2,1)} %shard_map.239.refs_0_.left_ref, bf16[4,1536,512]{2,1,0:T(8,128)(2,1)} %shard_map.237.refs_4_.refs_1_.weight_ref), custom_call_target="tpu_custom_call" | custom-call | flops 1000 | bytes 1000 | tf_op jit(solution)/shard_map/pallas_call | solution.py:327
  196.0 10.6 %collective-permute-done.19.refs_7_ = bf16[160,2048]{1,0:T(8,128)(2,1)} collective-permute-done((bf16[160,2048]{1,0:T(8,128)(2,1)}, bf16[160,2048]{1,0:T(8,128)(2,1)}, u32[]{:S(2)}, u32[]{:S(2)}) %collective-permute-start.19) | collective-permute-done | bytes 655392 | tf_op jit(solution)/shard_map/ppermute | solution.py:66
  225.9 24.0 %collective-permute-done.23 = bf16[320,2048]{1,0:T(8,128)(2,1)S(1)} collective-permute-done((bf16[320,2048]{1,0:T(8,128)(2,1)}, bf16[320,2048]{1,0:T(8,128)(2,1)S(1)}, u32[]{:S(2)}, u32[]{:S(2)}) %collective-permute-start.23) | collective-permute-done | bytes 1310752 | tf_op jit(solution)/shard_map/ppermute | solution.py:66
  254.8 29.2 %collective-permute-done.25.refs_2_ = bf16[320,2048]{1,0:T(8,128)(2,1)S(1)} collective-permute-done((bf16[320,2048]{1,0:T(8,128)(2,1)S(1)}, bf16[320,2048]{1,0:T(8,128)(2,1)S(1)}, u32[]{:S(2)}, u32[]{:S(2)}) %collective-permute-start.25) | collective-permute-done | bytes 1310752 | tf_op jit(solution)/shard_map/ppermute | solution.py:66
  291.0 27.5 %shard_map.242 = (bf16[3,1280,512]{2,1,0:T(8,128)(2,1)}, bf16[4,1536,512]{2,1,0:T(8,128)(2,1)}) custom-call(bf16[320,2048]{1,0:T(8,128)(2,1)} %copy-done.3, bf16[320,2048]{1,0:T(8,128)(2,1)} %copy-done.8, bf16[320,2048]{1,0:T(8,128)(2,1)} %copy-done.6, bf16[320,2048]{1,0:T(8,128)(2,1)} %collective-permute-done.26.refs_3_, bf16[320,2048]{1,0:T(8,128)(2,1)} %copy-done, ...), custom_call_target="tpu_custom_call" | custom-call | flops 1000 | bytes 1000 | tf_op jit(solution)/shard_map/pallas_call | solution.py:274
  318.6 27.8 %shard_map.243 = (bf16[3,1280,512]{2,1,0:T(8,128)(2,1)}, bf16[4,1536,512]{2,1,0:T(8,128)(2,1)}) custom-call(bf16[320,2048]{1,0:T(8,128)(2,1)} %copy-done.3, bf16[320,2048]{1,0:T(8,128)(2,1)} %copy-done.8, bf16[320,2048]{1,0:T(8,128)(2,1)} %copy-done.6, bf16[320,2048]{1,0:T(8,128)(2,1)} %collective-permute-done.26.refs_3_, bf16[320,2048]{1,0:T(8,128)(2,1)} %copy-done, ...), custom_call_target="tpu_custom_call" | custom-call | flops 1000 | bytes 1000 | tf_op jit(solution)/shard_map/pallas_call | solution.py:274
  346.5 18.1 %shard_map.244.refs_4_.refs_5_.refs_2_.left_ref = bf16[3,1280,512]{2,1,0:T(8,128)(2,1)} custom-call(bf16[320,2048]{1,0:T(8,128)(2,1)} %copy-done.3, bf16[320,2048]{1,0:T(8,128)(2,1)} %copy-done.8, bf16[320,2048]{1,0:T(8,128)(2,1)} %copy-done.6, bf16[320,2048]{1,0:T(8,128)(2,1)} %collective-permute-done.26.refs_3_, bf16[320,2048]{1,0:T(8,128)(2,1)} %copy-done, ...), custom_call_target="tpu_custom_call" | custom-call | flops 1000 | bytes 1000 | tf_op jit(solution)/shard_map/pallas_call | solution.py:274
  364.6 25.7 %shard_map.245 = (f32[2,320,2048]{2,1,0:T(8,128)}, bf16[2,320,2048]{2,1,0:T(8,128)(2,1)}) custom-call(bf16[3,1280,512]{2,1,0:T(8,128)(2,1)} %get-tuple-element.143.refs_0_.refs_1_, bf16[3,1280,512]{2,1,0:T(8,128)(2,1)} %get-tuple-element.143.refs_0_.refs_1_, bf16[3,1280,512]{2,1,0:T(8,128)(2,1)} %get-tuple-element.144.refs_2_.refs_3_.refs_1_, ...), custom_call_target="tpu_custom_call" | custom-call | flops 1000 | bytes 1000 | tf_op jit(solution)/shard_map/pallas_call | solution.py:327
  401.1 16.8 %shard_map.246 = (f32[2,320,2048]{2,1,0:T(8,128)}, bf16[2,320,2048]{2,1,0:T(8,128)(2,1)}) custom-call(bf16[3,1280,512]{2,1,0:T(8,128)(2,1)} %get-tuple-element.143.refs_0_.refs_1_, bf16[3,1280,512]{2,1,0:T(8,128)(2,1)} %get-tuple-element.144.refs_2_.refs_3_.refs_1_, bf16[3,1280,512]{2,1,0:T(8,128)(2,1)} %shard_map.244.refs_4_.refs_5_.refs_2_.left_ref, ...), custom_call_target="tpu_custom_call" | custom-call | flops 1000 | bytes 1000 | tf_op jit(solution)/shard_map/pallas_call | solution.py:327
  417.9 13.4 %collective-permute-done.31.mate = bf16[320,2048]{1,0:T(8,128)(2,1)S(1)} collective-permute-done((bf16[320,2048]{1,0:T(8,128)(2,1)S(1)}, bf16[320,2048]{1,0:T(8,128)(2,1)S(1)}, u32[]{:S(2)}, u32[]{:S(2)}) %collective-permute-start.31) | collective-permute-done | bytes 1310752 | tf_op jit(solution)/shard_map/ppermute | solution.py:66
  432.4 7.3 %shard_map.247 = (f32[320,2048]{1,0:T(8,128)}, bf16[320,2048]{1,0:T(8,128)(2,1)}, f32[1,2048]{1,0:T(1,128)}) custom-call(f32[320,2048]{1,0:T(8,128)} %get-tuple-element.261.mine, bf16[320,2048]{1,0:T(8,128)(2,1)} %copy-done.33, f32[320,2048]{1,0:T(8,128)} %copy-done.1, f32[1,2048]{1,0:T(1,128)} %bitcast.119, bf16[320,2048]{1,0:T(8,128)(2,1)} %cot.1), custom_call_target="tpu_custom_call" | custom-call | flops 1000 | bytes 1000 | tf_op jit(solution)/shard_map/pallas_call | solution.py:696
  440.3 14.6 %shard_map.248 = bf16[4,1536,512]{2,1,0:T(8,128)(2,1)} custom-call(bf16[3,1280,512]{2,1,0:T(8,128)(2,1)} %shard_map.244.refs_4_.refs_5_.refs_2_.left_ref, bf16[320,2048]{1,0:T(8,128)(2,1)} %copy-done.3, bf16[320,2048]{1,0:T(8,128)(2,1)} %copy-done.8, bf16[320,2048]{1,0:T(8,128)(2,1)} %copy-done.6, bf16[320,2048]{1,0:T(8,128)(2,1)} %collective-permute-done.26.refs_3_, ...), custom_call_target="tpu_custom_call" | custom-call | flops 1000 | bytes 1000 | tf_op jit(solution)/shard_map/pallas_call | solution.py:381
  454.9 15.2 %collective-permute-done.33.refs_2_.cot_c = bf16[320,2048]{1,0:T(8,128)(2,1)} collective-permute-done((bf16[320,2048]{1,0:T(8,128)(2,1)}, bf16[320,2048]{1,0:T(8,128)(2,1)}, u32[]{:S(2)}, u32[]{:S(2)}) %collective-permute-start.33) | collective-permute-done | bytes 1310752 | tf_op jit(solution)/shard_map/ppermute | solution.py:66
  478.7 7.9 %shard_map.249 = bf16[4,512,512]{2,1,0:T(8,128)(2,1)} custom-call(bf16[1280,512]{1,0:T(8,128)(2,1)} %shard_map.239.refs_0_.left_ref, bf16[320,2048]{1,0:T(8,128)(2,1)} %get-tuple-element.149.refs_0_.cot_a, bf16[320,2048]{1,0:T(8,128)(2,1)} %collective-permute-done.32.refs_1_.cot_b, bf16[320,2048]{1,0:T(8,128)(2,1)} %collective-permute-done.33.refs_2_.cot_c, ...), custom_call_target="tpu_custom_call" | custom-call | flops 1000 | bytes 1000 | tf_op jit(solution)/shard_map/pallas_call | solution.py:381
  486.6 33.1 %shard_map.250 = (bf16[1280,1024]{1,0:T(8,128)(2,1)}, f32[8,128]{1,0:T(8,128)}) custom-call(bf16[320,2048]{1,0:T(8,128)(2,1)} %get-tuple-element.149.refs_0_.cot_a, bf16[320,2048]{1,0:T(8,128)(2,1)} %collective-permute-done.32.refs_1_.cot_b, bf16[320,2048]{1,0:T(8,128)(2,1)} %collective-permute-done.33.refs_2_.cot_c, ...), custom_call_target="tpu_custom_call" | custom-call | flops 399999991808 | bytes 1000 | tf_op jit(solution)/shard_map/pallas_call | solution.py:632
  519.7 11.1 %shard_map.251 = bf16[4,1024,512]{2,1,0:T(8,128)(2,1)} custom-call(bf16[1280,1024]{1,0:T(8,128)(2,1)} %get-tuple-element.155.left_ref.refs_0_, bf16[320,2048]{1,0:T(8,128)(2,1)} %fusion.2.refs_0_, bf16[320,2048]{1,0:T(8,128)(2,1)} %copy-done.14, bf16[320,2048]{1,0:T(8,128)(2,1)} %collective-permute-done.9.refs_2_, ...), custom_call_target="tpu_custom_call" | custom-call | flops 1000 | bytes 1000 | tf_op jit(solution)/shard_map/pallas_call | solution.py:381
  530.8 12.3 %shard_map.252 = (f32[2,320,2048]{2,1,0:T(8,128)}, bf16[2,320,2048]{2,1,0:T(8,128)(2,1)}) custom-call(bf16[1280,1024]{1,0:T(8,128)(2,1)} %get-tuple-element.155.left_ref.refs_0_, bf16[4,1536,512]{2,1,0:T(8,128)(2,1)} %shard_map.237.refs_4_.refs_1_.weight_ref), custom_call_target="tpu_custom_call" | custom-call | flops 1000 | bytes 1000 | tf_op jit(solution)/shard_map/pallas_call | solution.py:327
  561.1 23.8 %collective-permute-done.35 = bf16[1024,512]{1,0:T(8,128)(2,1)S(1)} collective-permute-done((bf16[1024,512]{1,0:T(8,128)(2,1)S(1)}, bf16[1024,512]{1,0:T(8,128)(2,1)S(1)}, u32[]{:S(2)}, u32[]{:S(2)}) %collective-permute-start.35) | collective-permute-done | bytes 1048608 | tf_op jit(solution)/shard_map/ppermute | solution.py:66
  593.6 11.2 %collective-permute-done.43 = bf16[1536,256]{1,0:T(8,128)(2,1)S(1)} collective-permute-done((bf16[1536,256]{1,0:T(8,128)(2,1)S(1)}, bf16[1536,256]{1,0:T(8,128)(2,1)S(1)}, u32[]{:S(2)}, u32[]{:S(2)}) %collective-permute-start.43) | collective-permute-done | bytes 786464 | tf_op jit(solution)/shard_map/ppermute | solution.py:66
  632.0 36.6 %collective-permute-done.45 = bf16[320,2048]{1,0:T(8,128)(2,1)} collective-permute-done((bf16[320,2048]{1,0:T(8,128)(2,1)}, bf16[320,2048]{1,0:T(8,128)(2,1)}, u32[]{:S(2)}, u32[]{:S(2)}) %collective-permute-start.45) | collective-permute-done | bytes 1310752 | tf_op jit(solution)/shard_map/ppermute | solution.py:66
  (434 shorter events, 232.2 us)
Async XLA Ops:
  7.2 311.4 %all-gather.3.cloned.1.call-start = ((), (), s32[]{:S(2)}) async-start(), calls=%async_computation.4 | async-start | bytes 7864320 | tf_op jit(solution)/shard_map/all_gather | solution.py:774
  10.5 39.0 %collective-permute-start.4 = (bf16[1536,128]{1,0:T(8,128)(2,1)}, bf16[1536,128]{1,0:T(8,128)(2,1)}, u32[]{:S(2)}, u32[]{:S(2)}) collective-permute-start(bf16[1536,128]{1,0:T(8,128)(2,1)} %pad_maximum_fusion.7), channel_id=1, source_target_pairs={{0,24},{2,26},{4,28},{6,30},{8,16},{10,18},{12,20},{14,22},{16,8},... | collective-permute-start | bytes 1179656 | tf_op jit(solution)/shard_map/ppermute | solution.py:66
  54.9 54.6 %collective-permute-start.7 = (bf16[1536,512]{1,0:T(8,128)(2,1)}, bf16[1536,512]{1,0:T(8,128)(2,1)}, u32[]{:S(2)}, u32[]{:S(2)}) collective-permute-start(bf16[1536,512]{1,0:T(8,128)(2,1)} %maximum_select_fusion.own_ref), channel_id=1, source_target_pairs={{0,4},{2,6},{4,0},{6,2},{8,12},{10,14},{12,8},{14,10},{16,20},{18,... | collective-permute-start | bytes 4718600 | tf_op jit(solution)/shard_map/ppermute | solution.py:66
  56.4 53.1 %collective-permute-start.6 = (bf16[1536,512]{1,0:T(8,128)(2,1)}, bf16[1536,512]{1,0:T(8,128)(2,1)}, u32[]{:S(2)}, u32[]{:S(2)}) collective-permute-start(bf16[1536,512]{1,0:T(8,128)(2,1)} %maximum_select_fusion.own_ref), channel_id=1, source_target_pairs={{0,2},{2,0},{4,6},{6,4},{8,10},{10,8},{12,14},{14,12},{16,18},{18,... | collective-permute-start | bytes 4718600 | tf_op jit(solution)/shard_map/ppermute | solution.py:66
  60.6 48.9 %collective-permute-start.9 = (bf16[320,2048]{1,0:T(8,128)(2,1)}, bf16[320,2048]{1,0:T(8,128)(2,1)}, u32[]{:S(2)}, u32[]{:S(2)}) collective-permute-start(bf16[320,2048]{1,0:T(8,128)(2,1)} %fusion.2.refs_0_), channel_id=1, source_target_pairs={{0,8},{2,10},{4,12},{6,14},{8,0},{10,2},{12,4},{14,6},{16,24},{18,... | collective-permute-start | bytes 3932168 | tf_op jit(solution)/shard_map/ppermute | solution.py:66
  65.5 43.2 %collective-permute-start.8 = (bf16[1536,256]{1,0:T(8,128)(2,1)S(1)}, bf16[1536,256]{1,0:T(8,128)(2,1)S(1)}, u32[]{:S(2)}, u32[]{:S(2)}) collective-permute-start(bf16[1536,256]{1,0:T(8,128)(2,1)S(1)} %maximum_select_fusion.6), channel_id=1, source_target_pairs={{0,16},{2,18},{4,20},{6,22},{8,24},{10,26},{12,28},{14,30},{16,0},... | collective-permute-start | bytes 2359304 | tf_op jit(solution)/shard_map/ppermute | solution.py:66
  66.3 58.4 %collective-permute-start.13 = (bf16[3072,128]{1,0:T(8,128)(2,1)S(1)}, bf16[3072,128]{1,0:T(8,128)(2,1)S(1)}, u32[]{:S(2)}, u32[]{:S(2)}) collective-permute-start(bf16[3072,128]{1,0:T(8,128)(2,1)S(1)} %copy-done.58), channel_id=1, source_target_pairs={{0,8},{2,10},{4,12},{6,14},{8,0},{10,2},{12,4},{14,6},{16,24},{18,... | collective-permute-start | bytes 2359304 | tf_op jit(solution)/shard_map/ppermute | solution.py:66
  167.5 179.0 %all-gather.5.cloned.1.call-start = ((), (), s32[]{:S(2)}) async-start(), calls=%async_computation.5 | async-start | bytes 7864320 | tf_op jit(solution)/shard_map/all_gather | solution.py:774
  210.2 221.1 %reduce-scatter.13.cloned.1.call-start = ((), (), s32[]{:S(2)}) async-start(), calls=%async_computation.6 | async-start | bytes 7864320
  318.5 151.6 %reduce-scatter.15.cloned.1.call-start = ((), (), s32[]{:S(2)}) async-start(), calls=%async_computation.7 | async-start | bytes 7864320
  346.4 198.8 %reduce-scatter.17.cloned.1.call-start = ((), (), s32[]{:S(2)}) async-start(), calls=%async_computation.8 | async-start | bytes 7864320
  440.3 38.4 %collective-permute-start.32 = (bf16[320,2048]{1,0:T(8,128)(2,1)}, bf16[320,2048]{1,0:T(8,128)(2,1)}, u32[]{:S(2)}, u32[]{:S(2)}) collective-permute-start(bf16[320,2048]{1,0:T(8,128)(2,1)} %get-tuple-element.149.refs_0_.cot_a), channel_id=1, source_target_pairs={{0,1},{1,0},{2,3},{3,2},{4,5},{5,4},{6,7},{7,6},{8,9},{9,8},{10,11... | collective-permute-start | bytes 3932168 | tf_op jit(solution)/shard_map/ppermute | solution.py:730
  470.2 152.9 %reduce-scatter.19.cloned.1.call-start = ((), (), s32[]{:S(2)}) async-start(), calls=%async_computation.9 | async-start | bytes 2621440
  474.3 68.7 %collective-permute-start.39 = (bf16[3072,128]{1,0:T(8,128)(2,1)}, bf16[3072,128]{1,0:T(8,128)(2,1)}, u32[]{:S(2)}, u32[]{:S(2)}) collective-permute-start(bf16[3072,128]{1,0:T(8,128)(2,1)} %get-tuple-element.271), channel_id=1, source_target_pairs={{0,24},{2,26},{4,28},{6,30},{8,16},{10,18},{12,20},{14,22},{16,8},... | collective-permute-start | bytes 2359304 | tf_op jit(solution)/shard_map/ppermute | solution.py:66
  474.4 70.8 %collective-permute-start.38 = (bf16[3072,128]{1,0:T(8,128)(2,1)}, bf16[3072,128]{1,0:T(8,128)(2,1)}, u32[]{:S(2)}, u32[]{:S(2)}) collective-permute-start(bf16[3072,128]{1,0:T(8,128)(2,1)} %get-tuple-element.272), channel_id=1, source_target_pairs={{0,16},{2,18},{4,20},{6,22},{8,24},{10,26},{12,28},{14,30},{16,0},... | collective-permute-start | bytes 2359304 | tf_op jit(solution)/shard_map/ppermute | solution.py:66
  476.4 68.8 %collective-permute-start.37 = (bf16[3072,128]{1,0:T(8,128)(2,1)}, bf16[3072,128]{1,0:T(8,128)(2,1)}, u32[]{:S(2)}, u32[]{:S(2)}) collective-permute-start(bf16[3072,128]{1,0:T(8,128)(2,1)} %get-tuple-element.273), channel_id=1, source_target_pairs={{0,8},{2,10},{4,12},{6,14},{8,0},{10,2},{12,4},{14,6},{16,24},{18,... | collective-permute-start | bytes 2359304 | tf_op jit(solution)/shard_map/ppermute | solution.py:66
  547.4 37.5 %collective-permute-start.35 = (bf16[1024,512]{1,0:T(8,128)(2,1)S(1)}, bf16[1024,512]{1,0:T(8,128)(2,1)S(1)}, u32[]{:S(2)}, u32[]{:S(2)}) collective-permute-start(bf16[1024,512]{1,0:T(8,128)(2,1)S(1)} %pad_maximum_fusion.1), channel_id=1, source_target_pairs={{0,2},{2,0},{4,6},{6,4},{8,10},{10,8},{12,14},{14,12},{16,18},{18,... | collective-permute-start | bytes 3145736 | tf_op jit(solution)/shard_map/ppermute | solution.py:66
  548.8 38.7 %collective-permute-start.36 = (bf16[1024,512]{1,0:T(8,128)(2,1)S(1)}, bf16[1024,512]{1,0:T(8,128)(2,1)S(1)}, u32[]{:S(2)}, u32[]{:S(2)}) collective-permute-start(bf16[1024,512]{1,0:T(8,128)(2,1)S(1)} %pad_maximum_fusion.2), channel_id=1, source_target_pairs={{0,4},{2,6},{4,0},{6,2},{8,12},{10,14},{12,8},{14,10},{16,20},{18,... | collective-permute-start | bytes 3145736 | tf_op jit(solution)/shard_map/ppermute | solution.py:66
  559.2 47.7 %collective-permute-start.42 = (bf16[320,2048]{1,0:T(8,128)(2,1)S(1)}, bf16[320,2048]{1,0:T(8,128)(2,1)S(1)}, u32[]{:S(2)}, u32[]{:S(2)}) collective-permute-start(bf16[320,2048]{1,0:T(8,128)(2,1)S(1)} %fusion.12), channel_id=1, source_target_pairs={{0,8},{2,10},{4,12},{6,14},{8,0},{10,2},{12,4},{14,6},{16,24},{18,... | collective-permute-start | bytes 3932168 | tf_op jit(solution)/shard_map/ppermute | solution.py:66
  559.4 45.4 %collective-permute-start.43 = (bf16[1536,256]{1,0:T(8,128)(2,1)S(1)}, bf16[1536,256]{1,0:T(8,128)(2,1)S(1)}, u32[]{:S(2)}, u32[]{:S(2)}) collective-permute-start(bf16[1536,256]{1,0:T(8,128)(2,1)S(1)} %constant_dynamic-slice_fusion.4), channel_id=1, source_target_pairs={{0,16},{2,18},{4,20},{6,22},{8,24},{10,26},{12,28},{14,30},{16,0},... | collective-permute-start | bytes 2359304 | tf_op jit(solution)/shard_map/ppermute | solution.py:66
  617.1 51.5 %collective-permute-start.45 = (bf16[320,2048]{1,0:T(8,128)(2,1)}, bf16[320,2048]{1,0:T(8,128)(2,1)}, u32[]{:S(2)}, u32[]{:S(2)}) collective-permute-start(bf16[320,2048]{1,0:T(8,128)(2,1)} %fusion.13), channel_id=1, source_target_pairs={{0,8},{2,10},{4,12},{6,14},{8,0},{10,2},{12,4},{14,6},{16,24},{18,... | collective-permute-start | bytes 3932168 | tf_op jit(solution)/shard_map/ppermute | solution.py:66
  627.4 52.1 %collective-permute-start.53 = (bf16[1536,128]{1,0:T(8,128)(2,1)S(1)}, bf16[1536,128]{1,0:T(8,128)(2,1)S(1)}, u32[]{:S(2)}, u32[]{:S(2)}) collective-permute-start(bf16[1536,128]{1,0:T(8,128)(2,1)S(1)} %get-tuple-element.268), channel_id=1, source_target_pairs={{0,24},{2,26},{4,28},{6,30},{8,16},{10,18},{12,20},{14,22},{16,8},... | collective-permute-start | bytes 1179656 | tf_op jit(solution)/shard_map/ppermute | solution.py:66
  629.0 50.6 %collective-permute-start.52 = (bf16[1536,128]{1,0:T(8,128)(2,1)S(1)}, bf16[1536,128]{1,0:T(8,128)(2,1)S(1)}, u32[]{:S(2)}, u32[]{:S(2)}) collective-permute-start(bf16[1536,128]{1,0:T(8,128)(2,1)S(1)} %get-tuple-element.269), channel_id=1, source_target_pairs={{0,16},{2,18},{4,20},{6,22},{8,24},{10,26},{12,28},{14,30},{16,0},... | collective-permute-start | bytes 1179656 | tf_op jit(solution)/shard_map/ppermute | solution.py:66
  629.8 49.8 %collective-permute-start.51 = (bf16[1536,128]{1,0:T(8,128)(2,1)S(1)}, bf16[1536,128]{1,0:T(8,128)(2,1)S(1)}, u32[]{:S(2)}, u32[]{:S(2)}) collective-permute-start(bf16[1536,128]{1,0:T(8,128)(2,1)S(1)} %get-tuple-element.270), channel_id=1, source_target_pairs={{0,8},{2,10},{4,12},{6,14},{8,0},{10,2},{12,4},{14,6},{16,24},{18,... | collective-permute-start | bytes 1179656 | tf_op jit(solution)/shard_map/ppermute | solution.py:66
  (116 other events, 1823.4 us)
Sparse Core Ops, SparseCore 0:
  167.6 79.7 all-gather.2
  249.8 70.1 all-gather.4
  323.0 70.2 reduce-scatter.12
  396.1 70.1 reduce-scatter.14
  470.3 69.0 reduce-scatter.16
  545.4 46.7 reduce-scatter.18

commit v3 on v2

--- a/solution.py
+++ b/solution.py
@@ -709,6 +709,66 @@
     return total, total_low, gain_grad[0]
 
 
+def split_kernel(side_ref, query, key, value, out, own_ref, other_ref):
+    for ref, side in ((own_ref, side_ref[0]), (other_ref, 1 - side_ref[0])):
+        first = 0
+        for weight in (query, key, value):
+            size = weight.shape[1] // 2
+            half = weight[:, pl.ds(pl.multiple_of(side * size, size), size)]
+            ref[first : first + size, :] = low(wide(half).T)
+            first += size
+        size = out.shape[0] // 2
+        ref[first : first + size, :] = out[pl.ds(pl.multiple_of(side * size, size), size), :]
+
+
+def split_attention(side, query, key, value, out):
+    units = (query.shape[1] + key.shape[1] + value.shape[1] + out.shape[0]) // 2
+    shape = jax.ShapeDtypeStruct((units, out.shape[1]), out.dtype)
+    return pl.pallas_call(
+        split_kernel,
+        out_shape=[shape, shape],
+        in_specs=[pl.BlockSpec(memory_space=pltpu.SMEM)]
+        + [pl.BlockSpec(memory_space=pltpu.VMEM)] * 4,
+        out_specs=[pl.BlockSpec(memory_space=pltpu.VMEM)] * 2,
+        compiler_params=params(),
+        cost_estimate=small_cost(),
+    )(side, query, key, value, out)
+
+
+def finish_kernel(counts, places, side_ref, *refs):
+    groups, first = [], 0
+    for mine, other in counts:
+        groups.append((refs[first : first + mine], refs[first + mine : first + mine + other]))
+        first += mine + other
+    outs = refs[first:]
+    side = side_ref[0]
+    for group, row, size, out, place, extent, turned in places:
+        for which, parts in zip((side, 1 - side), groups[group]):
+            total = None
+            for part in parts:
+                values = wide(part[row : row + size, :])
+                total = values if total is None else total + values
+            at = pl.ds(pl.multiple_of(which * extent + place, size), size)
+            if turned:
+                outs[out][:, at] = total.T
+            else:
+                outs[out][at, :] = total
+
+
+def finish(side, groups, places, shapes):
+    counts = tuple((len(mine), len(other)) for mine, other in groups)
+    parts = [part for mine, other in groups for part in (*mine, *other)]
+    return pl.pallas_call(
+        functools.partial(finish_kernel, counts, tuple(places)),
+        out_shape=[jax.ShapeDtypeStruct(shape, jnp.float32) for shape in shapes],
+        in_specs=[pl.BlockSpec(memory_space=pltpu.SMEM)]
+        + [pl.BlockSpec(memory_space=pltpu.VMEM)] * len(parts),
+        out_specs=[pl.BlockSpec(memory_space=pltpu.VMEM)] * len(shapes),
+        compiler_params=params(),
+        cost_estimate=small_cost(),
+    )(side, *parts)
+
+
 class Sequence:
     def __init__(self):
         self.last = ()
@@ -888,17 +948,15 @@
     def columns(mask):
         return lax.dynamic_slice_in_dim(total, (place ^ (mask // 4)) * size, size, 1)
 
-    return [wide(columns(0))] + [exchange(low(columns(m)), m) for m in masks[1:]]
-
-
-def last_end(own, received):
-    mine, other = own, None
-    for mask, values in zip(far_masks()[1:], received):
-        if mask & PAIR:
-            other = wide(values) if other is None else other + wide(values)
-        else:
-            mine = mine + wide(values)
-    return mine, other
+    return [low(columns(0))] + [exchange(low(columns(m)), m) for m in masks[1:]]
+
+
+def last_parts(own, received):
+    masks = far_masks()[1:]
+    return (
+        [own] + [v for m, v in zip(masks, received) if not m & PAIR],
+        [v for m, v in zip(masks, received) if m & PAIR],
+    )
 
 
 def team_halves(projected):
@@ -950,17 +1008,11 @@
             lax.dynamic_slice_in_dim(weight, (1 - side) * size, size, axis),
         )
 
-    q_half, k_half, v_half = halves(w_query, 1), halves(w_key, 1), halves(w_value, 1)
-    q_cols, kv_cols = q_half[0].shape[1], k_half[0].shape[1]
+    q_cols, kv_cols = w_query.shape[1] // 2, w_key.shape[1] // 2
     qkv_cols = q_cols + 2 * kv_cols
     q_heads, kv_heads = q_cols // head_width, kv_cols // head_width
-    out_half = halves(w_out, 0)
-    attn_own, attn_other = [
-        jnp.concatenate(
-            [jnp.concatenate([q_half[s], k_half[s], v_half[s]], axis=1).T, out_half[s]], axis=0
-        )
-        for s in (0, 1)
-    ]
+    side_arg = side.reshape(1).astype(jnp.int32)
+    attn_own, attn_other = split_attention(side_arg, w_query, w_key, w_value, w_out)
     ends_mate = exchange(wide(seq_ends), PAIR)
     attn_far = near_start(attn_own, attn_other)
     g_half, u_half, d_half = halves(w_gate, 1), halves(w_up, 1), halves(w_down, 0)
@@ -1118,7 +1170,6 @@
     token_mate, late_far = seq.wait(token_mate, late_far)
     late_mine, late_other = team_scatter_start(late_keep, late_far)
     sum_mate = exchange(seq.tie(sum_mate), PAIR)
-    early_mine, early_other = last_end(early[0], early[1:])
     attn_back = token_mine + wide(token_mate)
     token_from, gain_attn_part = attn_norm_pull(attn_back)
     grad_tokens = from_order(hidden_grad_total + token_from)
@@ -1137,39 +1188,32 @@
     final = last_start(
         jnp.concatenate([scatter_end(qkv_full, *qkv_steps), wide(out_scattered)], axis=0)
     )
-    late_other, sum_mate = seq.wait(late_other, sum_mate)
-    late_other = wide(late_other)
+    late_other, sum_mate, *final = seq.wait(late_other, sum_mate, *final)
     mlp_sum = sum_mine + wide(sum_mate)
     out_tokens = from_order(low(hidden_in + live_mine * mlp_sum))
     gain_sums = far_sum(seq.tie(gain_parts))
-    cut = 3 * units
-    teams = [
-        (early_mine[:cut], early_other[:cut]),
-        (early_mine[cut:], early_other[cut:]),
-        (late_mine, late_other),
-    ]
-
-    def pick(pair, start, stop):
-        return in_turn(pair[0][start:stop], pair[1][start:stop], 0)
-
-    def units_of(kind):
-        cut = slice(kind * units, (kind + 1) * units)
-        return in_turn(
-            jnp.concatenate([keep[cut] for keep, _ in teams], axis=0),
-            jnp.concatenate([other[cut] for _, other in teams], axis=0),
-            0,
-        )
-
-    grad_gate = units_of(0).T
-    grad_up = units_of(1).T
-    grad_down = units_of(2)
-    seq.mark(grad_gate, grad_up, grad_down, out_tokens, grad_tokens)
-    final = seq.wait(*final)
-    attn_team = last_end(final[0], final[1:])
-    grad_out = pick(attn_team, qkv_cols, qkv_cols + q_cols)
-    grad_query = pick(attn_team, 0, q_cols).T
-    grad_key = pick(attn_team, q_cols, q_cols + kv_cols).T
-    grad_value = pick(attn_team, q_cols + kv_cols, qkv_cols).T
+    where = [(0, 0), (0, 3 * units), (1, 0)]
+    grad_gate, grad_up, grad_down = finish(
+        side_arg,
+        [last_parts(early[0], early[1:]), ([late_mine], [late_other])],
+        [
+            (group, first + kind * units, units, kind, chunk * units, all_units, kind < 2)
+            for chunk, (group, first) in enumerate(where)
+            for kind in range(3)
+        ],
+        [w_gate.shape, w_up.shape, w_down.shape],
+    )
+    grad_query, grad_key, grad_value, grad_out = finish(
+        side_arg,
+        [last_parts(final[0], final[1:])],
+        [
+            (0, 0, q_cols, 0, 0, q_cols, True),
+            (0, q_cols, kv_cols, 1, 0, kv_cols, True),
+            (0, q_cols + kv_cols, kv_cols, 2, 0, kv_cols, True),
+            (0, qkv_cols, q_cols, 3, 0, q_cols, False),
+        ],
+        [w_query.shape, w_key.shape, w_value.shape, w_out.shape],
+    )
     return (
         out_tokens,
         grad_tokens,

time: 705 us -> 702 us (level)
  Pallas kernels: 250 us -> 259 us
  other arithmetic: 74.6 us -> 66 us
    unnamed x184 -> x120, local copies, waits for them, and re-layouts: 27 us -> 11.4 us
    pallas_call x0 -> x3, Pallas kernels: none -> 9.94 us  [the longest x2 7.76 us: finish(): pl.pallas_call(functools.partial(finish_kernel, counts, tuple(places)), o...]
    select_n x11 -> x9, other arithmetic: 17.3 us -> 15.6 us  [in_turn(): jnp.where(bit_side(bit) == 0, jnp.concatenate([mine, theirs], axis=axis),...]
  transfers between devices with their start and end apart: 62 -> 62, of which waited for: 29 -> 29; matrix products, arithmetic and copies ran while one was open for 14% -> 13% of each run, Pallas kernels for 36% -> 37%
where the time goes in v3:
time: 702 us; the launch traced here: 696 us
  waiting for transfers between devices  268 us (38%)
  Pallas kernels  259 us (37%)
  other arithmetic  66 us (9%)
  starting transfers between devices  44.2 us (6%)
  local copies, waits for them, and re-layouts  43.8 us (6%)
  between operations  15.2 us (2%)
    ppermute x42, waiting for transfers between devices, exchange(): return lax.ppermute(values, 'dp', [(i, i ^ mask) for i in range(size)])  253 us
    pallas_call x3, Pallas kernels, mlp_units(): pl.pallas_call(functools.partial(mlp_kernel, pieces, tiles, with_grad, co...  73.4 us
    pallas_call x4, Pallas kernels, project(): pl.pallas_call(functools.partial(project_kernel, pieces, rows, parts), gr...  62.7 us
    ppermute x42, starting transfers between devices, exchange(): return lax.ppermute(values, 'dp', [(i, i ^ mask) for i in range(size)])  41.9 us
    pallas_call x3, Pallas kernels, weight_grad(): pl.pallas_call(functools.partial(weight_grad_kernel, pieces, tuple(cuts),...  34.5 us
    pallas_call x1, Pallas kernels, attend_back(): pl.pallas_call(functools.partial(attend_back_kernel, pieces_of(parts, wid...  32.5 us
    convert_element_type x10, other arithmetic, low(): return values.astype(jnp.bfloat16)  24.5 us
    select_n x9, other arithmetic, in_turn(): jnp.where(bit_side(bit) == 0, jnp.concatenate([mine, theirs], axis=axis),...  15.6 us
  transfers between devices with their start and end apart: 62, of which 29 were waited for; matrix products, arithmetic and copies ran while one was open for 13% of the time, Pallas kernels for 37%

profile of v3, /device:TPU:0, one launch (start us, length us, event | category | flops | bytes accessed | tf_op | source)
XLA Modules:
  0.0 695.7 jit_solution(9286287496266337579)
XLA Ops:
  24.8 8.8 %collective-permute-done.5 = f32[1,4]{1,0:T(1,128)S(1)} collective-permute-done((f32[1,4]{1,0:T(1,128)S(1)}, f32[1,4]{1,0:T(1,128)S(1)}, u32[]{:S(2)}, u32[]{:S(2)}) %collective-permute-start.5) | collective-permute-done | bytes 48 | tf_op jit(solution)/shard_map/ppermute | solution.py:66
  65.5 42.1 %collective-permute-done.8 = bf16[1536,256]{1,0:T(8,128)(2,1)S(1)} collective-permute-done((bf16[1536,256]{1,0:T(8,128)(2,1)S(1)}, bf16[1536,256]{1,0:T(8,128)(2,1)S(1)}, u32[]{:S(2)}, u32[]{:S(2)}) %collective-permute-start.8) | collective-permute-done | bytes 786464 | tf_op jit(solution)/shard_map/ppermute | solution.py:66
  114.1 9.6 %collective-permute-done.13 = bf16[3072,128]{1,0:T(8,128)(2,1)S(1)} collective-permute-done((bf16[3072,128]{1,0:T(8,128)(2,1)S(1)}, bf16[3072,128]{1,0:T(8,128)(2,1)S(1)}, u32[]{:S(2)}, u32[]{:S(2)}) %collective-permute-start.13) | collective-permute-done | bytes 786464 | tf_op jit(solution)/shard_map/ppermute | solution.py:66
  144.8 12.1 %shard_map.239 = (f32[1280,768]{1,0:T(8,128)}, bf16[1280,768]{1,0:T(8,128)(2,1)}, bf16[1280,256]{1,0:T(8,128)(2,1)}) custom-call(bf16[320,2048]{1,0:T(8,128)(2,1)} %fusion.2.refs_0_, bf16[320,2048]{1,0:T(8,128)(2,1)} %copy-done.13, bf16[320,2048]{1,0:T(8,128)(2,1)} %collective-permute-done.9.refs_2_, bf16[320,2048]{1,0:T(8,128)(2,1)} %collective-permute-done.10.refs_3_, ...), custom_call_target="tpu_custom_call" | custom-call | flops 1000 | bytes 1000 | tf_op jit(solution)/shard_map/pallas_call | solution.py:443
  172.8 12.3 %shard_map.240.refs_0_.left_ref = bf16[1280,512]{1,0:T(8,128)(2,1)} custom-call(bf16[1280,768]{1,0:T(8,128)(2,1)} %get-tuple-element.124.q_ref.k_ref, bf16[1280,768]{1,0:T(8,128)(2,1)} %get-tuple-element.124.q_ref.k_ref, bf16[1280,256]{1,0:T(8,128)(2,1)} %get-tuple-element.133.v_ref, s32[2,640,8]{2,1,0:T(8,128)} %stack.55.row_ref, ...), custom_call_target="tpu_custom_call" | custom-call | flops 1000 | bytes 1000 | tf_op jit(solution)/shard_map/pallas_call | solution.py:516
  185.1 8.9 %shard_map.241 = (f32[2,320,2048]{2,1,0:T(8,128)}, bf16[2,320,2048]{2,1,0:T(8,128)(2,1)}) custom-call(bf16[1280,512]{1,0:T(8,128)(2,1)} %shard_map.240.refs_0_.left_ref, bf16[4,1536,512]{2,1,0:T(8,128)(2,1)} %shard_map.238.refs_4_.refs_1_.weight_ref), custom_call_target="tpu_custom_call" | custom-call | flops 1000 | bytes 1000 | tf_op jit(solution)/shard_map/pallas_call | solution.py:327
  194.0 10.8 %collective-permute-done.19.refs_7_ = bf16[160,2048]{1,0:T(8,128)(2,1)} collective-permute-done((bf16[160,2048]{1,0:T(8,128)(2,1)}, bf16[160,2048]{1,0:T(8,128)(2,1)}, u32[]{:S(2)}, u32[]{:S(2)}) %collective-permute-start.19) | collective-permute-done | bytes 655392 | tf_op jit(solution)/shard_map/ppermute | solution.py:66
  223.3 24.0 %collective-permute-done.23 = bf16[320,2048]{1,0:T(8,128)(2,1)S(1)} collective-permute-done((bf16[320,2048]{1,0:T(8,128)(2,1)}, bf16[320,2048]{1,0:T(8,128)(2,1)S(1)}, u32[]{:S(2)}, u32[]{:S(2)}) %collective-permute-start.23) | collective-permute-done | bytes 1310752 | tf_op jit(solution)/shard_map/ppermute | solution.py:66
  251.0 29.2 %collective-permute-done.25.refs_2_ = bf16[320,2048]{1,0:T(8,128)(2,1)S(1)} collective-permute-done((bf16[320,2048]{1,0:T(8,128)(2,1)S(1)}, bf16[320,2048]{1,0:T(8,128)(2,1)S(1)}, u32[]{:S(2)}, u32[]{:S(2)}) %collective-permute-start.25) | collective-permute-done | bytes 1310752 | tf_op jit(solution)/shard_map/ppermute | solution.py:66
  287.2 27.5 %shard_map.243 = (bf16[3,1280,512]{2,1,0:T(8,128)(2,1)}, bf16[4,1536,512]{2,1,0:T(8,128)(2,1)}) custom-call(bf16[320,2048]{1,0:T(8,128)(2,1)} %copy-done.3, bf16[320,2048]{1,0:T(8,128)(2,1)} %copy-done.8, bf16[320,2048]{1,0:T(8,128)(2,1)} %copy-done.6, bf16[320,2048]{1,0:T(8,128)(2,1)} %collective-permute-done.26.refs_3_, bf16[320,2048]{1,0:T(8,128)(2,1)} %copy-done, ...), custom_call_target="tpu_custom_call" | custom-call | flops 1000 | bytes 1000 | tf_op jit(solution)/shard_map/pallas_call | solution.py:274
  314.9 27.8 %shard_map.244 = (bf16[3,1280,512]{2,1,0:T(8,128)(2,1)}, bf16[4,1536,512]{2,1,0:T(8,128)(2,1)}) custom-call(bf16[320,2048]{1,0:T(8,128)(2,1)} %copy-done.3, bf16[320,2048]{1,0:T(8,128)(2,1)} %copy-done.8, bf16[320,2048]{1,0:T(8,128)(2,1)} %copy-done.6, bf16[320,2048]{1,0:T(8,128)(2,1)} %collective-permute-done.26.refs_3_, bf16[320,2048]{1,0:T(8,128)(2,1)} %copy-done, ...), custom_call_target="tpu_custom_call" | custom-call | flops 1000 | bytes 1000 | tf_op jit(solution)/shard_map/pallas_call | solution.py:274
  342.8 18.1 %shard_map.245.refs_4_.refs_5_.refs_2_.left_ref = bf16[3,1280,512]{2,1,0:T(8,128)(2,1)} custom-call(bf16[320,2048]{1,0:T(8,128)(2,1)} %copy-done.3, bf16[320,2048]{1,0:T(8,128)(2,1)} %copy-done.8, bf16[320,2048]{1,0:T(8,128)(2,1)} %copy-done.6, bf16[320,2048]{1,0:T(8,128)(2,1)} %collective-permute-done.26.refs_3_, bf16[320,2048]{1,0:T(8,128)(2,1)} %copy-done, ...), custom_call_target="tpu_custom_call" | custom-call | flops 1000 | bytes 1000 | tf_op jit(solution)/shard_map/pallas_call | solution.py:274
  360.9 25.6 %shard_map.246 = (f32[2,320,2048]{2,1,0:T(8,128)}, bf16[2,320,2048]{2,1,0:T(8,128)(2,1)}) custom-call(bf16[3,1280,512]{2,1,0:T(8,128)(2,1)} %get-tuple-element.154.refs_0_.refs_1_, bf16[3,1280,512]{2,1,0:T(8,128)(2,1)} %get-tuple-element.154.refs_0_.refs_1_, bf16[3,1280,512]{2,1,0:T(8,128)(2,1)} %get-tuple-element.155.refs_2_.refs_3_.refs_1_, ...), custom_call_target="tpu_custom_call" | custom-call | flops 1000 | bytes 1000 | tf_op jit(solution)/shard_map/pallas_call | solution.py:327
  397.5 15.8 %shard_map.247 = (f32[2,320,2048]{2,1,0:T(8,128)}, bf16[2,320,2048]{2,1,0:T(8,128)(2,1)}) custom-call(bf16[3,1280,512]{2,1,0:T(8,128)(2,1)} %get-tuple-element.154.refs_0_.refs_1_, bf16[3,1280,512]{2,1,0:T(8,128)(2,1)} %get-tuple-element.155.refs_2_.refs_3_.refs_1_, bf16[3,1280,512]{2,1,0:T(8,128)(2,1)} %shard_map.245.refs_4_.refs_5_.refs_2_.left_ref, ...), custom_call_target="tpu_custom_call" | custom-call | flops 1000 | bytes 1000 | tf_op jit(solution)/shard_map/pallas_call | solution.py:327
  413.2 14.4 %collective-permute-done.31.mate = bf16[320,2048]{1,0:T(8,128)(2,1)S(1)} collective-permute-done((bf16[320,2048]{1,0:T(8,128)(2,1)S(1)}, bf16[320,2048]{1,0:T(8,128)(2,1)S(1)}, u32[]{:S(2)}, u32[]{:S(2)}) %collective-permute-start.31) | collective-permute-done | bytes 1310752 | tf_op jit(solution)/shard_map/ppermute | solution.py:66
  436.7 14.7 %shard_map.249 = bf16[4,1536,512]{2,1,0:T(8,128)(2,1)} custom-call(bf16[3,1280,512]{2,1,0:T(8,128)(2,1)} %shard_map.245.refs_4_.refs_5_.refs_2_.left_ref, bf16[320,2048]{1,0:T(8,128)(2,1)} %copy-done.3, bf16[320,2048]{1,0:T(8,128)(2,1)} %copy-done.8, bf16[320,2048]{1,0:T(8,128)(2,1)} %copy-done.6, bf16[320,2048]{1,0:T(8,128)(2,1)} %collective-permute-done.26.refs_3_, ...), custom_call_target="tpu_custom_call" | custom-call | flops 1000 | bytes 1000 | tf_op jit(solution)/shard_map/pallas_call | solution.py:381
  451.4 15.1 %collective-permute-done.33.refs_2_.cot_c = bf16[320,2048]{1,0:T(8,128)(2,1)} collective-permute-done((bf16[320,2048]{1,0:T(8,128)(2,1)}, bf16[320,2048]{1,0:T(8,128)(2,1)}, u32[]{:S(2)}, u32[]{:S(2)}) %collective-permute-start.33) | collective-permute-done | bytes 1310752 | tf_op jit(solution)/shard_map/ppermute | solution.py:66
  482.7 32.5 %shard_map.251 = (bf16[1280,1024]{1,0:T(8,128)(2,1)}, f32[8,128]{1,0:T(8,128)}) custom-call(bf16[320,2048]{1,0:T(8,128)(2,1)} %get-tuple-element.160.refs_0_.cot_a, bf16[320,2048]{1,0:T(8,128)(2,1)} %collective-permute-done.32.refs_1_.cot_b, bf16[320,2048]{1,0:T(8,128)(2,1)} %collective-permute-done.33.refs_2_.cot_c, ...), custom_call_target="tpu_custom_call" | custom-call | flops 399999991808 | bytes 1000 | tf_op jit(solution)/shard_map/pallas_call | solution.py:632
  515.2 11.9 %shard_map.252 = bf16[4,1024,512]{2,1,0:T(8,128)(2,1)} custom-call(bf16[1280,1024]{1,0:T(8,128)(2,1)} %get-tuple-element.166.left_ref.refs_0_, bf16[320,2048]{1,0:T(8,128)(2,1)} %fusion.2.refs_0_, bf16[320,2048]{1,0:T(8,128)(2,1)} %copy-done.13, bf16[320,2048]{1,0:T(8,128)(2,1)} %collective-permute-done.9.refs_2_, ...), custom_call_target="tpu_custom_call" | custom-call | flops 1000 | bytes 1000 | tf_op jit(solution)/shard_map/pallas_call | solution.py:381
  527.2 12.4 %shard_map.253 = (f32[2,320,2048]{2,1,0:T(8,128)}, bf16[2,320,2048]{2,1,0:T(8,128)(2,1)}) custom-call(bf16[1280,1024]{1,0:T(8,128)(2,1)} %get-tuple-element.166.left_ref.refs_0_, bf16[4,1536,512]{2,1,0:T(8,128)(2,1)} %shard_map.238.refs_4_.refs_1_.weight_ref), custom_call_target="tpu_custom_call" | custom-call | flops 1000 | bytes 1000 | tf_op jit(solution)/shard_map/pallas_call | solution.py:327
  556.4 26.2 %collective-permute-done.35 = bf16[1024,512]{1,0:T(8,128)(2,1)} collective-permute-done((bf16[1024,512]{1,0:T(8,128)(2,1)}, bf16[1024,512]{1,0:T(8,128)(2,1)}, u32[]{:S(2)}, u32[]{:S(2)}) %collective-permute-start.35) | collective-permute-done | bytes 1048608 | tf_op jit(solution)/shard_map/ppermute | solution.py:66
  605.5 7.9 %collective-permute-done.49 = f32[4352]{0:T(1024)S(1)} collective-permute-done((f32[4352]{0:T(1024)S(1)}, f32[4352]{0:T(1024)S(1)}, u32[]{:S(2)}, u32[]{:S(2)}) %collective-permute-start.49) | collective-permute-done | bytes 17440 | tf_op jit(solution)/shard_map/ppermute | solution.py:66
  629.6 25.6 %collective-permute-done.53.refs_3_ = bf16[1536,128]{1,0:T(8,128)(2,1)S(1)} collective-permute-done((bf16[1536,128]{1,0:T(8,128)(2,1)}, bf16[1536,128]{1,0:T(8,128)(2,1)S(1)}, u32[]{:S(2)}, u32[]{:S(2)}) %collective-permute-start.53) | collective-permute-done | bytes 393248 | tf_op jit(solution)/shard_map/ppermute | solution.py:66
  662.1 9.0 %collective-permute-done.51.refs_2_ = bf16[1536,128]{1,0:T(8,128)(2,1)} collective-permute-done((bf16[1536,128]{1,0:T(8,128)(2,1)}, bf16[1536,128]{1,0:T(8,128)(2,1)}, u32[]{:S(2)}, u32[]{:S(2)}) %collective-permute-start.51) | collective-permute-done | bytes 393248 | tf_op jit(solution)/shard_map/ppermute | solution.py:66
  (346 shorter events, 238.2 us)
Async XLA Ops:
  7.2 307.7 %all-gather.3.cloned.1.call-start = ((), (), s32[]{:S(2)}) async-start(), calls=%async_computation.4 | async-start | bytes 7864320 | tf_op jit(solution)/shard_map/all_gather | solution.py:834
  9.4 39.0 %collective-permute-start.4 = (bf16[1536,128]{1,0:T(8,128)(2,1)}, bf16[1536,128]{1,0:T(8,128)(2,1)}, u32[]{:S(2)}, u32[]{:S(2)}) collective-permute-start(bf16[1536,128]{1,0:T(8,128)(2,1)} %get-tuple-element.111), channel_id=1, source_target_pairs={{0,24},{2,26},{4,28},{6,30},{8,16},{10,18},{12,20},{14,22},{16,8},... | collective-permute-start | bytes 1179656 | tf_op jit(solution)/shard_map/ppermute | solution.py:66
  53.9 54.6 %collective-permute-start.7 = (bf16[1536,512]{1,0:T(8,128)(2,1)}, bf16[1536,512]{1,0:T(8,128)(2,1)}, u32[]{:S(2)}, u32[]{:S(2)}) collective-permute-start(bf16[1536,512]{1,0:T(8,128)(2,1)} %maximum_select_fusion.own_ref), channel_id=1, source_target_pairs={{0,4},{2,6},{4,0},{6,2},{8,12},{10,14},{12,8},{14,10},{16,20},{18,... | collective-permute-start | bytes 4718600 | tf_op jit(solution)/shard_map/ppermute | solution.py:66
  55.4 53.1 %collective-permute-start.6 = (bf16[1536,512]{1,0:T(8,128)(2,1)}, bf16[1536,512]{1,0:T(8,128)(2,1)}, u32[]{:S(2)}, u32[]{:S(2)}) collective-permute-start(bf16[1536,512]{1,0:T(8,128)(2,1)} %maximum_select_fusion.own_ref), channel_id=1, source_target_pairs={{0,2},{2,0},{4,6},{6,4},{8,10},{10,8},{12,14},{14,12},{16,18},{18,... | collective-permute-start | bytes 4718600 | tf_op jit(solution)/shard_map/ppermute | solution.py:66
  59.5 48.9 %collective-permute-start.9 = (bf16[320,2048]{1,0:T(8,128)(2,1)}, bf16[320,2048]{1,0:T(8,128)(2,1)}, u32[]{:S(2)}, u32[]{:S(2)}) collective-permute-start(bf16[320,2048]{1,0:T(8,128)(2,1)} %fusion.2.refs_0_), channel_id=1, source_target_pairs={{0,8},{2,10},{4,12},{6,14},{8,0},{10,2},{12,4},{14,6},{16,24},{18,... | collective-permute-start | bytes 3932168 | tf_op jit(solution)/shard_map/ppermute | solution.py:66
  64.6 43.0 %collective-permute-start.8 = (bf16[1536,256]{1,0:T(8,128)(2,1)S(1)}, bf16[1536,256]{1,0:T(8,128)(2,1)S(1)}, u32[]{:S(2)}, u32[]{:S(2)}) collective-permute-start(bf16[1536,256]{1,0:T(8,128)(2,1)S(1)} %maximum_select_fusion.6), channel_id=1, source_target_pairs={{0,16},{2,18},{4,20},{6,22},{8,24},{10,26},{12,28},{14,30},{16,0},... | collective-permute-start | bytes 2359304 | tf_op jit(solution)/shard_map/ppermute | solution.py:66
  65.1 58.5 %collective-permute-start.13 = (bf16[3072,128]{1,0:T(8,128)(2,1)S(1)}, bf16[3072,128]{1,0:T(8,128)(2,1)S(1)}, u32[]{:S(2)}, u32[]{:S(2)}) collective-permute-start(bf16[3072,128]{1,0:T(8,128)(2,1)S(1)} %copy-done.43), channel_id=1, source_target_pairs={{0,8},{2,10},{4,12},{6,14},{8,0},{10,2},{12,4},{14,6},{16,24},{18,... | collective-permute-start | bytes 2359304 | tf_op jit(solution)/shard_map/ppermute | solution.py:66
  166.5 176.3 %all-gather.5.cloned.1.call-start = ((), (), s32[]{:S(2)}) async-start(), calls=%async_computation.5 | async-start | bytes 7864320 | tf_op jit(solution)/shard_map/all_gather | solution.py:834
  207.7 219.9 %reduce-scatter.13.cloned.1.call-start = ((), (), s32[]{:S(2)}) async-start(), calls=%async_computation.6 | async-start | bytes 7864320
  250.5 34.8 %collective-permute-start.24 = (bf16[320,2048]{1,0:T(8,128)(2,1)S(1)}, bf16[320,2048]{1,0:T(8,128)(2,1)S(1)}, u32[]{:S(2)}, u32[]{:S(2)}) collective-permute-start(bf16[320,2048]{1,0:T(8,128)(2,1)S(1)} %multiply_convert_fusion.refs_0_), channel_id=1, source_target_pairs={{0,1},{1,0},{2,3},{3,2},{4,5},{5,4},{6,7},{7,6},{8,9},{9,8},{10,11... | collective-permute-start | bytes 3932168 | tf_op jit(solution)/shard_map/ppermute | solution.py:790
  314.8 151.7 %reduce-scatter.15.cloned.1.call-start = ((), (), s32[]{:S(2)}) async-start(), calls=%async_computation.7 | async-start | bytes 7864320
  342.7 198.5 %reduce-scatter.17.cloned.1.call-start = ((), (), s32[]{:S(2)}) async-start(), calls=%async_computation.8 | async-start | bytes 7864320
  436.6 38.2 %collective-permute-start.32 = (bf16[320,2048]{1,0:T(8,128)(2,1)}, bf16[320,2048]{1,0:T(8,128)(2,1)}, u32[]{:S(2)}, u32[]{:S(2)}) collective-permute-start(bf16[320,2048]{1,0:T(8,128)(2,1)} %get-tuple-element.160.refs_0_.cot_a), channel_id=1, source_target_pairs={{0,1},{1,0},{2,3},{3,2},{4,5},{5,4},{6,7},{7,6},{8,9},{9,8},{10,11... | collective-permute-start | bytes 3932168 | tf_op jit(solution)/shard_map/ppermute | solution.py:790
  466.5 154.6 %reduce-scatter.19.cloned.1.call-start = ((), (), s32[]{:S(2)}) async-start(), calls=%async_computation.9 | async-start | bytes 2621440
  470.4 69.1 %collective-permute-start.39 = (bf16[3072,128]{1,0:T(8,128)(2,1)}, bf16[3072,128]{1,0:T(8,128)(2,1)}, u32[]{:S(2)}, u32[]{:S(2)}) collective-permute-start(bf16[3072,128]{1,0:T(8,128)(2,1)} %get-tuple-element.221), channel_id=1, source_target_pairs={{0,24},{2,26},{4,28},{6,30},{8,16},{10,18},{12,20},{14,22},{16,8},... | collective-permute-start | bytes 2359304 | tf_op jit(solution)/shard_map/ppermute | solution.py:66
  472.0 69.3 %collective-permute-start.38 = (bf16[3072,128]{1,0:T(8,128)(2,1)}, bf16[3072,128]{1,0:T(8,128)(2,1)}, u32[]{:S(2)}, u32[]{:S(2)}) collective-permute-start(bf16[3072,128]{1,0:T(8,128)(2,1)} %get-tuple-element.222), channel_id=1, source_target_pairs={{0,16},{2,18},{4,20},{6,22},{8,24},{10,26},{12,28},{14,30},{16,0},... | collective-permute-start | bytes 2359304 | tf_op jit(solution)/shard_map/ppermute | solution.py:66
  472.4 68.8 %collective-permute-start.37 = (bf16[3072,128]{1,0:T(8,128)(2,1)}, bf16[3072,128]{1,0:T(8,128)(2,1)}, u32[]{:S(2)}, u32[]{:S(2)}) collective-permute-start(bf16[3072,128]{1,0:T(8,128)(2,1)} %get-tuple-element.223), channel_id=1, source_target_pairs={{0,8},{2,10},{4,12},{6,14},{8,0},{10,2},{12,4},{14,6},{16,24},{18,... | collective-permute-start | bytes 2359304 | tf_op jit(solution)/shard_map/ppermute | solution.py:66
  545.5 37.1 %collective-permute-start.35 = (bf16[1024,512]{1,0:T(8,128)(2,1)}, bf16[1024,512]{1,0:T(8,128)(2,1)}, u32[]{:S(2)}, u32[]{:S(2)}) collective-permute-start(bf16[1024,512]{1,0:T(8,128)(2,1)} %pad_maximum_fusion.1), channel_id=1, source_target_pairs={{0,2},{2,0},{4,6},{6,4},{8,10},{10,8},{12,14},{14,12},{16,18},{18,... | collective-permute-start | bytes 3145736 | tf_op jit(solution)/shard_map/ppermute | solution.py:66
  547.8 37.5 %collective-permute-start.36 = (bf16[1024,512]{1,0:T(8,128)(2,1)}, bf16[1024,512]{1,0:T(8,128)(2,1)}, u32[]{:S(2)}, u32[]{:S(2)}) collective-permute-start(bf16[1024,512]{1,0:T(8,128)(2,1)} %pad_maximum_fusion.2), channel_id=1, source_target_pairs={{0,4},{2,6},{4,0},{6,2},{8,12},{10,14},{12,8},{14,10},{16,20},{18,... | collective-permute-start | bytes 3145736 | tf_op jit(solution)/shard_map/ppermute | solution.py:66
  553.2 47.6 %collective-permute-start.42 = (bf16[320,2048]{1,0:T(8,128)(2,1)}, bf16[320,2048]{1,0:T(8,128)(2,1)S(1)}, u32[]{:S(2)}, u32[]{:S(2)}) collective-permute-start(bf16[320,2048]{1,0:T(8,128)(2,1)} %fusion.12), channel_id=1, source_target_pairs={{0,8},{2,10},{4,12},{6,14},{8,0},{10,2},{12,4},{14,6},{16,24},{18,... | collective-permute-start | bytes 3932168 | tf_op jit(solution)/shard_map/ppermute | solution.py:66
  554.5 45.0 %collective-permute-start.43 = (bf16[1536,256]{1,0:T(8,128)(2,1)S(1)}, bf16[1536,256]{1,0:T(8,128)(2,1)S(1)}, u32[]{:S(2)}, u32[]{:S(2)}) collective-permute-start(bf16[1536,256]{1,0:T(8,128)(2,1)S(1)} %constant_dynamic-slice_fusion.4), channel_id=1, source_target_pairs={{0,16},{2,18},{4,20},{6,22},{8,24},{10,26},{12,28},{14,30},{16,0},... | collective-permute-start | bytes 2359304 | tf_op jit(solution)/shard_map/ppermute | solution.py:66
  615.7 55.4 %collective-permute-start.45 = (bf16[320,2048]{1,0:T(8,128)(2,1)}, bf16[320,2048]{1,0:T(8,128)(2,1)}, u32[]{:S(2)}, u32[]{:S(2)}) collective-permute-start(bf16[320,2048]{1,0:T(8,128)(2,1)} %fusion.13), channel_id=1, source_target_pairs={{0,8},{2,10},{4,12},{6,14},{8,0},{10,2},{12,4},{14,6},{16,24},{18,... | collective-permute-start | bytes 3932168 | tf_op jit(solution)/shard_map/ppermute | solution.py:66
  626.4 35.7 %collective-permute-start.52 = (bf16[1536,128]{1,0:T(8,128)(2,1)}, bf16[1536,128]{1,0:T(8,128)(2,1)S(1)}, u32[]{:S(2)}, u32[]{:S(2)}) collective-permute-start(bf16[1536,128]{1,0:T(8,128)(2,1)} %get-tuple-element.228), channel_id=1, source_target_pairs={{0,16},{2,18},{4,20},{6,22},{8,24},{10,26},{12,28},{14,30},{16,0},... | collective-permute-start | bytes 1179656 | tf_op jit(solution)/shard_map/ppermute | solution.py:66
  627.5 43.6 %collective-permute-start.51 = (bf16[1536,128]{1,0:T(8,128)(2,1)}, bf16[1536,128]{1,0:T(8,128)(2,1)}, u32[]{:S(2)}, u32[]{:S(2)}) collective-permute-start(bf16[1536,128]{1,0:T(8,128)(2,1)} %get-tuple-element.229), channel_id=1, source_target_pairs={{0,8},{2,10},{4,12},{6,14},{8,0},{10,2},{12,4},{14,6},{16,24},{18,... | collective-permute-start | bytes 1179656 | tf_op jit(solution)/shard_map/ppermute | solution.py:66
  (93 other events, 1812.1 us)
Sparse Core Ops, SparseCore 0:
  166.6 79.0 all-gather.2
  248.1 70.1 all-gather.4
  321.3 70.2 reduce-scatter.12
  394.4 70.1 reduce-scatter.14
  467.5 70.2 reduce-scatter.16
  553.3 44.3 reduce-scatter.18
